TPU v7x, 128 devices: a whole 4x4x4 slice. The times are simulated.
128 devices in a mesh: dp: 16 (over x, y), tensor: 8 (over z, core).
Axes of the slice: x: 4, y: 4, z: 4, core: 2. Of those that a mesh axis runs over, the one named last changes fastest.
Arguments:
- activations: bfloat16 [4096, 5120], P('dp'), may hold values from -6 to 6
- out_grad: bfloat16 [4096, 5120], P('dp'), may hold values from -85 to 85, as said below
- gate_pre: bfloat16 [4096, 13824], P('dp', 'tensor'), may hold values from -6 to 6
- up_pre: bfloat16 [4096, 13824], P('dp', 'tensor'), may hold values from -26 to 26
- down_weight: bfloat16 [5120, 13824], P(None, 'tensor'), may hold values from -0.0546875 to 0.0546875
- clip_bounds: float32 [2], replicated, may hold values from 1.5 to 4
Outputs:
- grad_down: bfloat16 [5120, 13824], P('dp', 'tensor')
- grad_gate: bfloat16 [5120, 13824], P('dp', 'tensor')
Inputs may be any that keep to these rules, and one draw needn't show every extreme that they name: out_grad has a common scale within each example.
All inputs are finite; a program needn't handle non-finite values.
Results may differ from a plain program's by a relative error of at most 0.019.
Values may be sent and summed in bfloat16 or wider, within the bound.
No kernel may reach another device: no remote copies, remote signals or barrier semaphores. Data moves between devices by JAX's collectives and lax.ppermute only.
A program may use at most 192 MiB of HBM per device.

v0:
```python
import math

import jax
import jax.numpy as jnp
from jax import lax
from jax.sharding import PartitionSpec as P

SEQ = 256


def silu_slope(values):
    sigma = jax.nn.sigmoid(values)
    return sigma * (1.0 + values * (1.0 - sigma))


def pair_gram(matrix):
    return lax.dot_general(
        matrix, matrix, (((1,), (1,)), ((), ())), preferred_element_type=jnp.float32
    )


def rows_product(left_rows, right_rows):
    return lax.dot_general(
        left_rows, right_rows, (((0,), (0,)), ((), ())), preferred_element_type=jnp.float32
    )


def local(activations, out_grad, gate_pre, up_pre, down_weight, clip_bounds):
    row_count = activations.shape[0]
    model_width = activations.shape[1]
    hidden_width = gate_pre.shape[1]
    dp_count = lax.axis_size("dp")
    local_examples = row_count // SEQ
    example_total = local_examples * dp_count
    gate_val = gate_pre.astype(jnp.float32)
    up_val = up_pre.astype(jnp.float32)
    hidden = (jax.nn.silu(gate_val) * up_val).astype(jnp.bfloat16)
    hidden_grad = jnp.dot(out_grad, down_weight, preferred_element_type=jnp.float32)
    gate_grad = (hidden_grad * up_val * silu_slope(gate_val)).astype(jnp.bfloat16)

    def example_squares(example):
        x_rows, o_rows, h_rows, g_rows = (activations, out_grad, hidden, gate_grad)
        down_sq = jnp.sum(pair_gram(h_rows) * pair_gram(o_rows))
        gate_sq = jnp.sum(pair_gram(x_rows) * pair_gram(g_rows))
        return jnp.stack([down_sq, gate_sq])

    partials = lax.map(example_squares, jnp.arange(local_examples, dtype=jnp.int32))
    squares = lax.psum(partials, "tensor")
    full_hidden = hidden_width * lax.axis_size("tensor")
    radius = clip_bounds * math.sqrt(float(model_width * full_hidden * SEQ))
    factor = radius / jnp.maximum(jnp.sqrt(squares), radius)
    row_factor = jnp.repeat(factor, SEQ, axis=0)
    scaled_hidden = (row_factor[:, 0:1] * hidden.astype(jnp.float32)).astype(jnp.bfloat16)
    scaled_gate_grad = (row_factor[:, 1:2] * gate_grad.astype(jnp.float32)).astype(jnp.bfloat16)
    columns = out_grad
    down_sum = lax.psum_scatter(
        rows_product(columns, scaled_hidden).astype(jnp.bfloat16),
        "dp",
        scatter_dimension=0,
        tiled=True,
    ).astype(jnp.float32)
    columns = activations
    gate_sum = lax.psum_scatter(
        rows_product(columns, scaled_gate_grad).astype(jnp.bfloat16),
        "dp",
        scatter_dimension=0,
        tiled=True,
    ).astype(jnp.float32)
    grad_down = (down_sum / example_total).astype(jnp.bfloat16)
    grad_gate = (gate_sum / example_total).astype(jnp.bfloat16)
    return (grad_down, grad_gate)


def solution(mesh):
    in_specs = (
        P("dp", None),
        P("dp", None),
        P("dp", "tensor"),
        P("dp", "tensor"),
        P(None, "tensor"),
        P(),
    )
    out_specs = (P("dp", "tensor"), P("dp", "tensor"))
    return jax.shard_map(local, mesh=mesh, in_specs=in_specs, out_specs=out_specs, check_vma=False)
```

profile of v0, /device:TPU:0, one launch (start us, length us, event | category | flops | bytes accessed | tf_op | source)
XLA Modules:
  0.0 335.3 jit_solution(6965261072666121713)
XLA Ops:
  7.2 0.0 copy-start
  7.2 0.0 reduce-scatter.9.cloned.1.call-start
  7.2 3.6 %fusion.16 = f32[256,256]{1,0:T(8,128)S(1)} fusion(bf16[256,5120]{1,0:T(8,128)(2,1)} %param.6), kind=kOutput, calls=%fused_computation.31 | convolution fusion | flops 671088640 | bytes 2883584 | tf_op jit(solution)/shard_map/while/body/eval_jaxpr/dot_general | solution.py:17
  10.8 0.0 copy-done
  10.8 0.0 copy-start.2
  10.8 0.0 copy-start.3
  10.8 0.9 fusion.15
  11.7 0.3 copy-done.2
  12.0 0.3 copy-done.3
  12.2 0.6 fusion.4
  12.9 11.6 %fusion.3 = bf16[256,1728]{0,1:T(8,128)(2,1)S(1)} fusion(bf16[256,5120]{1,0:T(8,128)(2,1)S(1)} %copy-done, bf16[5120,1728]{0,1:T(8,128)(2,1)} %param.10, bf16[256,1728]{0,1:T(8,128)(2,1)S(1)} %copy-done.2, bf16[256,1728]{0,1:T(8,128)(2,1)S(1)} %copy-done.3), kind=kOutput, calls=%fused_computation.11 | convolution fusion | flops 4535156736 | bytes 22970368 | tf_op jit(solution)/shard_map/dot_general | solution.py:38
  24.5 0.0 copy-start.1
  24.5 0.0 copy-start.4
  24.5 1.1 fusion.13
  25.6 1.1 fusion.12
  26.7 0.0 copy-done.1
  26.7 1.4 maximum_bitcast_fusion
  28.1 16.1 %psum.7 = f32[1,2]{1,0:T(1,128)S(1)} all-reduce(f32[1,2]{1,0:T(1,128)S(1)} %maximum_bitcast_fusion), channel_id=1, replica_groups=mesh['dp'=16,'tensor'=8] {'tensor'}, use_global_device_ids=true, to_apply=%region_2.0 | all-reduce | flops 2 | bytes 16 | tf_op jit(solution)/shard_map/psum | solution.py:48
  44.3 0.0 copy-done.4
  44.3 0.6 fusion.14
  44.9 13.5 %fusion.1 = bf16[5120,1728]{0,1:T(8,128)(2,1)} fusion(bf16[256,5120]{1,0:T(8,128)(2,1)} %param.6, bf16[256,1728]{0,1:T(8,128)(2,1)} %copy-done.1, f32[]{:T(128)} %bitcast.6), kind=kOutput, calls=%fused_computation.3 | convolution fusion | flops 4540022784 | bytes 21200900 | tf_op jit(solution)/shard_map/dot_general | solution.py:23
  58.4 23.0 %copy.14 = bf16[5120,1728]{1,0:T(8,128)(2,1)} copy(bf16[5120,1728]{0,1:T(8,128)(2,1)} %fusion.1) | data formatting | bytes 35389440
  81.3 0.0 reduce-scatter.9.cloned.1.call-update
  81.4 0.0 reduce-scatter.7.cloned.1.call-start
  81.4 9.6 %fusion = bf16[5120,1728]{0,1:T(8,128)(2,1)} fusion(bf16[256,5120]{1,0:T(8,128)(2,1)S(1)} %copy-done, bf16[256,1728]{0,1:T(8,128)(2,1)S(1)} %fusion.4, f32[]{:T(128)} %bitcast.4), kind=kOutput, calls=%fused_computation.2 | convolution fusion | flops 4540022784 | bytes 21200900 | tf_op jit(solution)/shard_map/dot_general | solution.py:23
  91.0 23.1 %copy.12 = bf16[5120,1728]{1,0:T(8,128)(2,1)} copy(bf16[5120,1728]{0,1:T(8,128)(2,1)} %fusion) | data formatting | bytes 35389440
  114.1 0.0 reduce-scatter.7.cloned.1.call-update
  114.1 84.7 %reduce-scatter.9.cloned.1.call-done = bf16[320,1728]{1,0:T(8,128)(2,1)} async-done(((bf16[5120,1728]{1,0:T(8,128)(2,1)}), bf16[320,1728]{1,0:T(8,128)(2,1)}) %reduce-scatter.9.cloned.1.call-update) | async-done | bytes 1105936
  198.8 2.5 copy.15
  201.3 2.7 multiply_convert_fusion
  204.0 2.4 copy.11
  206.4 114.5 %reduce-scatter.7.cloned.1.call-done = bf16[320,1728]{1,0:T(8,128)(2,1)} async-done(((bf16[5120,1728]{1,0:T(8,128)(2,1)}), bf16[320,1728]{1,0:T(8,128)(2,1)}) %reduce-scatter.7.cloned.1.call-update) | async-done | bytes 1105936
  320.9 2.5 copy.13
  323.3 2.6 multiply_convert_fusion.1
  326.0 2.4 copy.10
  (1 shorter events, 0.0 us)
Async XLA Ops:
  7.2 3.6 %copy-start = (bf16[256,5120]{1,0:T(8,128)(2,1)S(1)}, bf16[256,5120]{1,0:T(8,128)(2,1)}, u32[]{:S(2)}) copy-start(bf16[256,5120]{1,0:T(8,128)(2,1)} %param.7) | copy-start | bytes 7864324
  7.2 191.7 %reduce-scatter.9.cloned.1.call-start = ((), (), s32[]{:S(2)}) async-start(), calls=%async_computation.3 | async-start | bytes 19496960
  10.8 1.2 copy-start.2
  10.8 1.4 copy-start.3
  24.5 2.2 copy-start.1
  24.5 19.7 %copy-start.4 = (f32[2]{0:T(128)S(1)}, f32[2]{0:T(128)}, u32[]{:S(2)}) copy-start(f32[2]{0:T(128)} %param.11) | copy-start | bytes 28
  81.4 239.5 %reduce-scatter.7.cloned.1.call-start = ((), (), s32[]{:S(2)}) async-start(), calls=%async_computation.2 | async-start | bytes 19496960
Sparse Core Ops, SparseCore 0:
  81.5 117.3 reduce-scatter.8
  202.7 118.0 reduce-scatter.6
where the time goes:
time: 337 us; the launch traced here: 335 us
  waiting for transfers between devices  199 us (59%)
  local copies, waits for them, and re-layouts  57 us (17%)
  matrix products  41.4 us (12%)
  blocking collectives  16.1 us (5%)
  between operations  14.1 us (4%)
  other arithmetic  7.34 us (2%)
    unnamed x4, waiting for transfers between devices  199 us
    unnamed x16, local copies, waits for them, and re-layouts  56.4 us
    dot_general x2, matrix products, rows_product(): lax.dot_general(left_rows, right_rows, (((0,), (0,)), ((), ())), preferre...  23.1 us
    psum x1, blocking collectives, local(): squares = lax.psum(partials, 'tensor')  16.1 us
    dot_general x1, matrix products, local(): jnp.dot(out_grad, down_weight, preferred_element_type=jnp.float32)  11.6 us
  transfers between devices with their start and end apart: 2, of which 2 were waited for; matrix products, arithmetic and copies ran while one was open for 12% of the time, Pallas kernels for 0%

commit v1 on v0

v1 whole, which is shorter than its diff:
```python
import functools
import math

import jax
import jax.numpy as jnp
from jax import lax
from jax.experimental import pallas as pl
from jax.experimental.pallas import tpu as pltpu
from jax.sharding import Mesh, PartitionSpec as P

SEQ = 256
RING = 4
CORES = 2
STEPS = (0, 1, -1, 2)
LANES = 128
MIB = 1024 * 1024
HEAVY = pl.CostEstimate(flops=10**12, bytes_accessed=10**9, transcendentals=0)
SMALL = pl.CostEstimate(flops=0, bytes_accessed=0, transcendentals=0)


def move(value, axes, goal):
    pairs = []
    for x in range(RING):
        for y in range(RING):
            for core in range(2):
                to_x, to_y = goal(x, y, core)
                pairs.append(((x * RING + y) * 2 + core, (to_x % RING * RING + to_y % RING) * 2 + core))
    return lax.ppermute(value, axes, pairs)


def shift(value, axis, step):
    if axis != "spread":
        return lax.ppermute(value, axis, [(i, (i + step) % RING) for i in range(RING)])
    pairs = []
    for x in range(RING):
        for y in range(RING):
            for core in range(2):
                to_x, to_y = ((x + step) % RING, y) if core == 0 else (x, (y + step) % RING)
                pairs.append(((x * RING + y) * 2 + core, (to_x * RING + to_y) * 2 + core))
    return lax.ppermute(value, ("x", "y", "core"), pairs)


def swap(value, axis, bit):
    return lax.ppermute(value, axis, [(i, i ^ bit) for i in range(2 if axis == "core" else RING)])


def dot_last(left, right):
    return lax.dot_general(left, right, (((1,), (1,)), ((), ())), preferred_element_type=jnp.float32)


def dot_first(left, right):
    return lax.dot_general(left, right, (((0,), (0,)), ((), ())), preferred_element_type=jnp.float32)


def around(value, axis):
    return [value] + [shift(value, axis, s) for s in STEPS[1:]]


def ring_reduce(lefts, right, axis):
    up, down, near, own = (dot_last(left, right).astype(jnp.bfloat16) for left in lefts)
    half = own.shape[0] // 2
    wide = lambda v: v.astype(jnp.float32)
    up = shift(up, axis, 1)
    down = shift(down, axis, -1)
    sum_up = shift((wide(near[:half]) + wide(up[:half])).astype(jnp.bfloat16), axis, 1)
    sum_down = shift((wide(near[half:]) + wide(down[:half])).astype(jnp.bfloat16), axis, -1)
    top = wide(own[:half]) + wide(down[half:]) + wide(sum_up)
    bottom = wide(own[half:]) + wide(up[half:]) + wide(sum_down)
    return jnp.concatenate([top, bottom], axis=0)


ANY = pl.BlockSpec(memory_space=pl.ANY)
SMEM = pl.BlockSpec(memory_space=pltpu.SMEM)
VMEM = pl.BlockSpec(memory_space=pltpu.VMEM)


def call(kernel, name, inputs, after, outs, cost, limit, scratch=(), aliases=None, in_specs=None, out_specs=None):
    count = len(inputs)

    def body(*refs):
        kernel(*refs[:count], *refs[count + len(after) :])

    return pl.pallas_call(
        body,
        in_specs=(in_specs or [VMEM] * count) + [ANY] * len(after),
        out_specs=out_specs or [VMEM] * len(outs),
        out_shape=outs,
        scratch_shapes=list(scratch),
        input_output_aliases=aliases or {},
        compiler_params=pltpu.CompilerParams(vmem_limit_bytes=limit * MIB),
        cost_estimate=cost,
        name=name,
    )(*inputs, *after)


def gate_kernel(weight_ref, out_ref, gate_ref, up_ref, *rest):
    grad_ref = rest[-1]
    hidden_grad = dot_last(weight_ref[...], out_ref[...])
    gate = gate_ref[...].astype(jnp.float32)
    sigma = 1.0 / (1.0 + jnp.exp(-gate))
    slope = sigma * (1.0 + gate * (1.0 - sigma))
    grad_ref[...] = (hidden_grad * up_ref[...].astype(jnp.float32) * slope).astype(grad_ref.dtype)


def gate_gradient(weight, out_grad, gate, up, after, rows):
    width, depth = weight.shape
    tokens = out_grad.shape[0]
    block = pl.BlockSpec((rows, tokens), lambda i: (i, 0))
    return pl.pallas_call(
        gate_kernel,
        grid=(width // rows,),
        in_specs=[
            pl.BlockSpec((rows, depth), lambda i: (i, 0)),
            pl.BlockSpec((tokens, depth), lambda i: (0, 0)),
            block,
            block,
        ]
        + [pl.BlockSpec(memory_space=pl.ANY)] * len(after),
        out_specs=block,
        out_shape=jax.ShapeDtypeStruct((width, tokens), jnp.bfloat16),
        compiler_params=pltpu.CompilerParams(vmem_limit_bytes=50 * MIB),
        cost_estimate=HEAVY,
        name="gate_gradient",
    )(weight, out_grad, gate, up, *after)


def squares_kernel(out_ref, act_ref, hidden_ref, gate_ref, total_ref):
    down = jnp.sum(dot_first(hidden_ref[...], hidden_ref[...]) * dot_last(out_ref[...], out_ref[...]))
    gate = jnp.sum(dot_first(gate_ref[...], gate_ref[...]) * dot_last(act_ref[...], act_ref[...]))
    row = lax.broadcasted_iota(jnp.int32, total_ref.shape, 0)
    total_ref[...] = jnp.where(row < RING, down, gate)


def factor_kernel(*refs):
    total = refs[0][...] + refs[1][...] + refs[2][...] + refs[3][...]
    row = lax.broadcasted_iota(jnp.int32, total.shape, 0)
    radius = jnp.where(row < RING, refs[4][0], refs[4][1])
    refs[5][...] = radius / jnp.maximum(jnp.sqrt(total), radius)
    refs[6][...] = jnp.ones_like(refs[6])


def stack_kernel(*refs):
    blocks, wide_ref = refs[:RING], refs[-1]
    for at, block in enumerate(blocks):
        wide_ref[at] = block[...]


def stacked(blocks, after):
    rows, tokens = blocks[0].shape
    steps = 4
    return pl.pallas_call(
        stack_kernel,
        grid=(steps,),
        in_specs=[pl.BlockSpec((rows // steps, tokens), lambda i: (i, 0))] * RING + [ANY] * len(after),
        out_specs=pl.BlockSpec((RING, rows // steps, tokens), lambda i: (0, i, 0)),
        out_shape=jax.ShapeDtypeStruct((RING, rows, tokens), blocks[0].dtype),
        compiler_params=pltpu.CompilerParams(vmem_limit_bytes=6 * MIB),
        cost_estimate=SMALL,
        name="stack",
    )(*blocks, *after)


def lefts_kernel(owner, goal_ref, mine_ref, other_ref, *refs):
    factors, outs, held_ref, sems = refs[:RING], refs[RING : 2 * RING], refs[-2], refs[-1]
    rows, tokens = outs[0].shape[0], mine_ref.shape[2]
    half = rows // 2
    far, after, before, own = range(4)
    halves = ((far, 0), (after, 1), (far, 1), (before, 0), (after, 0), (before, 1), (own, 0), (own, 1))
    waits = []
    for source, here in ((mine_ref, goal_ref[0] == owner), (other_ref, goal_ref[0] != owner)):
        copies = []
        for at, (goal, part) in enumerate(halves):
            start = pl.multiple_of(goal_ref[1 + goal] * rows + part * half, 16)
            for block in range(RING):
                lanes = pl.ds(block * tokens, tokens)
                target = held_ref.at[at // 2, pl.ds(at % 2 * half, half), lanes]
                copies.append(pltpu.make_async_copy(source.at[block, pl.ds(start, half), :], target, sems.at[at, block]))

        @pl.when(here)
        def _():
            for copy in copies:
                copy.start()

        waits = copies
    scale = jnp.concatenate([f[pl.ds(owner * RING, 1), :] for f in factors for _ in range(tokens // LANES)], axis=1)
    for at, out in enumerate(outs):
        for copy in waits[at * 2 * RING : (at + 1) * 2 * RING]:
            copy.wait()
        out[...] = (held_ref[at].astype(jnp.float32) * scale).astype(out.dtype)


def lefts_of(owner, goals, mine, other, factors, after):
    blocks, depth, tokens = mine.shape
    shape = (depth // RING, blocks * tokens)
    return call(
        functools.partial(lefts_kernel, owner),
        "lefts",
        [goals, mine, other, *factors],
        after,
        [jax.ShapeDtypeStruct(shape, mine.dtype)] * RING,
        SMALL,
        10,
        [pltpu.VMEM((RING, *shape), mine.dtype), pltpu.SemaphoreType.DMA((2 * RING, RING))],
        None,
        [SMEM, ANY, ANY] + [VMEM] * RING,
    )


def parts_kernel(place_ref, out_ref, act_ref, *refs):
    targets, window_ref, sems = refs[:RING], refs[RING], refs[RING + 1]
    rows, tokens = targets[0].shape
    owned = rows // RING
    for at in range(RING):
        place = place_ref[1 + at]

        @pl.when(place_ref[0] == 0)
        def _():
            lanes = pl.ds(pl.multiple_of(place * rows, LANES), rows)
            pltpu.make_async_copy(out_ref.at[:, lanes], window_ref.at[at], sems.at[at]).start()

        @pl.when(place_ref[0] != 0)
        def _():
            lanes = pl.ds(at * rows, rows)
            pltpu.make_async_copy(act_ref.at[:, lanes], window_ref.at[at], sems.at[at]).start()

    for at in range(RING):
        pltpu.make_async_copy(out_ref.at[:, pl.ds(0, rows)], window_ref.at[at], sems.at[at]).wait()
    for at in range(RING):
        turned = window_ref[at].T

        @pl.when(place_ref[0] == 0)
        def _():
            targets[at][...] = turned

        @pl.when(place_ref[0] != 0)
        def _():
            for goal in range(RING):
                for place in range(RING):

                    @pl.when(place_ref[1 + goal] == place)
                    def _():
                        targets[goal][pl.ds(at * owned, owned), :] = turned[place * owned : (place + 1) * owned]


def column_parts(out_grad, activations, places, after):
    tokens, depth = out_grad.shape
    rows = depth // RING
    return call(
        parts_kernel,
        "column_parts",
        [places, out_grad, activations],
        after,
        [jax.ShapeDtypeStruct((rows, tokens), out_grad.dtype)] * RING,
        SMALL,
        16,
        [pltpu.VMEM((RING, tokens, rows), out_grad.dtype), pltpu.SemaphoreType.DMA((RING,))],
        None,
        [SMEM, ANY, ANY],
    )


def local(activations, out_grad, gate_pre, up_pre, down_weight, clip_bounds):
    tokens, model_width = activations.shape
    full_hidden = gate_pre.shape[1] * RING * CORES
    example_total = RING * RING
    at_x, at_y, at_core = (lax.axis_index(a) for a in ("x", "y", "core"))

    gate, up = gate_pre.T, up_pre.T
    gate_val = gate.astype(jnp.float32)
    hidden = (jax.nn.silu(gate_val) * up.astype(jnp.float32)).astype(jnp.bfloat16)
    place = jnp.where(at_core == 0, at_x, at_y)
    parts = column_parts(out_grad, activations, jnp.stack([at_core] + [(place + s) % RING for s in STEPS]), [hidden])
    parts_here = [parts[0], *(shift(p, "spread", s) for p, s in zip(parts[1:], STEPS[1:], strict=True))]
    gate_grad = gate_gradient(down_weight.T, out_grad, gate, up, [hidden, parts[0]], 288)
    hidden_blocks, gate_blocks = around(hidden, "x"), around(gate_grad, "y")

    small = jax.ShapeDtypeStruct((2 * RING, LANES), jnp.float32)
    (squares,) = call(squares_kernel, "squares", [out_grad, activations, hidden, gate_grad], parts_here[1:], [small], SMALL, 10)
    sums = around(squares + swap(squares, "core", 1), "z")
    mine = stacked(parts_here, sums[1:])
    radius = clip_bounds * math.sqrt(float(model_width * full_hidden * SEQ))
    factor, unit = call(
        factor_kernel,
        "factor",
        [*sums, radius],
        [*hidden_blocks[1:3], *gate_blocks[1:3], mine],
        [small, jax.ShapeDtypeStruct((1, 1), jnp.float32)],
        SMALL,
        1,
        in_specs=[VMEM] * 4 + [SMEM],
    )
    other = swap(mine, "core", 1)
    far = [hidden_blocks[3], gate_blocks[3]]
    goals_of = lambda at: jnp.stack([at_core] + [(at + s) % RING for s in (2, 1, -1, 0)])
    along_x, along_y = around(factor, "x"), around(factor, "y")
    gate_lefts = lefts_of(1, goals_of(at_x), mine, other, along_y, [*far, *along_x[1:]])
    down_lefts = lefts_of(0, goals_of(at_y), mine, other, along_x, far)

    def wide(blocks):
        return jnp.concatenate([(unit * b.astype(jnp.float32)).astype(jnp.bfloat16) for b in blocks], axis=1)

    down = ring_reduce(down_lefts, wide(hidden_blocks), "y")
    gated = ring_reduce(gate_lefts, wide(gate_blocks), "x")
    return ((down / example_total).astype(jnp.bfloat16), (gated / example_total).astype(jnp.bfloat16))


def solution(mesh):
    torus = Mesh(mesh.devices.reshape(RING, RING, RING, 2), ("x", "y", "z", "core"))
    dp, tensor = ("x", "y"), ("z", "core")
    in_specs = (P(dp, None), P(dp, None), P(dp, tensor), P(dp, tensor), P(None, tensor), P())
    out_specs = (P(dp, tensor), P(dp, tensor))
    return jax.shard_map(local, mesh=torus, in_specs=in_specs, out_specs=out_specs, check_vma=False)
```

time: 337 us -> 147 us (0.44)
  the two profiles are of different devices: /device:TPU:0 before, /device:TPU:64 now
where the time goes in v1:
time: 147 us; the launch traced here: 146 us
  starting transfers between devices  50.2 us (34%)
  waiting for transfers between devices  34.1 us (23%)
  Pallas kernels  25.4 us (17%)
  matrix products  16.9 us (11%)
  other arithmetic  14 us (10%)
  local copies, waits for them, and re-layouts  4.47 us (3%)
    ppermute x23, starting transfers between devices, shift(): lax.ppermute(value, axis, [(i, (i + step) % RING) for i in range(RING)])  45 us
    ppermute x23, waiting for transfers between devices, shift(): lax.ppermute(value, axis, [(i, (i + step) % RING) for i in range(RING)])  32.9 us
    dot_general x8, matrix products, dot_last(): lax.dot_general(left, right, (((1,), (1,)), ((), ())), preferred_element_...  16.9 us
    pallas_call x1, Pallas kernels, gate_gradient(): pl.pallas_call(gate_kernel, grid=(width // rows,), in_specs=[pl.BlockSpec...  11.9 us
    pallas_call x5, Pallas kernels, call(): pl.pallas_call(body, in_specs=(in_specs or [VMEM] * count) + [ANY] * len(...  10.9 us
    convert_element_type x6, other arithmetic, wide(): (unit * b.astype(jnp.float32)).astype(jnp.bfloat16)  7.64 us
    ppermute x3, starting transfers between devices, shift(): return lax.ppermute(value, ('x', 'y', 'core'), pairs)  5.12 us
    unnamed x28, local copies, waits for them, and re-layouts  3.12 us
  transfers between devices with their start and end apart: 28, of which 10 were waited for; matrix products, arithmetic and copies ran while one was open for 17% of the time, Pallas kernels for 14%

profile of v1, /device:TPU:64, one launch (start us, length us, event | category | flops | bytes accessed | tf_op | source)
XLA Modules:
  0.0 146.1 jit_solution(9488269992530330769)
XLA Ops:
  0.7 2.1 %fusion.6.refs_3_.rest_0_.refs_2_ = bf16[1728,256]{1,0:T(8,128)(2,1)S(1)} fusion(bf16[256,1728]{0,1:T(8,128)(2,1)} %param.9, bf16[256,1728]{0,1:T(8,128)(2,1)} %param.8), kind=kLoop, calls=%fused_computation.28 | loop fusion | flops 3538944 | bytes 2654208 | tf_op jit(solution)/shard_map/convert_element_type | solution.py:270
  2.9 2.0 %copy-done.4 = bf16[256,5120]{1,0:T(8,128)(2,1)S(1)} copy-done((bf16[256,5120]{1,0:T(8,128)(2,1)S(1)}, bf16[256,5120]{1,0:T(8,128)(2,1)}, u32[]{:S(2)}) %copy-start.4) | copy-done | bytes 2621464
  4.9 3.2 %column_parts.1 = (bf16[1280,256]{1,0:T(8,128)(2,1)S(1)}, bf16[1280,256]{1,0:T(8,128)(2,1)}, bf16[1280,256]{1,0:T(8,128)(2,1)}, bf16[1280,256]{1,0:T(8,128)(2,1)}) custom-call(s32[5]{0:T(128)S(1)} %stack.61.refs_0_, bf16[256,5120]{1,0:T(8,128)(2,1)S(1)} %copy-done.2, bf16[256,5120]{1,0:T(8,128)(2,1)S(1)} %copy-done.4, ...), custom_call_target="tpu_custom_call" | custom-call | tf_op jit(solution)/shard_map/column_parts/pallas_call | solution.py:83
  8.1 1.6 %collective-permute-start = (bf16[1280,256]{1,0:T(8,128)(2,1)}, bf16[1280,256]{1,0:T(8,128)(2,1)}, u32[]{:S(2)}, u32[]{:S(2)}) collective-permute-start(bf16[1280,256]{1,0:T(8,128)(2,1)} %get-tuple-element.17), channel_id=1, source_target_pairs={{0,32},{1,9},{8,40},{9,17},{16,48},{17,25},{24,56},{25,1},{32,64},... | collective-permute-start | bytes 1966088 | tf_op jit(solution)/shard_map/ppermute | solution.py:40
  9.7 1.7 %collective-permute-start.1 = (bf16[1280,256]{1,0:T(8,128)(2,1)}, bf16[1280,256]{1,0:T(8,128)(2,1)}, u32[]{:S(2)}, u32[]{:S(2)}) collective-permute-start(bf16[1280,256]{1,0:T(8,128)(2,1)} %get-tuple-element.18), channel_id=1, source_target_pairs={{0,96},{1,25},{8,104},{9,1},{16,112},{17,9},{24,120},{25,17},{32,0... | collective-permute-start | bytes 1966088 | tf_op jit(solution)/shard_map/ppermute | solution.py:40
  11.5 1.8 %collective-permute-start.2 = (bf16[1280,256]{1,0:T(8,128)(2,1)}, bf16[1280,256]{1,0:T(8,128)(2,1)}, u32[]{:S(2)}, u32[]{:S(2)}) collective-permute-start(bf16[1280,256]{1,0:T(8,128)(2,1)} %get-tuple-element.19), channel_id=1, source_target_pairs={{0,64},{1,17},{8,72},{9,25},{16,80},{17,1},{24,88},{25,9},{32,96},... | collective-permute-start | bytes 1966088 | tf_op jit(solution)/shard_map/ppermute | solution.py:40
  13.3 11.9 %gate_gradient.1.refs_3_ = bf16[1728,256]{1,0:T(8,128)(2,1)} custom-call(bf16[1728,5120]{1,0:T(8,128)(2,1)} %bitcast.29, bf16[256,5120]{1,0:T(8,128)(2,1)} %refs_0_.1, bf16[1728,256]{1,0:T(8,128)(2,1)S(1)} %bitcast.28, bf16[1728,256]{1,0:T(8,128)(2,1)S(1)} %bitcast.27, bf16[1728,256]{1,0:T(8,128)(2,1)} %copy-done, ...), custom_call_target="tpu_custom_call" | custom-call | flops 999999995904 | bytes 1000000000 | tf_op jit(solution)/shard_map/gate_gradient/pallas_call | solution.py:109
  25.2 1.6 %collective-permute-start.10 = (bf16[1728,256]{1,0:T(8,128)(2,1)}, bf16[1728,256]{1,0:T(8,128)(2,1)S(1)}, u32[]{:S(2)}, u32[]{:S(2)}) collective-permute-start(bf16[1728,256]{1,0:T(8,128)(2,1)} %gate_gradient.1.refs_3_), channel_id=1, source_target_pairs={{0,8},{8,16},{16,24},{24,0},{1,9},{9,17},{17,25},{25,1},{2,10},{10... | collective-permute-start | bytes 2654216 | tf_op jit(solution)/shard_map/ppermute | solution.py:33
  26.8 1.7 %collective-permute-start.11 = (bf16[1728,256]{1,0:T(8,128)(2,1)}, bf16[1728,256]{1,0:T(8,128)(2,1)S(1)}, u32[]{:S(2)}, u32[]{:S(2)}) collective-permute-start(bf16[1728,256]{1,0:T(8,128)(2,1)} %gate_gradient.1.refs_3_), channel_id=1, source_target_pairs={{0,24},{8,0},{16,8},{24,16},{1,25},{9,1},{17,9},{25,17},{2,26},{10... | collective-permute-start | bytes 2654216 | tf_op jit(solution)/shard_map/ppermute | solution.py:33
  29.1 2.7 %collective-permute-start.9 = (bf16[1728,256]{1,0:T(8,128)(2,1)S(1)}, bf16[1728,256]{1,0:T(8,128)(2,1)}, u32[]{:S(2)}, u32[]{:S(2)}) collective-permute-start(bf16[1728,256]{1,0:T(8,128)(2,1)S(1)} %copy-done.1), channel_id=1, source_target_pairs={{0,96},{32,0},{64,32},{96,64},{1,97},{33,1},{65,33},{97,65},{2,98}... | collective-permute-start | bytes 2654216 | tf_op jit(solution)/shard_map/ppermute | solution.py:33
  31.7 3.4 %squares.1 = f32[8,128]{1,0:T(8,128)S(1)} custom-call(bf16[256,5120]{1,0:T(8,128)(2,1)S(1)} %copy-done.3, bf16[256,5120]{1,0:T(8,128)(2,1)S(1)} %copy-done.5, bf16[1728,256]{1,0:T(8,128)(2,1)S(1)} %copy-done.1, bf16[1728,256]{1,0:T(8,128)(2,1)} %gate_gradient.1.refs_3_, bf16[1280,256]{1,0:T(8,128)(2,1)} %collective-permute-done.refs_4_.refs_1_, ...), custom_call_target="tpu_custom_call" | custom-call | tf_op jit(solution)/shard_map/squares/pallas_call | solution.py:83
  35.2 1.2 collective-permute-done.3
  36.4 1.6 %collective-permute-start.4 = (f32[8,128]{1,0:T(8,128)S(1)}, f32[8,128]{1,0:T(8,128)S(1)}, u32[]{:S(2)}, u32[]{:S(2)}) collective-permute-start(f32[8,128]{1,0:T(8,128)S(1)} %add.122.refs_0_), channel_id=1, source_target_pairs={{0,2},{2,4},{4,6},{6,0},{1,3},{3,5},{5,7},{7,1},{8,10},{10,12},{12... | collective-permute-start | bytes 12296 | tf_op jit(solution)/shard_map/ppermute | solution.py:33
  38.0 2.0 %collective-permute-done.4.refs_4_.refs_1_ = f32[8,128]{1,0:T(8,128)S(1)} collective-permute-done((f32[8,128]{1,0:T(8,128)S(1)}, f32[8,128]{1,0:T(8,128)S(1)}, u32[]{:S(2)}, u32[]{:S(2)}) %collective-permute-start.4) | collective-permute-done | bytes 4128 | tf_op jit(solution)/shard_map/ppermute | solution.py:33
  40.6 3.0 %collective-permute-done.5.refs_5_.refs_2_ = f32[8,128]{1,0:T(8,128)S(1)} collective-permute-done((f32[8,128]{1,0:T(8,128)S(1)}, f32[8,128]{1,0:T(8,128)S(1)}, u32[]{:S(2)}, u32[]{:S(2)}) %collective-permute-start.5) | collective-permute-done | bytes 4128 | tf_op jit(solution)/shard_map/ppermute | solution.py:33
  43.6 1.7 %collective-permute-start.6 = (f32[8,128]{1,0:T(8,128)S(1)}, f32[8,128]{1,0:T(8,128)S(1)}, u32[]{:S(2)}, u32[]{:S(2)}) collective-permute-start(f32[8,128]{1,0:T(8,128)S(1)} %add.122.refs_0_), channel_id=1, source_target_pairs={{0,4},{2,6},{4,0},{6,2},{1,5},{3,7},{5,1},{7,3},{8,12},{10,14},{12... | collective-permute-start | bytes 12296 | tf_op jit(solution)/shard_map/ppermute | solution.py:33
  46.5 2.2 %collective-permute-done.6.refs_6_.refs_3_ = f32[8,128]{1,0:T(8,128)S(1)} collective-permute-done((f32[8,128]{1,0:T(8,128)S(1)}, f32[8,128]{1,0:T(8,128)S(1)}, u32[]{:S(2)}, u32[]{:S(2)}) %collective-permute-start.6) | collective-permute-done | bytes 4128 | tf_op jit(solution)/shard_map/ppermute | solution.py:33
  48.7 2.1 %collective-permute-start.16 = (bf16[1728,256]{1,0:T(8,128)(2,1)}, bf16[1728,256]{1,0:T(8,128)(2,1)S(1)}, u32[]{:S(2)}, u32[]{:S(2)}) collective-permute-start(bf16[1728,256]{1,0:T(8,128)(2,1)} %gate_gradient.1.refs_3_), channel_id=1, source_target_pairs={{0,16},{8,24},{16,0},{24,8},{1,17},{9,25},{17,1},{25,9},{2,18},{10... | collective-permute-start | bytes 2654216 | tf_op jit(solution)/shard_map/ppermute | solution.py:33
  50.7 1.1 copy-done.9
  51.8 2.6 %stack.67.refs_9_.refs_1_ = bf16[4,1280,256]{2,1,0:T(8,128)(2,1)S(1)} custom-call(bf16[1280,256]{1,0:T(8,128)(2,1)S(1)} %copy-done.9, bf16[1280,256]{1,0:T(8,128)(2,1)} %collective-permute-done.refs_4_.refs_1_, bf16[1280,256]{1,0:T(8,128)(2,1)} %collective-permute-done.1.refs_5_.refs_2_, bf16[1280,256]{1,0:T(8,128)(2,1)} %collective-permute-done.2.refs_6_.refs_3_, ...), custom_call_target="tpu_custom_call" | custom-call | tf_op jit(solution)/shard_map/stack/pallas_call | solution.py:151
  56.5 13.6 %collective-permute-start.13 = (f32[8,128]{1,0:T(8,128)S(1)}, f32[8,128]{1,0:T(8,128)S(1)}, u32[]{:S(2)}, u32[]{:S(2)}) collective-permute-start(f32[8,128]{1,0:T(8,128)S(1)} %get-tuple-element.20.refs_3_), channel_id=1, source_target_pairs={{0,96},{32,0},{64,32},{96,64},{1,97},{33,1},{65,33},{97,65},{2,98}... | collective-permute-start | bytes 12296 | tf_op jit(solution)/shard_map/ppermute | solution.py:33
  71.0 2.2 %multiply_convert_fusion.5 = (bf16[1728,256]{1,0:T(8,128)(2,1)S(1)}, bf16[1728,256]{1,0:T(8,128)(2,1)S(1)}) fusion(bf16[1728,256]{1,0:T(8,128)(2,1)} %collective-permute-done.9.refs_6_, f32[]{:T(128)} %bitcast.12, bf16[1728,256]{1,0:T(8,128)(2,1)S(1)} %collective-permute-done.8.refs_5_), kind=kLoop, calls=%fused_computation.25 | loop fusion | flops 2654208 | bytes 3538948 | tf_op jit(solution)/shard_map/convert_element_type | solution.py:300
  73.2 2.0 %multiply_convert_fusion.3 = bf16[1728,256]{1,0:T(8,128)(2,1)S(1)} fusion(bf16[1728,256]{1,0:T(8,128)(2,1)} %gate_gradient.1.refs_3_, f32[]{:T(128)} %bitcast.12), kind=kLoop, calls=%fused_computation.23 | loop fusion | flops 1327104 | bytes 1769476 | tf_op jit(solution)/shard_map/convert_element_type | solution.py:300
  76.0 2.3 %collective-permute-start.14 = (f32[8,128]{1,0:T(8,128)S(1)}, f32[8,128]{1,0:T(8,128)S(1)}, u32[]{:S(2)}, u32[]{:S(2)}) collective-permute-start(f32[8,128]{1,0:T(8,128)S(1)} %get-tuple-element.20.refs_3_), channel_id=1, source_target_pairs={{0,64},{32,96},{64,0},{96,32},{1,65},{33,97},{65,1},{97,33},{2,66}... | collective-permute-start | bytes 12296 | tf_op jit(solution)/shard_map/ppermute | solution.py:33
  79.3 3.6 %collective-permute-start.22 = (f32[8,128]{1,0:T(8,128)S(1)}, f32[8,128]{1,0:T(8,128)S(1)}, u32[]{:S(2)}, u32[]{:S(2)}) collective-permute-start(f32[8,128]{1,0:T(8,128)S(1)} %get-tuple-element.20.refs_3_), channel_id=1, source_target_pairs={{0,24},{8,0},{16,8},{24,16},{1,25},{9,1},{17,9},{25,17},{2,26},{10... | collective-permute-start | bytes 12296 | tf_op jit(solution)/shard_map/ppermute | solution.py:33
  82.9 1.5 collective-permute-start.23
  85.3 2.8 %collective-permute-done.23.refs_6_ = f32[8,128]{1,0:T(8,128)S(1)} collective-permute-done((f32[8,128]{1,0:T(8,128)S(1)}, f32[8,128]{1,0:T(8,128)S(1)}, u32[]{:S(2)}, u32[]{:S(2)}) %collective-permute-start.23) | collective-permute-done | bytes 4128 | tf_op jit(solution)/shard_map/ppermute | solution.py:33
  88.1 1.7 %lefts.3 = (bf16[320,1024]{1,0:T(8,128)(2,1)S(1)}, bf16[320,1024]{1,0:T(8,128)(2,1)S(1)}, bf16[320,1024]{1,0:T(8,128)(2,1)S(1)}, bf16[320,1024]{1,0:T(8,128)(2,1)S(1)}) custom-call(s32[5]{0:T(128)S(1)} %copy-done.11, bf16[4,1280,256]{2,1,0:T(8,128)(2,1)S(1)} %stack.67.refs_9_.refs_1_, bf16[4,1280,256]{2,1,0:T(8,128)(2,1)S(1)} %collective-permute-done.7.refs_2_, ...), custom_call_target="tpu_custom_call" | custom-call | tf_op jit(solution)/shard_map/lefts/pallas_call | solution.py:83
  89.7 2.1 %convolution_convert_fusion.3 = bf16[320,1728]{1,0:T(8,128)(2,1)S(1)} fusion(bf16[320,1024]{1,0:T(8,128)(2,1)S(1)} %get-tuple-element.26, bf16[1728,256]{1,0:T(8,128)(2,1)S(1)} %multiply_convert_fusion, bf16[1728,256]{1,0:T(8,128)(2,1)S(1)} %get-tuple-element.38, bf16[1728,256]{1,0:T(8,128)(2,1)S(1)} %get-tuple-element.39, ...), kind=kOutput, calls=%fused_computation.5 | convolution fusion | flops 1147170816 | bytes 5300224 | tf_op jit(solution)/shard_map/dot_general | solution.py:48
  91.8 2.1 %convolution_convert_fusion.2 = bf16[320,1728]{1,0:T(8,128)(2,1)S(1)} fusion(bf16[320,1024]{1,0:T(8,128)(2,1)S(1)} %get-tuple-element.27, bf16[1728,256]{1,0:T(8,128)(2,1)S(1)} %multiply_convert_fusion, bf16[1728,256]{1,0:T(8,128)(2,1)S(1)} %get-tuple-element.38, bf16[1728,256]{1,0:T(8,128)(2,1)S(1)} %get-tuple-element.39, ...), kind=kOutput, calls=%fused_computation.4 | convolution fusion | flops 1147170816 | bytes 5300224 | tf_op jit(solution)/shard_map/dot_general | solution.py:48
  94.0 1.2 collective-permute-start.24
  95.2 2.1 %convolution_convert_fusion = bf16[320,1728]{1,0:T(8,128)(2,1)S(1)} fusion(bf16[320,1024]{1,0:T(8,128)(2,1)S(1)} %get-tuple-element.29, bf16[1728,256]{1,0:T(8,128)(2,1)S(1)} %multiply_convert_fusion, bf16[1728,256]{1,0:T(8,128)(2,1)S(1)} %get-tuple-element.38, bf16[1728,256]{1,0:T(8,128)(2,1)S(1)} %get-tuple-element.39, ...), kind=kOutput, calls=%fused_computation.2 | convolution fusion | flops 1147170816 | bytes 5300224 | tf_op jit(solution)/shard_map/dot_general | solution.py:48
  98.3 1.6 %lefts.2 = (bf16[320,1024]{1,0:T(8,128)(2,1)S(1)}, bf16[320,1024]{1,0:T(8,128)(2,1)S(1)}, bf16[320,1024]{1,0:T(8,128)(2,1)S(1)}, bf16[320,1024]{1,0:T(8,128)(2,1)S(1)}) custom-call(s32[5]{0:T(128)S(1)} %copy-done.10, bf16[4,1280,256]{2,1,0:T(8,128)(2,1)S(1)} %stack.67.refs_9_.refs_1_, bf16[4,1280,256]{2,1,0:T(8,128)(2,1)S(1)} %collective-permute-done.7.refs_2_, ...), custom_call_target="tpu_custom_call" | custom-call | tf_op jit(solution)/shard_map/lefts/pallas_call | solution.py:83
  99.9 2.1 %convolution_convert_fusion.6 = bf16[320,1728]{1,0:T(8,128)(2,1)S(1)} fusion(bf16[320,1024]{1,0:T(8,128)(2,1)S(1)} %get-tuple-element.23, bf16[1728,256]{1,0:T(8,128)(2,1)S(1)} %multiply_convert_fusion.4, bf16[1728,256]{1,0:T(8,128)(2,1)S(1)} %get-tuple-element.40, bf16[1728,256]{1,0:T(8,128)(2,1)S(1)} %get-tuple-element.41, ...), kind=kOutput, calls=%fused_computation.8 | convolution fusion | flops 1147170816 | bytes 5300224 | tf_op jit(solution)/shard_map/dot_general | solution.py:48
  102.0 2.0 %collective-permute-start.17 = (bf16[320,1728]{1,0:T(8,128)(2,1)S(1)}, bf16[320,1728]{1,0:T(8,128)(2,1)S(1)}, u32[]{:S(2)}, u32[]{:S(2)}) collective-permute-start(bf16[320,1728]{1,0:T(8,128)(2,1)S(1)} %convolution_convert_fusion.6), channel_id=1, source_target_pairs={{0,24},{8,0},{16,8},{24,16},{1,25},{9,1},{17,9},{25,17},{2,26},{10... | collective-permute-start | bytes 3317768 | tf_op jit(solution)/shard_map/ppermute | solution.py:33
  104.1 2.1 %convolution_convert_fusion.4 = bf16[320,1728]{1,0:T(8,128)(2,1)S(1)} fusion(bf16[320,1024]{1,0:T(8,128)(2,1)S(1)} %get-tuple-element.25, bf16[1728,256]{1,0:T(8,128)(2,1)S(1)} %multiply_convert_fusion.4, bf16[1728,256]{1,0:T(8,128)(2,1)S(1)} %get-tuple-element.40, bf16[1728,256]{1,0:T(8,128)(2,1)S(1)} %get-tuple-element.41, ...), kind=kOutput, calls=%fused_computation.6 | convolution fusion | flops 1147170816 | bytes 5300224 | tf_op jit(solution)/shard_map/dot_general | solution.py:48
  106.5 2.1 %convolution_convert_fusion.1 = bf16[320,1728]{1,0:T(8,128)(2,1)S(1)} fusion(bf16[320,1024]{1,0:T(8,128)(2,1)S(1)} %get-tuple-element.28, bf16[1728,256]{1,0:T(8,128)(2,1)S(1)} %multiply_convert_fusion, bf16[1728,256]{1,0:T(8,128)(2,1)S(1)} %get-tuple-element.38, bf16[1728,256]{1,0:T(8,128)(2,1)S(1)} %get-tuple-element.39, ...), kind=kOutput, calls=%fused_computation.3 | convolution fusion | flops 1147170816 | bytes 5300224 | tf_op jit(solution)/shard_map/dot_general | solution.py:48
  108.6 2.1 %convolution_convert_fusion.7 = bf16[320,1728]{1,0:T(8,128)(2,1)S(1)} fusion(bf16[320,1024]{1,0:T(8,128)(2,1)S(1)} %get-tuple-element.21, bf16[1728,256]{1,0:T(8,128)(2,1)S(1)} %multiply_convert_fusion.4, bf16[1728,256]{1,0:T(8,128)(2,1)S(1)} %get-tuple-element.40, bf16[1728,256]{1,0:T(8,128)(2,1)S(1)} %get-tuple-element.41, ...), kind=kOutput, calls=%fused_computation.9 | convolution fusion | flops 1147170816 | bytes 5300224 | tf_op jit(solution)/shard_map/dot_general | solution.py:48
  110.8 8.7 %collective-permute-done.24 = bf16[320,1728]{1,0:T(8,128)(2,1)S(1)} collective-permute-done((bf16[320,1728]{1,0:T(8,128)(2,1)S(1)}, bf16[320,1728]{1,0:T(8,128)(2,1)S(1)}, u32[]{:S(2)}, u32[]{:S(2)}) %collective-permute-start.24) | collective-permute-done | bytes 1105952 | tf_op jit(solution)/shard_map/ppermute | solution.py:33
  119.5 4.2 %collective-permute-done.25 = bf16[320,1728]{1,0:T(8,128)(2,1)S(1)} collective-permute-done((bf16[320,1728]{1,0:T(8,128)(2,1)S(1)}, bf16[320,1728]{1,0:T(8,128)(2,1)S(1)}, u32[]{:S(2)}, u32[]{:S(2)}) %collective-permute-start.25) | collective-permute-done | bytes 1105952 | tf_op jit(solution)/shard_map/ppermute | solution.py:33
  124.1 3.2 %collective-permute-start.27 = (bf16[160,1728]{1,0:T(8,128)(2,1)S(1)}, bf16[160,1728]{1,0:T(8,128)(2,1)S(1)}, u32[]{:S(2)}, u32[]{:S(2)}) collective-permute-start(bf16[160,1728]{1,0:T(8,128)(2,1)S(1)} %get-tuple-element.33), channel_id=1, source_target_pairs={{0,96},{32,0},{64,32},{96,64},{1,97},{33,1},{65,33},{97,65},{2,98}... | collective-permute-start | bytes 1658888 | tf_op jit(solution)/shard_map/ppermute | solution.py:33
  127.3 2.1 %convolution_convert_fusion.5 = bf16[320,1728]{1,0:T(8,128)(2,1)S(1)} fusion(bf16[320,1024]{1,0:T(8,128)(2,1)S(1)} %get-tuple-element.24, bf16[1728,256]{1,0:T(8,128)(2,1)S(1)} %multiply_convert_fusion.4, bf16[1728,256]{1,0:T(8,128)(2,1)S(1)} %get-tuple-element.40, bf16[1728,256]{1,0:T(8,128)(2,1)S(1)} %get-tuple-element.41, ...), kind=kOutput, calls=%fused_computation.7 | convolution fusion | flops 1147170816 | bytes 5300224 | tf_op jit(solution)/shard_map/dot_general | solution.py:48
  129.4 2.5 %collective-permute-done.18 = bf16[320,1728]{1,0:T(8,128)(2,1)S(1)} collective-permute-done((bf16[320,1728]{1,0:T(8,128)(2,1)S(1)}, bf16[320,1728]{1,0:T(8,128)(2,1)S(1)}, u32[]{:S(2)}, u32[]{:S(2)}) %collective-permute-start.18) | collective-permute-done | bytes 1105952 | tf_op jit(solution)/shard_map/ppermute | solution.py:33
  132.3 3.2 %collective-permute-start.20 = (bf16[160,1728]{1,0:T(8,128)(2,1)S(1)}, bf16[160,1728]{1,0:T(8,128)(2,1)S(1)}, u32[]{:S(2)}, u32[]{:S(2)}) collective-permute-start(bf16[160,1728]{1,0:T(8,128)(2,1)S(1)} %get-tuple-element.37), channel_id=1, source_target_pairs={{0,24},{8,0},{16,8},{24,16},{1,25},{9,1},{17,9},{25,17},{2,26},{10... | collective-permute-start | bytes 1658888 | tf_op jit(solution)/shard_map/ppermute | solution.py:33
  135.5 1.6 %collective-permute-done.26 = bf16[160,1728]{1,0:T(8,128)(2,1)S(1)} collective-permute-done((bf16[160,1728]{1,0:T(8,128)(2,1)S(1)}, bf16[160,1728]{1,0:T(8,128)(2,1)S(1)}, u32[]{:S(2)}, u32[]{:S(2)}) %collective-permute-start.26) | collective-permute-done | bytes 552992 | tf_op jit(solution)/shard_map/ppermute | solution.py:33
  137.6 1.1 fusion.1
  138.8 5.8 %collective-permute-done.19 = bf16[160,1728]{1,0:T(8,128)(2,1)S(1)} collective-permute-done((bf16[160,1728]{1,0:T(8,128)(2,1)S(1)}, bf16[160,1728]{1,0:T(8,128)(2,1)S(1)}, u32[]{:S(2)}, u32[]{:S(2)}) %collective-permute-start.19) | collective-permute-done | bytes 552992 | tf_op jit(solution)/shard_map/ppermute | solution.py:33
  145.0 1.1 fusion
  (69 shorter events, 11.2 us)
Async XLA Ops:
  0.6 2.3 %copy-start.2 = (bf16[256,5120]{1,0:T(8,128)(2,1)S(1)}, bf16[256,5120]{1,0:T(8,128)(2,1)}, u32[]{:S(2)}) copy-start(bf16[256,5120]{1,0:T(8,128)(2,1)} %refs_0_.1) | copy-start | bytes 7864324
  2.8 5.3 %copy-start = (bf16[1728,256]{1,0:T(8,128)(2,1)}, bf16[1728,256]{1,0:T(8,128)(2,1)S(1)}, u32[]{:S(2)}) copy-start(bf16[1728,256]{1,0:T(8,128)(2,1)S(1)} %fusion.6.refs_3_.rest_0_.refs_2_) | copy-start | bytes 2654212
  2.9 2.0 %copy-start.4 = (bf16[256,5120]{1,0:T(8,128)(2,1)S(1)}, bf16[256,5120]{1,0:T(8,128)(2,1)}, u32[]{:S(2)}) copy-start(bf16[256,5120]{1,0:T(8,128)(2,1)} %refs_1_.3) | copy-start | bytes 7864324
  4.9 8.4 %copy-start.6 = (bf16[256,1728]{0,1:T(8,128)(2,1)S(1)}, bf16[256,1728]{0,1:T(8,128)(2,1)}, u32[]{:S(2)}) copy-start(bf16[256,1728]{0,1:T(8,128)(2,1)} %param.9) | copy-start | bytes 2654212
  4.9 8.4 %copy-start.7 = (bf16[256,1728]{0,1:T(8,128)(2,1)S(1)}, bf16[256,1728]{0,1:T(8,128)(2,1)}, u32[]{:S(2)}) copy-start(bf16[256,1728]{0,1:T(8,128)(2,1)} %param.8) | copy-start | bytes 2654212
  8.1 17.1 %copy-start.8 = (bf16[1280,256]{1,0:T(8,128)(2,1)}, bf16[1280,256]{1,0:T(8,128)(2,1)S(1)}, u32[]{:S(2)}) copy-start(bf16[1280,256]{1,0:T(8,128)(2,1)S(1)} %get-tuple-element.16.rest_1_.refs_0_) | copy-start | bytes 1966084
  8.1 20.3 %collective-permute-start = (bf16[1280,256]{1,0:T(8,128)(2,1)}, bf16[1280,256]{1,0:T(8,128)(2,1)}, u32[]{:S(2)}, u32[]{:S(2)}) collective-permute-start(bf16[1280,256]{1,0:T(8,128)(2,1)} %get-tuple-element.17), channel_id=1, source_target_pairs={{0,32},{1,9},{8,40},{9,17},{16,48},{17,25},{24,56},{25,1},{32,64},... | collective-permute-start | bytes 1966088 | tf_op jit(solution)/shard_map/ppermute | solution.py:40
  9.7 19.4 %collective-permute-start.1 = (bf16[1280,256]{1,0:T(8,128)(2,1)}, bf16[1280,256]{1,0:T(8,128)(2,1)}, u32[]{:S(2)}, u32[]{:S(2)}) collective-permute-start(bf16[1280,256]{1,0:T(8,128)(2,1)} %get-tuple-element.18), channel_id=1, source_target_pairs={{0,96},{1,25},{8,104},{9,1},{16,112},{17,9},{24,120},{25,17},{32,0... | collective-permute-start | bytes 1966088 | tf_op jit(solution)/shard_map/ppermute | solution.py:40
  11.5 20.3 %collective-permute-start.2 = (bf16[1280,256]{1,0:T(8,128)(2,1)}, bf16[1280,256]{1,0:T(8,128)(2,1)}, u32[]{:S(2)}, u32[]{:S(2)}) collective-permute-start(bf16[1280,256]{1,0:T(8,128)(2,1)} %get-tuple-element.19), channel_id=1, source_target_pairs={{0,64},{1,17},{8,72},{9,25},{16,80},{17,1},{24,88},{25,9},{32,96},... | collective-permute-start | bytes 1966088 | tf_op jit(solution)/shard_map/ppermute | solution.py:40
  13.3 15.2 %copy-start.1 = (bf16[1728,256]{1,0:T(8,128)(2,1)S(1)}, bf16[1728,256]{1,0:T(8,128)(2,1)}, u32[]{:S(2)}) copy-start(bf16[1728,256]{1,0:T(8,128)(2,1)} %copy-done) | copy-start | bytes 2654212
  13.3 18.5 %copy-start.3 = (bf16[256,5120]{1,0:T(8,128)(2,1)S(1)}, bf16[256,5120]{1,0:T(8,128)(2,1)}, u32[]{:S(2)}) copy-start(bf16[256,5120]{1,0:T(8,128)(2,1)} %refs_0_.1) | copy-start | bytes 7864324
  13.3 18.4 %copy-start.5 = (bf16[256,5120]{1,0:T(8,128)(2,1)S(1)}, bf16[256,5120]{1,0:T(8,128)(2,1)}, u32[]{:S(2)}) copy-start(bf16[256,5120]{1,0:T(8,128)(2,1)} %refs_1_.3) | copy-start | bytes 7864324
  25.2 14.8 %copy-start.13 = (f32[2]{0:T(128)S(1)}, f32[2]{0:T(128)}, u32[]{:S(2)}) copy-start(f32[2]{0:T(128)} %param.11) | copy-start | bytes 28
  25.2 29.2 %collective-permute-start.10 = (bf16[1728,256]{1,0:T(8,128)(2,1)}, bf16[1728,256]{1,0:T(8,128)(2,1)S(1)}, u32[]{:S(2)}, u32[]{:S(2)}) collective-permute-start(bf16[1728,256]{1,0:T(8,128)(2,1)} %gate_gradient.1.refs_3_), channel_id=1, source_target_pairs={{0,8},{8,16},{16,24},{24,0},{1,9},{9,17},{17,25},{25,1},{2,10},{10... | collective-permute-start | bytes 2654216 | tf_op jit(solution)/shard_map/ppermute | solution.py:33
  26.8 28.1 %collective-permute-start.11 = (bf16[1728,256]{1,0:T(8,128)(2,1)}, bf16[1728,256]{1,0:T(8,128)(2,1)S(1)}, u32[]{:S(2)}, u32[]{:S(2)}) collective-permute-start(bf16[1728,256]{1,0:T(8,128)(2,1)} %gate_gradient.1.refs_3_), channel_id=1, source_target_pairs={{0,24},{8,0},{16,8},{24,16},{1,25},{9,1},{17,9},{25,17},{2,26},{10... | collective-permute-start | bytes 2654216 | tf_op jit(solution)/shard_map/ppermute | solution.py:33
  28.5 26.5 %collective-permute-start.8 = (bf16[1728,256]{1,0:T(8,128)(2,1)S(1)}, bf16[1728,256]{1,0:T(8,128)(2,1)S(1)}, u32[]{:S(2)}, u32[]{:S(2)}) collective-permute-start(bf16[1728,256]{1,0:T(8,128)(2,1)S(1)} %copy-done.1), channel_id=1, source_target_pairs={{0,32},{32,64},{64,96},{96,0},{1,33},{33,65},{65,97},{97,1},{2,34}... | collective-permute-start | bytes 2654216 | tf_op jit(solution)/shard_map/ppermute | solution.py:33
  29.1 25.9 %collective-permute-start.9 = (bf16[1728,256]{1,0:T(8,128)(2,1)S(1)}, bf16[1728,256]{1,0:T(8,128)(2,1)}, u32[]{:S(2)}, u32[]{:S(2)}) collective-permute-start(bf16[1728,256]{1,0:T(8,128)(2,1)S(1)} %copy-done.1), channel_id=1, source_target_pairs={{0,96},{32,0},{64,32},{96,64},{1,97},{33,1},{65,33},{97,65},{2,98}... | collective-permute-start | bytes 2654216 | tf_op jit(solution)/shard_map/ppermute | solution.py:33
  35.1 1.2 collective-permute-start.3
  36.4 3.6 %collective-permute-start.4 = (f32[8,128]{1,0:T(8,128)S(1)}, f32[8,128]{1,0:T(8,128)S(1)}, u32[]{:S(2)}, u32[]{:S(2)}) collective-permute-start(f32[8,128]{1,0:T(8,128)S(1)} %add.122.refs_0_), channel_id=1, source_target_pairs={{0,2},{2,4},{4,6},{6,0},{1,3},{3,5},{5,7},{7,1},{8,10},{10,12},{12... | collective-permute-start | bytes 12296 | tf_op jit(solution)/shard_map/ppermute | solution.py:33
  40.0 3.6 %collective-permute-start.5 = (f32[8,128]{1,0:T(8,128)S(1)}, f32[8,128]{1,0:T(8,128)S(1)}, u32[]{:S(2)}, u32[]{:S(2)}) collective-permute-start(f32[8,128]{1,0:T(8,128)S(1)} %add.122.refs_0_), channel_id=1, source_target_pairs={{0,6},{2,0},{4,2},{6,4},{1,7},{3,1},{5,3},{7,5},{8,14},{10,8},{12,... | collective-permute-start | bytes 12296 | tf_op jit(solution)/shard_map/ppermute | solution.py:33
  43.6 5.1 %collective-permute-start.6 = (f32[8,128]{1,0:T(8,128)S(1)}, f32[8,128]{1,0:T(8,128)S(1)}, u32[]{:S(2)}, u32[]{:S(2)}) collective-permute-start(f32[8,128]{1,0:T(8,128)S(1)} %add.122.refs_0_), channel_id=1, source_target_pairs={{0,4},{2,6},{4,0},{6,2},{1,5},{3,7},{5,1},{7,3},{8,12},{10,14},{12... | collective-permute-start | bytes 12296 | tf_op jit(solution)/shard_map/ppermute | solution.py:33
  48.7 27.3 %collective-permute-start.16 = (bf16[1728,256]{1,0:T(8,128)(2,1)}, bf16[1728,256]{1,0:T(8,128)(2,1)S(1)}, u32[]{:S(2)}, u32[]{:S(2)}) collective-permute-start(bf16[1728,256]{1,0:T(8,128)(2,1)} %gate_gradient.1.refs_3_), channel_id=1, source_target_pairs={{0,16},{8,24},{16,0},{24,8},{1,17},{9,25},{17,1},{25,9},{2,18},{10... | collective-permute-start | bytes 2654216 | tf_op jit(solution)/shard_map/ppermute | solution.py:33
  50.7 1.1 copy-start.9
  51.8 3.1 %copy-start.12 = (f32[2]{0:T(128)S(1)}, f32[2]{0:T(128)}, u32[]{:S(2)}) copy-start(f32[2]{0:T(128)} %broadcast_multiply_fusion.refs_4_) | copy-start | bytes 28
  54.4 24.8 %collective-permute-start.15 = (bf16[1728,256]{1,0:T(8,128)(2,1)S(1)}, bf16[1728,256]{1,0:T(8,128)(2,1)S(1)}, u32[]{:S(2)}, u32[]{:S(2)}) collective-permute-start(bf16[1728,256]{1,0:T(8,128)(2,1)S(1)} %copy-done.1), channel_id=1, source_target_pairs={{0,64},{32,96},{64,0},{96,32},{1,65},{33,97},{65,1},{97,33},{2,66}... | collective-permute-start | bytes 2654216 | tf_op jit(solution)/shard_map/ppermute | solution.py:33
  54.9 33.1 %collective-permute-start.7 = (bf16[4,1280,256]{2,1,0:T(8,128)(2,1)S(1)}, bf16[4,1280,256]{2,1,0:T(8,128)(2,1)S(1)}, u32[]{:S(2)}, u32[]{:S(2)}) collective-permute-start(bf16[4,1280,256]{2,1,0:T(8,128)(2,1)S(1)} %stack.67.refs_9_.refs_1_), channel_id=1, source_target_pairs={{0,1},{1,0},{2,3},{3,2},{4,5},{5,4},{6,7},{7,6},{8,9},{9,8},{10,11... | collective-permute-start | bytes 7864328 | tf_op jit(solution)/shard_map/ppermute | solution.py:44
  56.0 23.3 %collective-permute-start.12 = (f32[8,128]{1,0:T(8,128)S(1)}, f32[8,128]{1,0:T(8,128)S(1)}, u32[]{:S(2)}, u32[]{:S(2)}) collective-permute-start(f32[8,128]{1,0:T(8,128)S(1)} %get-tuple-element.20.refs_3_), channel_id=1, source_target_pairs={{0,32},{32,64},{64,96},{96,0},{1,33},{33,65},{65,97},{97,1},{2,34}... | collective-permute-start | bytes 12296 | tf_op jit(solution)/shard_map/ppermute | solution.py:33
  56.5 26.5 %collective-permute-start.13 = (f32[8,128]{1,0:T(8,128)S(1)}, f32[8,128]{1,0:T(8,128)S(1)}, u32[]{:S(2)}, u32[]{:S(2)}) collective-permute-start(f32[8,128]{1,0:T(8,128)S(1)} %get-tuple-element.20.refs_3_), channel_id=1, source_target_pairs={{0,96},{32,0},{64,32},{96,64},{1,97},{33,1},{65,33},{97,65},{2,98}... | collective-permute-start | bytes 12296 | tf_op jit(solution)/shard_map/ppermute | solution.py:33
  75.2 12.9 %copy-start.11 = (s32[5]{0:T(128)S(1)}, s32[5]{0:T(128)}, u32[]{:S(2)}) copy-start(s32[5]{0:T(128)} %stack.66.refs_0_) | copy-start | bytes 64
  76.0 9.2 %collective-permute-start.14 = (f32[8,128]{1,0:T(8,128)S(1)}, f32[8,128]{1,0:T(8,128)S(1)}, u32[]{:S(2)}, u32[]{:S(2)}) collective-permute-start(f32[8,128]{1,0:T(8,128)S(1)} %get-tuple-element.20.refs_3_), channel_id=1, source_target_pairs={{0,64},{32,96},{64,0},{96,32},{1,65},{33,97},{65,1},{97,33},{2,66}... | collective-permute-start | bytes 12296 | tf_op jit(solution)/shard_map/ppermute | solution.py:33
  79.2 6.0 %collective-permute-start.21 = (f32[8,128]{1,0:T(8,128)S(1)}, f32[8,128]{1,0:T(8,128)S(1)}, u32[]{:S(2)}, u32[]{:S(2)}) collective-permute-start(f32[8,128]{1,0:T(8,128)S(1)} %get-tuple-element.20.refs_3_), channel_id=1, source_target_pairs={{0,8},{8,16},{16,24},{24,0},{1,9},{9,17},{17,25},{25,1},{2,10},{10... | collective-permute-start | bytes 12296 | tf_op jit(solution)/shard_map/ppermute | solution.py:33
  79.3 6.0 %collective-permute-start.22 = (f32[8,128]{1,0:T(8,128)S(1)}, f32[8,128]{1,0:T(8,128)S(1)}, u32[]{:S(2)}, u32[]{:S(2)}) collective-permute-start(f32[8,128]{1,0:T(8,128)S(1)} %get-tuple-element.20.refs_3_), channel_id=1, source_target_pairs={{0,24},{8,0},{16,8},{24,16},{1,25},{9,1},{17,9},{25,17},{2,26},{10... | collective-permute-start | bytes 12296 | tf_op jit(solution)/shard_map/ppermute | solution.py:33
  82.9 5.1 %collective-permute-start.23 = (f32[8,128]{1,0:T(8,128)S(1)}, f32[8,128]{1,0:T(8,128)S(1)}, u32[]{:S(2)}, u32[]{:S(2)}) collective-permute-start(f32[8,128]{1,0:T(8,128)S(1)} %get-tuple-element.20.refs_3_), channel_id=1, source_target_pairs={{0,16},{8,24},{16,0},{24,8},{1,17},{9,25},{17,1},{25,9},{2,18},{10... | collective-permute-start | bytes 12296 | tf_op jit(solution)/shard_map/ppermute | solution.py:33
  94.0 25.5 %collective-permute-start.24 = (bf16[320,1728]{1,0:T(8,128)(2,1)S(1)}, bf16[320,1728]{1,0:T(8,128)(2,1)S(1)}, u32[]{:S(2)}, u32[]{:S(2)}) collective-permute-start(bf16[320,1728]{1,0:T(8,128)(2,1)S(1)} %convolution_convert_fusion.2), channel_id=1, source_target_pairs={{0,96},{32,0},{64,32},{96,64},{1,97},{33,1},{65,33},{97,65},{2,98}... | collective-permute-start | bytes 3317768 | tf_op jit(solution)/shard_map/ppermute | solution.py:33
  95.2 3.1 %copy-start.10 = (s32[5]{0:T(128)S(1)}, s32[5]{0:T(128)}, u32[]{:S(2)}) copy-start(s32[5]{0:T(128)} %stack.56.refs_0_) | copy-start | bytes 64
  97.3 26.4 %collective-permute-start.25 = (bf16[320,1728]{1,0:T(8,128)(2,1)S(1)}, bf16[320,1728]{1,0:T(8,128)(2,1)S(1)}, u32[]{:S(2)}, u32[]{:S(2)}) collective-permute-start(bf16[320,1728]{1,0:T(8,128)(2,1)S(1)} %convolution_convert_fusion), channel_id=1, source_target_pairs={{0,32},{32,64},{64,96},{96,0},{1,33},{33,65},{65,97},{97,1},{2,34}... | collective-permute-start | bytes 3317768 | tf_op jit(solution)/shard_map/ppermute | solution.py:33
  102.0 27.4 %collective-permute-start.17 = (bf16[320,1728]{1,0:T(8,128)(2,1)S(1)}, bf16[320,1728]{1,0:T(8,128)(2,1)S(1)}, u32[]{:S(2)}, u32[]{:S(2)}) collective-permute-start(bf16[320,1728]{1,0:T(8,128)(2,1)S(1)} %convolution_convert_fusion.6), channel_id=1, source_target_pairs={{0,24},{8,0},{16,8},{24,16},{1,25},{9,1},{17,9},{25,17},{2,26},{10... | collective-permute-start | bytes 3317768 | tf_op jit(solution)/shard_map/ppermute | solution.py:33
  106.2 25.8 %collective-permute-start.18 = (bf16[320,1728]{1,0:T(8,128)(2,1)S(1)}, bf16[320,1728]{1,0:T(8,128)(2,1)S(1)}, u32[]{:S(2)}, u32[]{:S(2)}) collective-permute-start(bf16[320,1728]{1,0:T(8,128)(2,1)S(1)} %convolution_convert_fusion.4), channel_id=1, source_target_pairs={{0,8},{8,16},{16,24},{24,0},{1,9},{9,17},{17,25},{25,1},{2,10},{10... | collective-permute-start | bytes 3317768 | tf_op jit(solution)/shard_map/ppermute | solution.py:33
  124.0 13.2 %collective-permute-start.26 = (bf16[160,1728]{1,0:T(8,128)(2,1)S(1)}, bf16[160,1728]{1,0:T(8,128)(2,1)S(1)}, u32[]{:S(2)}, u32[]{:S(2)}) collective-permute-start(bf16[160,1728]{1,0:T(8,128)(2,1)S(1)} %get-tuple-element.32), channel_id=1, source_target_pairs={{0,32},{32,64},{64,96},{96,0},{1,33},{33,65},{65,97},{97,1},{2,34}... | collective-permute-start | bytes 1658888 | tf_op jit(solution)/shard_map/ppermute | solution.py:33
  124.1 13.1 %collective-permute-start.27 = (bf16[160,1728]{1,0:T(8,128)(2,1)S(1)}, bf16[160,1728]{1,0:T(8,128)(2,1)S(1)}, u32[]{:S(2)}, u32[]{:S(2)}) collective-permute-start(bf16[160,1728]{1,0:T(8,128)(2,1)S(1)} %get-tuple-element.33), channel_id=1, source_target_pairs={{0,96},{32,0},{64,32},{96,64},{1,97},{33,1},{65,33},{97,65},{2,98}... | collective-permute-start | bytes 1658888 | tf_op jit(solution)/shard_map/ppermute | solution.py:33
  132.2 12.3 %collective-permute-start.19 = (bf16[160,1728]{1,0:T(8,128)(2,1)S(1)}, bf16[160,1728]{1,0:T(8,128)(2,1)S(1)}, u32[]{:S(2)}, u32[]{:S(2)}) collective-permute-start(bf16[160,1728]{1,0:T(8,128)(2,1)S(1)} %get-tuple-element.36), channel_id=1, source_target_pairs={{0,8},{8,16},{16,24},{24,0},{1,9},{9,17},{17,25},{25,1},{2,10},{10... | collective-permute-start | bytes 1658888 | tf_op jit(solution)/shard_map/ppermute | solution.py:33
  132.3 12.3 %collective-permute-start.20 = (bf16[160,1728]{1,0:T(8,128)(2,1)S(1)}, bf16[160,1728]{1,0:T(8,128)(2,1)S(1)}, u32[]{:S(2)}, u32[]{:S(2)}) collective-permute-start(bf16[160,1728]{1,0:T(8,128)(2,1)S(1)} %get-tuple-element.37), channel_id=1, source_target_pairs={{0,24},{8,0},{16,8},{24,16},{1,25},{9,1},{17,9},{25,17},{2,26},{10... | collective-permute-start | bytes 1658888 | tf_op jit(solution)/shard_map/ppermute | solution.py:33

commit v2 on v1

--- a/solution.py
+++ b/solution.py
@@ -94,18 +94,20 @@
 
 
 def gate_kernel(weight_ref, out_ref, gate_ref, up_ref, *rest):
-    grad_ref = rest[-1]
+    hidden_ref, grad_ref = rest[-2:]
+    gate = gate_ref[...].astype(jnp.float32)
+    up = up_ref[...].astype(jnp.float32)
+    sigma = 1.0 / (1.0 + jnp.exp(-gate))
+    hidden_ref[...] = (gate * sigma * up).astype(hidden_ref.dtype)
     hidden_grad = dot_last(weight_ref[...], out_ref[...])
-    gate = gate_ref[...].astype(jnp.float32)
-    sigma = 1.0 / (1.0 + jnp.exp(-gate))
-    slope = sigma * (1.0 + gate * (1.0 - sigma))
-    grad_ref[...] = (hidden_grad * up_ref[...].astype(jnp.float32) * slope).astype(grad_ref.dtype)
-
-
-def gate_gradient(weight, out_grad, gate, up, after, rows):
+    grad_ref[...] = (hidden_grad * up * (sigma * (1.0 + gate * (1.0 - sigma)))).astype(grad_ref.dtype)
+
+
+def hidden_and_gradient(weight, out_grad, gate, up, after, rows):
     width, depth = weight.shape
     tokens = out_grad.shape[0]
     block = pl.BlockSpec((rows, tokens), lambda i: (i, 0))
+    shape = jax.ShapeDtypeStruct((width, tokens), jnp.bfloat16)
     return pl.pallas_call(
         gate_kernel,
         grid=(width // rows,),
@@ -115,12 +117,12 @@
             block,
             block,
         ]
-        + [pl.BlockSpec(memory_space=pl.ANY)] * len(after),
-        out_specs=block,
-        out_shape=jax.ShapeDtypeStruct((width, tokens), jnp.bfloat16),
+        + [ANY] * len(after),
+        out_specs=[block, block],
+        out_shape=[shape, shape],
         compiler_params=pltpu.CompilerParams(vmem_limit_bytes=50 * MIB),
         cost_estimate=HEAVY,
-        name="gate_gradient",
+        name="hidden_and_gradient",
     )(weight, out_grad, gate, up, *after)
 
 
@@ -131,12 +133,32 @@
     total_ref[...] = jnp.where(row < RING, down, gate)
 
 
-def factor_kernel(*refs):
+def copy_kernel(source_ref, target_ref):
+    target_ref[...] = source_ref[...]
+
+
+def pack_kernel(*refs):
+    for at in range(RING - 1):
+        refs[RING + 1][at] = refs[at][...]
+
+
+def factor_kernel(unit, *refs):
     total = refs[0][...] + refs[1][...] + refs[2][...] + refs[3][...]
     row = lax.broadcasted_iota(jnp.int32, total.shape, 0)
-    radius = jnp.where(row < RING, refs[4][0], refs[4][1])
+    radius = jnp.where(row < RING, refs[4][0], refs[4][1]) * unit
     refs[5][...] = radius / jnp.maximum(jnp.sqrt(total), radius)
-    refs[6][...] = jnp.ones_like(refs[6])
+
+
+def wide_kernel(*refs):
+    tokens = refs[0].shape[1]
+    for at in range(RING):
+        refs[RING][:, pl.ds(at * tokens, tokens)] = refs[at][...]
+
+
+def wide(blocks, after):
+    rows, tokens = blocks[0].shape
+    shape = jax.ShapeDtypeStruct((rows, RING * tokens), blocks[0].dtype)
+    return call(wide_kernel, "wide", blocks, after, [shape], SMALL, 12)[0]
 
 
 def stack_kernel(*refs):
@@ -160,17 +182,19 @@
     )(*blocks, *after)
 
 
-def lefts_kernel(owner, goal_ref, mine_ref, other_ref, *refs):
-    factors, outs, held_ref, sems = refs[:RING], refs[RING : 2 * RING], refs[-2], refs[-1]
+def lefts_kernel(owner, axis, mine_ref, other_ref, *refs):
+    factor_ref, mine_factors, other_factors = refs[:3]
+    outs, held_ref, sems = refs[3 : 3 + RING], refs[-2], refs[-1]
     rows, tokens = outs[0].shape[0], mine_ref.shape[2]
     half = rows // 2
-    far, after, before, own = range(4)
+    core, at_axis = lax.axis_index("core"), lax.axis_index(axis)
+    far, after, before, own = 2, 1, RING - 1, 0
     halves = ((far, 0), (after, 1), (far, 1), (before, 0), (after, 0), (before, 1), (own, 0), (own, 1))
     waits = []
-    for source, here in ((mine_ref, goal_ref[0] == owner), (other_ref, goal_ref[0] != owner)):
+    for source, here in ((mine_ref, core == owner), (other_ref, core != owner)):
         copies = []
         for at, (goal, part) in enumerate(halves):
-            start = pl.multiple_of(goal_ref[1 + goal] * rows + part * half, 16)
+            start = pl.multiple_of(lax.rem(at_axis + goal, RING) * rows + part * half, 16)
             for block in range(RING):
                 lanes = pl.ds(block * tokens, tokens)
                 target = held_ref.at[at // 2, pl.ds(at % 2 * half, half), lanes]
@@ -182,43 +206,50 @@
                 copy.start()
 
         waits = copies
-    scale = jnp.concatenate([f[pl.ds(owner * RING, 1), :] for f in factors for _ in range(tokens // LANES)], axis=1)
+    line = pl.ds(owner * RING, 1)
+    scales = [factor_ref[line, :]]
+    for at in range(RING - 1):
+        scales.append(jnp.where(core == owner, mine_factors[at, line, :], other_factors[at, line, :]))
+    scale = jnp.concatenate([f for f in scales for _ in range(tokens // LANES)], axis=1)
     for at, out in enumerate(outs):
         for copy in waits[at * 2 * RING : (at + 1) * 2 * RING]:
             copy.wait()
         out[...] = (held_ref[at].astype(jnp.float32) * scale).astype(out.dtype)
 
 
-def lefts_of(owner, goals, mine, other, factors, after):
+def lefts_of(owner, axis, mine, other, factors):
     blocks, depth, tokens = mine.shape
     shape = (depth // RING, blocks * tokens)
     return call(
-        functools.partial(lefts_kernel, owner),
+        functools.partial(lefts_kernel, owner, axis),
         "lefts",
-        [goals, mine, other, *factors],
-        after,
+        [mine, other, *factors],
+        [],
         [jax.ShapeDtypeStruct(shape, mine.dtype)] * RING,
         SMALL,
         10,
         [pltpu.VMEM((RING, *shape), mine.dtype), pltpu.SemaphoreType.DMA((2 * RING, RING))],
         None,
-        [SMEM, ANY, ANY] + [VMEM] * RING,
-    )
-
-
-def parts_kernel(place_ref, out_ref, act_ref, *refs):
+        [ANY, ANY] + [VMEM] * 3,
+    )
+
+
+def parts_kernel(out_ref, act_ref, *refs):
     targets, window_ref, sems = refs[:RING], refs[RING], refs[RING + 1]
     rows, tokens = targets[0].shape
     owned = rows // RING
+    core = lax.axis_index("core")
+    at_place = jnp.where(core == 0, lax.axis_index("x"), lax.axis_index("y"))
+    places = [lax.rem(at_place + s + RING, RING) for s in STEPS]
     for at in range(RING):
-        place = place_ref[1 + at]
-
-        @pl.when(place_ref[0] == 0)
+        place = places[at]
+
+        @pl.when(core == 0)
         def _():
             lanes = pl.ds(pl.multiple_of(place * rows, LANES), rows)
             pltpu.make_async_copy(out_ref.at[:, lanes], window_ref.at[at], sems.at[at]).start()
 
-        @pl.when(place_ref[0] != 0)
+        @pl.when(core != 0)
         def _():
             lanes = pl.ds(at * rows, rows)
             pltpu.make_async_copy(act_ref.at[:, lanes], window_ref.at[at], sems.at[at]).start()
@@ -228,34 +259,34 @@
     for at in range(RING):
         turned = window_ref[at].T
 
-        @pl.when(place_ref[0] == 0)
+        @pl.when(core == 0)
         def _():
             targets[at][...] = turned
 
-        @pl.when(place_ref[0] != 0)
+        @pl.when(core != 0)
         def _():
             for goal in range(RING):
                 for place in range(RING):
 
-                    @pl.when(place_ref[1 + goal] == place)
+                    @pl.when(places[goal] == place)
                     def _():
                         targets[goal][pl.ds(at * owned, owned), :] = turned[place * owned : (place + 1) * owned]
 
 
-def column_parts(out_grad, activations, places, after):
+def column_parts(out_grad, activations):
     tokens, depth = out_grad.shape
     rows = depth // RING
     return call(
         parts_kernel,
         "column_parts",
-        [places, out_grad, activations],
-        after,
+        [out_grad, activations],
+        [],
         [jax.ShapeDtypeStruct((rows, tokens), out_grad.dtype)] * RING,
         SMALL,
         16,
         [pltpu.VMEM((RING, tokens, rows), out_grad.dtype), pltpu.SemaphoreType.DMA((RING,))],
         None,
-        [SMEM, ANY, ANY],
+        [ANY, ANY],
     )
 
 
@@ -263,44 +294,54 @@
     tokens, model_width = activations.shape
     full_hidden = gate_pre.shape[1] * RING * CORES
     example_total = RING * RING
-    at_x, at_y, at_core = (lax.axis_index(a) for a in ("x", "y", "core"))
-
-    gate, up = gate_pre.T, up_pre.T
-    gate_val = gate.astype(jnp.float32)
-    hidden = (jax.nn.silu(gate_val) * up.astype(jnp.float32)).astype(jnp.bfloat16)
-    place = jnp.where(at_core == 0, at_x, at_y)
-    parts = column_parts(out_grad, activations, jnp.stack([at_core] + [(place + s) % RING for s in STEPS]), [hidden])
+
+    parts = column_parts(out_grad, activations)
     parts_here = [parts[0], *(shift(p, "spread", s) for p, s in zip(parts[1:], STEPS[1:], strict=True))]
-    gate_grad = gate_gradient(down_weight.T, out_grad, gate, up, [hidden, parts[0]], 288)
-    hidden_blocks, gate_blocks = around(hidden, "x"), around(gate_grad, "y")
+    hidden, gate_grad = hidden_and_gradient(down_weight.T, out_grad, gate_pre.T, up_pre.T, [parts[0]], 288)
+    near_hidden = [shift(hidden, "x", s) for s in STEPS[1:3]]
+    near_gate = [shift(gate_grad, "y", s) for s in STEPS[1:3]]
 
     small = jax.ShapeDtypeStruct((2 * RING, LANES), jnp.float32)
-    (squares,) = call(squares_kernel, "squares", [out_grad, activations, hidden, gate_grad], parts_here[1:], [small], SMALL, 10)
+    mine = stacked(parts_here, [gate_grad])
+    other = swap(mine, "core", 1)
+    (squares,) = call(
+        squares_kernel, "squares", [out_grad, activations, hidden, gate_grad], parts_here[1:], [small], HEAVY, 10
+    )
+    (squares,) = call(copy_kernel, "held", [squares], [other], [small], SMALL, 1)
     sums = around(squares + swap(squares, "core", 1), "z")
-    mine = stacked(parts_here, sums[1:])
-    radius = clip_bounds * math.sqrt(float(model_width * full_hidden * SEQ))
-    factor, unit = call(
-        factor_kernel,
+    (factor,) = call(
+        functools.partial(factor_kernel, math.sqrt(float(model_width * full_hidden * SEQ))),
         "factor",
-        [*sums, radius],
-        [*hidden_blocks[1:3], *gate_blocks[1:3], mine],
-        [small, jax.ShapeDtypeStruct((1, 1), jnp.float32)],
+        [*sums, clip_bounds],
+        [*near_hidden, *near_gate],
+        [small],
         SMALL,
         1,
         in_specs=[VMEM] * 4 + [SMEM],
     )
-    other = swap(mine, "core", 1)
-    far = [hidden_blocks[3], gate_blocks[3]]
-    goals_of = lambda at: jnp.stack([at_core] + [(at + s) % RING for s in (2, 1, -1, 0)])
-    along_x, along_y = around(factor, "x"), around(factor, "y")
-    gate_lefts = lefts_of(1, goals_of(at_x), mine, other, along_y, [*far, *along_x[1:]])
-    down_lefts = lefts_of(0, goals_of(at_y), mine, other, along_x, far)
-
-    def wide(blocks):
-        return jnp.concatenate([(unit * b.astype(jnp.float32)).astype(jnp.bfloat16) for b in blocks], axis=1)
-
-    down = ring_reduce(down_lefts, wide(hidden_blocks), "y")
-    gated = ring_reduce(gate_lefts, wide(gate_blocks), "x")
+    mine_factors, hidden, gate_grad = call(
+        pack_kernel,
+        "pack",
+        [*(shift(factor, "spread", s) for s in STEPS[1:]), hidden, gate_grad],
+        [],
+        [
+            jax.ShapeDtypeStruct((RING - 1, *small.shape), jnp.float32),
+            *(jax.ShapeDtypeStruct(v.shape, v.dtype) for v in (hidden, gate_grad)),
+        ],
+        SMALL,
+        1,
+        (),
+        {RING - 1: 1, RING: 2},
+        [VMEM] * (RING - 1) + [ANY] * 2,
+        [VMEM] + [ANY] * 2,
+    )
+    hidden_blocks = [hidden, *near_hidden, shift(hidden, "x", 2)]
+    gate_blocks = [gate_grad, *near_gate, shift(gate_grad, "y", 2)]
+    factors = [factor, mine_factors, swap(mine_factors, "core", 1)]
+    gate_lefts = lefts_of(1, "x", mine, other, factors)
+    down_lefts = lefts_of(0, "y", mine, other, factors)
+    down = ring_reduce(down_lefts, wide(hidden_blocks, []), "y")
+    gated = ring_reduce(gate_lefts, wide(gate_blocks, []), "x")
     return ((down / example_total).astype(jnp.bfloat16), (gated / example_total).astype(jnp.bfloat16))
 
 

time: 147 us -> 139 us (0.946)
  the two profiles are of different devices: /device:TPU:64 before, /device:TPU:0 now
where the time goes in v2:
time: 139 us; the launch traced here: 138 us
  waiting for transfers between devices  48.7 us (35%)
  starting transfers between devices  38.5 us (28%)
  Pallas kernels  32.1 us (23%)
  matrix products  11.2 us (8%)
  other arithmetic  3.57 us (3%)
  local copies, waits for them, and re-layouts  3.49 us (3%)
    ppermute x17, waiting for transfers between devices, shift(): lax.ppermute(value, axis, [(i, (i + step) % RING) for i in range(RING)])  41.6 us
    ppermute x17, starting transfers between devices, shift(): lax.ppermute(value, axis, [(i, (i + step) % RING) for i in range(RING)])  28 us
    pallas_call x9, Pallas kernels, call(): pl.pallas_call(body, in_specs=(in_specs or [VMEM] * count) + [ANY] * len(...  15.5 us
    pallas_call x1, Pallas kernels, hidden_and_gradient(): pl.pallas_call(gate_kernel, grid=(width // rows,), in_specs=[pl.BlockSpec...  12.6 us
    dot_general x8, matrix products, dot_last(): lax.dot_general(left, right, (((1,), (1,)), ((), ())), preferred_element_...  11.2 us
    ppermute x6, starting transfers between devices, shift(): return lax.ppermute(value, ('x', 'y', 'core'), pairs)  10.3 us
    pallas_call x1, Pallas kernels, stacked(): pl.pallas_call(stack_kernel, grid=(steps,), in_specs=[pl.BlockSpec((rows...  3.96 us
    ppermute x3, waiting for transfers between devices, swap(): lax.ppermute(value, axis, [(i, i ^ bit) for i in range(2 if axis == 'core...  3.79 us
  transfers between devices with their start and end apart: 26, of which 13 were waited for; matrix products, arithmetic and copies ran while one was open for 10% of the time, Pallas kernels for 21%

profile of v2, /device:TPU:0, one launch (start us, length us, event | category | flops | bytes accessed | tf_op | source)
XLA Modules:
  0.0 138.4 jit_solution(6376122985001262809)
XLA Ops:
  0.6 1.7 %copy-done = bf16[256,5120]{1,0:T(8,128)(2,1)S(1)} copy-done((bf16[256,5120]{1,0:T(8,128)(2,1)S(1)}, bf16[256,5120]{1,0:T(8,128)(2,1)}, u32[]{:S(2)}) %copy-start) | copy-done | bytes 2621464
  2.4 1.7 %copy-done.2 = bf16[256,5120]{1,0:T(8,128)(2,1)S(1)} copy-done((bf16[256,5120]{1,0:T(8,128)(2,1)S(1)}, bf16[256,5120]{1,0:T(8,128)(2,1)}, u32[]{:S(2)}) %copy-start.2) | copy-done | bytes 2621464
  4.1 2.6 %column_parts.1 = (bf16[1280,256]{1,0:T(8,128)(2,1)S(1)}, bf16[1280,256]{1,0:T(8,128)(2,1)}, bf16[1280,256]{1,0:T(8,128)(2,1)}, bf16[1280,256]{1,0:T(8,128)(2,1)}) custom-call(bf16[256,5120]{1,0:T(8,128)(2,1)S(1)} %copy-done, bf16[256,5120]{1,0:T(8,128)(2,1)S(1)} %copy-done.2), custom_call_target="tpu_custom_call" | custom-call | tf_op jit(solution)/shard_map/column_parts/pallas_call | solution.py:83
  6.8 1.6 %collective-permute-start = (bf16[1280,256]{1,0:T(8,128)(2,1)}, bf16[1280,256]{1,0:T(8,128)(2,1)}, u32[]{:S(2)}, u32[]{:S(2)}) collective-permute-start(bf16[1280,256]{1,0:T(8,128)(2,1)} %get-tuple-element.20), channel_id=1, source_target_pairs={{0,32},{1,9},{8,40},{9,17},{16,48},{17,25},{24,56},{25,1},{32,64},... | collective-permute-start | bytes 1966088 | tf_op jit(solution)/shard_map/ppermute | solution.py:40
  8.4 1.7 %collective-permute-start.1 = (bf16[1280,256]{1,0:T(8,128)(2,1)}, bf16[1280,256]{1,0:T(8,128)(2,1)}, u32[]{:S(2)}, u32[]{:S(2)}) collective-permute-start(bf16[1280,256]{1,0:T(8,128)(2,1)} %get-tuple-element.21), channel_id=1, source_target_pairs={{0,96},{1,25},{8,104},{9,1},{16,112},{17,9},{24,120},{25,17},{32,0... | collective-permute-start | bytes 1966088 | tf_op jit(solution)/shard_map/ppermute | solution.py:40
  10.1 1.9 %collective-permute-start.2 = (bf16[1280,256]{1,0:T(8,128)(2,1)}, bf16[1280,256]{1,0:T(8,128)(2,1)}, u32[]{:S(2)}, u32[]{:S(2)}) collective-permute-start(bf16[1280,256]{1,0:T(8,128)(2,1)} %get-tuple-element.22), channel_id=1, source_target_pairs={{0,64},{1,17},{8,72},{9,25},{16,80},{17,1},{24,88},{25,9},{32,96},... | collective-permute-start | bytes 1966088 | tf_op jit(solution)/shard_map/ppermute | solution.py:40
  12.0 12.6 %hidden_and_gradient.1 = (bf16[1728,256]{1,0:T(8,128)(2,1)}, bf16[1728,256]{1,0:T(8,128)(2,1)}) custom-call(bf16[1728,5120]{1,0:T(8,128)(2,1)} %bitcast.20, bf16[256,5120]{1,0:T(8,128)(2,1)} %refs_0_.3, bf16[1728,256]{1,0:T(8,128)(2,1)S(1)} %bitcast.19, bf16[1728,256]{1,0:T(8,128)(2,1)} %bitcast.21, bf16[1280,256]{1,0:T(8,128)(2,1)S(1)} %get-tuple-element.19.rest_0_.refs_0_), custom_call_target="tpu_custom_call" | custom-call | flops 999999995904 | bytes 1000000000 | tf_op jit(solution)/shard_map/hidden_and_gradient/pallas_call | solution.py:111
  24.6 1.6 %collective-permute-start.10 = (bf16[1728,256]{1,0:T(8,128)(2,1)}, bf16[1728,256]{1,0:T(8,128)(2,1)}, u32[]{:S(2)}, u32[]{:S(2)}) collective-permute-start(bf16[1728,256]{1,0:T(8,128)(2,1)} %get-tuple-element.23.refs_4_.refs_3_), channel_id=1, source_target_pairs={{0,8},{8,16},{16,24},{24,0},{1,9},{9,17},{17,25},{25,1},{2,10},{10... | collective-permute-start | bytes 2654216 | tf_op jit(solution)/shard_map/ppermute | solution.py:33
  26.1 1.7 %collective-permute-start.11 = (bf16[1728,256]{1,0:T(8,128)(2,1)}, bf16[1728,256]{1,0:T(8,128)(2,1)}, u32[]{:S(2)}, u32[]{:S(2)}) collective-permute-start(bf16[1728,256]{1,0:T(8,128)(2,1)} %get-tuple-element.23.refs_4_.refs_3_), channel_id=1, source_target_pairs={{0,24},{8,0},{16,8},{24,16},{1,25},{9,1},{17,9},{25,17},{2,26},{10... | collective-permute-start | bytes 2654216 | tf_op jit(solution)/shard_map/ppermute | solution.py:33
  28.4 2.6 %collective-permute-start.9 = (bf16[1728,256]{1,0:T(8,128)(2,1)}, bf16[1728,256]{1,0:T(8,128)(2,1)}, u32[]{:S(2)}, u32[]{:S(2)}) collective-permute-start(bf16[1728,256]{1,0:T(8,128)(2,1)} %get-tuple-element.24.refs_2_.refs_3_), channel_id=1, source_target_pairs={{0,96},{32,0},{64,32},{96,64},{1,97},{33,1},{65,33},{97,65},{2,98}... | collective-permute-start | bytes 2654216 | tf_op jit(solution)/shard_map/ppermute | solution.py:33
  31.1 4.0 %stack.1.refs_0_ = bf16[4,1280,256]{2,1,0:T(8,128)(2,1)} custom-call(bf16[1280,256]{1,0:T(8,128)(2,1)S(1)} %get-tuple-element.19.rest_0_.refs_0_, bf16[1280,256]{1,0:T(8,128)(2,1)} %collective-permute-done.refs_1_.refs_4_, bf16[1280,256]{1,0:T(8,128)(2,1)} %collective-permute-done.1.refs_2_.refs_5_, ...), custom_call_target="tpu_custom_call" | custom-call | tf_op jit(solution)/shard_map/stack/pallas_call | solution.py:173
  35.0 3.6 %squares.1.refs_0_ = f32[8,128]{1,0:T(8,128)S(1)} custom-call(bf16[256,5120]{1,0:T(8,128)(2,1)S(1)} %copy-done.1, bf16[256,5120]{1,0:T(8,128)(2,1)S(1)} %copy-done.3, bf16[1728,256]{1,0:T(8,128)(2,1)} %get-tuple-element.24.refs_2_.refs_3_, bf16[1728,256]{1,0:T(8,128)(2,1)} %get-tuple-element.23.refs_4_.refs_3_, ...), custom_call_target="tpu_custom_call" | custom-call | flops 999999995904 | bytes 1000000000 | tf_op jit(solution)/shard_map/squares/pallas_call | solution.py:83
  38.7 1.6 %collective-permute-done.3.refs_1_ = bf16[4,1280,256]{2,1,0:T(8,128)(2,1)} collective-permute-done((bf16[4,1280,256]{2,1,0:T(8,128)(2,1)}, bf16[4,1280,256]{2,1,0:T(8,128)(2,1)}, u32[]{:S(2)}, u32[]{:S(2)}) %collective-permute-start.3) | collective-permute-done | bytes 2621472 | tf_op jit(solution)/shard_map/ppermute | solution.py:44
  40.4 1.0 collective-permute-done.4
  41.5 1.9 %collective-permute-start.5 = (f32[8,128]{1,0:T(8,128)S(1)}, f32[8,128]{1,0:T(8,128)S(1)}, u32[]{:S(2)}, u32[]{:S(2)}) collective-permute-start(f32[8,128]{1,0:T(8,128)S(1)} %add.39.refs_0_), channel_id=1, source_target_pairs={{0,2},{2,4},{4,6},{6,0},{1,3},{3,5},{5,7},{7,1},{8,10},{10,12},{12... | collective-permute-start | bytes 12296 | tf_op jit(solution)/shard_map/ppermute | solution.py:33
  43.4 3.7 %collective-permute-done.10.refs_7_.refs_1_ = bf16[1728,256]{1,0:T(8,128)(2,1)} collective-permute-done((bf16[1728,256]{1,0:T(8,128)(2,1)}, bf16[1728,256]{1,0:T(8,128)(2,1)}, u32[]{:S(2)}, u32[]{:S(2)}) %collective-permute-start.10) | collective-permute-done | bytes 884768 | tf_op jit(solution)/shard_map/ppermute | solution.py:33
  47.0 4.0 %collective-permute-start.6 = (f32[8,128]{1,0:T(8,128)S(1)}, f32[8,128]{1,0:T(8,128)S(1)}, u32[]{:S(2)}, u32[]{:S(2)}) collective-permute-start(f32[8,128]{1,0:T(8,128)S(1)} %add.39.refs_0_), channel_id=1, source_target_pairs={{0,6},{2,0},{4,2},{6,4},{1,7},{3,1},{5,3},{7,5},{8,14},{10,8},{12,... | collective-permute-start | bytes 12296 | tf_op jit(solution)/shard_map/ppermute | solution.py:33
  51.1 1.3 collective-permute-done.6.refs_2_
  52.4 3.8 %collective-permute-done.7.refs_3_ = f32[8,128]{1,0:T(8,128)S(1)} collective-permute-done((f32[8,128]{1,0:T(8,128)S(1)}, f32[8,128]{1,0:T(8,128)S(1)}, u32[]{:S(2)}, u32[]{:S(2)}) %collective-permute-start.7) | collective-permute-done | bytes 4128 | tf_op jit(solution)/shard_map/ppermute | solution.py:33
  56.8 1.5 %collective-permute-start.12 = (f32[8,128]{1,0:T(8,128)S(1)}, f32[8,128]{1,0:T(8,128)S(1)}, u32[]{:S(2)}, u32[]{:S(2)}) collective-permute-start(f32[8,128]{1,0:T(8,128)S(1)} %factor.1.refs_2_), channel_id=1, source_target_pairs={{0,32},{1,9},{8,40},{9,17},{16,48},{17,25},{24,56},{25,1},{32,64},... | collective-permute-start | bytes 12296 | tf_op jit(solution)/shard_map/ppermute | solution.py:40
  58.3 1.8 %collective-permute-start.13 = (f32[8,128]{1,0:T(8,128)S(1)}, f32[8,128]{1,0:T(8,128)S(1)}, u32[]{:S(2)}, u32[]{:S(2)}) collective-permute-start(f32[8,128]{1,0:T(8,128)S(1)} %factor.1.refs_2_), channel_id=1, source_target_pairs={{0,96},{1,25},{8,104},{9,1},{16,112},{17,9},{24,120},{25,17},{32,0... | collective-permute-start | bytes 12296 | tf_op jit(solution)/shard_map/ppermute | solution.py:40
  60.1 1.8 %collective-permute-start.14 = (f32[8,128]{1,0:T(8,128)S(1)}, f32[8,128]{1,0:T(8,128)S(1)}, u32[]{:S(2)}, u32[]{:S(2)}) collective-permute-start(f32[8,128]{1,0:T(8,128)S(1)} %factor.1.refs_2_), channel_id=1, source_target_pairs={{0,64},{1,17},{8,72},{9,25},{16,80},{17,1},{24,88},{25,9},{32,96},... | collective-permute-start | bytes 12296 | tf_op jit(solution)/shard_map/ppermute | solution.py:40
  61.9 3.3 %collective-permute-done.14.refs_2_ = f32[8,128]{1,0:T(8,128)S(1)} collective-permute-done((f32[8,128]{1,0:T(8,128)S(1)}, f32[8,128]{1,0:T(8,128)S(1)}, u32[]{:S(2)}, u32[]{:S(2)}) %collective-permute-start.14) | collective-permute-done | bytes 4128 | tf_op jit(solution)/shard_map/ppermute | solution.py:40
  65.7 1.8 %collective-permute-start.16 = (bf16[1728,256]{1,0:T(8,128)(2,1)}, bf16[1728,256]{1,0:T(8,128)(2,1)S(1)}, u32[]{:S(2)}, u32[]{:S(2)}) collective-permute-start(bf16[1728,256]{1,0:T(8,128)(2,1)} %get-tuple-element.27.refs_0_), channel_id=1, source_target_pairs={{0,64},{32,96},{64,0},{96,32},{1,65},{33,97},{65,1},{97,33},{2,66}... | collective-permute-start | bytes 2654216 | tf_op jit(solution)/shard_map/ppermute | solution.py:33
  67.4 1.2 collective-permute-done.15.refs_4_
  68.6 2.1 %lefts.3 = (bf16[320,1024]{1,0:T(8,128)(2,1)S(1)}, bf16[320,1024]{1,0:T(8,128)(2,1)S(1)}, bf16[320,1024]{1,0:T(8,128)(2,1)S(1)}, bf16[320,1024]{1,0:T(8,128)(2,1)S(1)}) custom-call(bf16[4,1280,256]{2,1,0:T(8,128)(2,1)} %stack.1.refs_0_, bf16[4,1280,256]{2,1,0:T(8,128)(2,1)} %collective-permute-done.3.refs_1_, f32[8,128]{1,0:T(8,128)S(1)} %factor.1.refs_2_, ...), custom_call_target="tpu_custom_call" | custom-call | tf_op jit(solution)/shard_map/lefts/pallas_call | solution.py:83
  70.8 2.2 %lefts.2 = (bf16[320,1024]{1,0:T(8,128)(2,1)S(1)}, bf16[320,1024]{1,0:T(8,128)(2,1)S(1)}, bf16[320,1024]{1,0:T(8,128)(2,1)S(1)}, bf16[320,1024]{1,0:T(8,128)(2,1)S(1)}) custom-call(bf16[4,1280,256]{2,1,0:T(8,128)(2,1)} %stack.1.refs_0_, bf16[4,1280,256]{2,1,0:T(8,128)(2,1)} %collective-permute-done.3.refs_1_, f32[8,128]{1,0:T(8,128)S(1)} %factor.1.refs_2_, ...), custom_call_target="tpu_custom_call" | custom-call | tf_op jit(solution)/shard_map/lefts/pallas_call | solution.py:83
  73.0 10.8 %collective-permute-done.21.refs_3_ = bf16[1728,256]{1,0:T(8,128)(2,1)S(1)} collective-permute-done((bf16[1728,256]{1,0:T(8,128)(2,1)}, bf16[1728,256]{1,0:T(8,128)(2,1)S(1)}, u32[]{:S(2)}, u32[]{:S(2)}) %collective-permute-start.21) | collective-permute-done | bytes 884768 | tf_op jit(solution)/shard_map/ppermute | solution.py:33
  83.8 2.2 %wide.3 = bf16[1728,1024]{1,0:T(8,128)(2,1)S(1)} custom-call(bf16[1728,256]{1,0:T(8,128)(2,1)} %get-tuple-element.32.refs_0_, bf16[1728,256]{1,0:T(8,128)(2,1)} %collective-permute-done.10.refs_7_.refs_1_, bf16[1728,256]{1,0:T(8,128)(2,1)} %collective-permute-done.11.refs_8_.refs_2_, bf16[1728,256]{1,0:T(8,128)(2,1)S(1)} %collective-permute-done.21.refs_3_), custom_call_target="tpu_custom_call" | custom-call | tf_op jit(solution)/shard_map/wide/pallas_call | solution.py:83
  86.0 1.4 %convolution_convert_fusion.2 = bf16[320,1728]{1,0:T(8,128)(2,1)S(1)} fusion(bf16[320,1024]{1,0:T(8,128)(2,1)S(1)} %get-tuple-element.33, bf16[1728,1024]{1,0:T(8,128)(2,1)S(1)} %wide.3), kind=kOutput, calls=%fused_computation.2 | convolution fusion | flops 1133015040 | bytes 5300224 | tf_op jit(solution)/shard_map/dot_general | solution.py:48
  87.4 4.5 %collective-permute-start.22 = (bf16[320,1728]{1,0:T(8,128)(2,1)S(1)}, bf16[320,1728]{1,0:T(8,128)(2,1)S(1)}, u32[]{:S(2)}, u32[]{:S(2)}) collective-permute-start(bf16[320,1728]{1,0:T(8,128)(2,1)S(1)} %convolution_convert_fusion.2), channel_id=1, source_target_pairs={{0,96},{32,0},{64,32},{96,64},{1,97},{33,1},{65,33},{97,65},{2,98}... | collective-permute-start | bytes 3317768 | tf_op jit(solution)/shard_map/ppermute | solution.py:33
  91.8 1.4 %convolution_convert_fusion = bf16[320,1728]{1,0:T(8,128)(2,1)S(1)} fusion(bf16[320,1024]{1,0:T(8,128)(2,1)S(1)} %get-tuple-element.35, bf16[1728,1024]{1,0:T(8,128)(2,1)S(1)} %wide.3), kind=kOutput, calls=%fused_computation | convolution fusion | flops 1133015040 | bytes 5300224 | tf_op jit(solution)/shard_map/dot_general | solution.py:48
  93.3 2.2 %wide.2 = bf16[1728,1024]{1,0:T(8,128)(2,1)S(1)} custom-call(bf16[1728,256]{1,0:T(8,128)(2,1)} %get-tuple-element.27.refs_0_, bf16[1728,256]{1,0:T(8,128)(2,1)} %collective-permute-done.8.refs_5_.refs_1_, bf16[1728,256]{1,0:T(8,128)(2,1)} %collective-permute-done.9.refs_6_.refs_2_, bf16[1728,256]{1,0:T(8,128)(2,1)S(1)} %collective-permute-done.16.refs_3_), custom_call_target="tpu_custom_call" | custom-call | tf_op jit(solution)/shard_map/wide/pallas_call | solution.py:83
  95.5 1.4 %convolution_convert_fusion.6 = bf16[320,1728]{1,0:T(8,128)(2,1)S(1)} fusion(bf16[320,1024]{1,0:T(8,128)(2,1)S(1)} %get-tuple-element.28, bf16[1728,1024]{1,0:T(8,128)(2,1)S(1)} %wide.2), kind=kOutput, calls=%fused_computation.6 | convolution fusion | flops 1133015040 | bytes 5300224 | tf_op jit(solution)/shard_map/dot_general | solution.py:48
  97.3 1.4 %convolution_convert_fusion.4 = bf16[320,1728]{1,0:T(8,128)(2,1)S(1)} fusion(bf16[320,1024]{1,0:T(8,128)(2,1)S(1)} %get-tuple-element.30, bf16[1728,1024]{1,0:T(8,128)(2,1)S(1)} %wide.2), kind=kOutput, calls=%fused_computation.4 | convolution fusion | flops 1133015040 | bytes 5300224 | tf_op jit(solution)/shard_map/dot_general | solution.py:48
  98.7 1.8 %collective-permute-start.18 = (bf16[320,1728]{1,0:T(8,128)(2,1)S(1)}, bf16[320,1728]{1,0:T(8,128)(2,1)S(1)}, u32[]{:S(2)}, u32[]{:S(2)}) collective-permute-start(bf16[320,1728]{1,0:T(8,128)(2,1)S(1)} %convolution_convert_fusion.4), channel_id=1, source_target_pairs={{0,8},{8,16},{16,24},{24,0},{1,9},{9,17},{17,25},{25,1},{2,10},{10... | collective-permute-start | bytes 3317768 | tf_op jit(solution)/shard_map/ppermute | solution.py:33
  100.5 1.4 %convolution_convert_fusion.3 = bf16[320,1728]{1,0:T(8,128)(2,1)S(1)} fusion(bf16[320,1024]{1,0:T(8,128)(2,1)S(1)} %get-tuple-element.31, bf16[1728,1024]{1,0:T(8,128)(2,1)S(1)} %wide.3), kind=kOutput, calls=%fused_computation.3 | convolution fusion | flops 1133015040 | bytes 5300224 | tf_op jit(solution)/shard_map/dot_general | solution.py:48
  101.9 1.4 %convolution_convert_fusion.1 = bf16[320,1728]{1,0:T(8,128)(2,1)S(1)} fusion(bf16[320,1024]{1,0:T(8,128)(2,1)S(1)} %get-tuple-element.34, bf16[1728,1024]{1,0:T(8,128)(2,1)S(1)} %wide.3), kind=kOutput, calls=%fused_computation.1 | convolution fusion | flops 1133015040 | bytes 5300224 | tf_op jit(solution)/shard_map/dot_general | solution.py:48
  103.3 1.4 %convolution_convert_fusion.7 = bf16[320,1728]{1,0:T(8,128)(2,1)S(1)} fusion(bf16[320,1024]{1,0:T(8,128)(2,1)S(1)} %get-tuple-element.26, bf16[1728,1024]{1,0:T(8,128)(2,1)S(1)} %wide.2), kind=kOutput, calls=%fused_computation.7 | convolution fusion | flops 1133015040 | bytes 5300224 | tf_op jit(solution)/shard_map/dot_general | solution.py:48
  104.7 9.1 %collective-permute-done.22 = bf16[320,1728]{1,0:T(8,128)(2,1)S(1)} collective-permute-done((bf16[320,1728]{1,0:T(8,128)(2,1)S(1)}, bf16[320,1728]{1,0:T(8,128)(2,1)S(1)}, u32[]{:S(2)}, u32[]{:S(2)}) %collective-permute-start.22) | collective-permute-done | bytes 1105952 | tf_op jit(solution)/shard_map/ppermute | solution.py:33
  113.8 4.9 %collective-permute-done.23 = bf16[320,1728]{1,0:T(8,128)(2,1)S(1)} collective-permute-done((bf16[320,1728]{1,0:T(8,128)(2,1)S(1)}, bf16[320,1728]{1,0:T(8,128)(2,1)S(1)}, u32[]{:S(2)}, u32[]{:S(2)}) %collective-permute-start.23) | collective-permute-done | bytes 1105952 | tf_op jit(solution)/shard_map/ppermute | solution.py:33
  119.1 3.2 %collective-permute-start.25 = (bf16[160,1728]{1,0:T(8,128)(2,1)S(1)}, bf16[160,1728]{1,0:T(8,128)(2,1)S(1)}, u32[]{:S(2)}, u32[]{:S(2)}) collective-permute-start(bf16[160,1728]{1,0:T(8,128)(2,1)S(1)} %get-tuple-element.39), channel_id=1, source_target_pairs={{0,96},{32,0},{64,32},{96,64},{1,97},{33,1},{65,33},{97,65},{2,98}... | collective-permute-start | bytes 1658888 | tf_op jit(solution)/shard_map/ppermute | solution.py:33
  122.3 1.4 %convolution_convert_fusion.5 = bf16[320,1728]{1,0:T(8,128)(2,1)S(1)} fusion(bf16[320,1024]{1,0:T(8,128)(2,1)S(1)} %get-tuple-element.29, bf16[1728,1024]{1,0:T(8,128)(2,1)S(1)} %wide.2), kind=kOutput, calls=%fused_computation.5 | convolution fusion | flops 1133015040 | bytes 5300224 | tf_op jit(solution)/shard_map/dot_general | solution.py:48
  125.5 2.4 %collective-permute-start.20 = (bf16[160,1728]{1,0:T(8,128)(2,1)S(1)}, bf16[160,1728]{1,0:T(8,128)(2,1)S(1)}, u32[]{:S(2)}, u32[]{:S(2)}) collective-permute-start(bf16[160,1728]{1,0:T(8,128)(2,1)S(1)} %get-tuple-element.43), channel_id=1, source_target_pairs={{0,24},{8,0},{16,8},{24,16},{1,25},{9,1},{17,9},{25,17},{2,26},{10... | collective-permute-start | bytes 1658888 | tf_op jit(solution)/shard_map/ppermute | solution.py:33
  127.8 3.4 %collective-permute-done.24 = bf16[160,1728]{1,0:T(8,128)(2,1)S(1)} collective-permute-done((bf16[160,1728]{1,0:T(8,128)(2,1)S(1)}, bf16[160,1728]{1,0:T(8,128)(2,1)S(1)}, u32[]{:S(2)}, u32[]{:S(2)}) %collective-permute-start.24) | collective-permute-done | bytes 552992 | tf_op jit(solution)/shard_map/ppermute | solution.py:33
  131.6 1.1 fusion.1
  132.7 4.1 %collective-permute-done.19 = bf16[160,1728]{1,0:T(8,128)(2,1)S(1)} collective-permute-done((bf16[160,1728]{1,0:T(8,128)(2,1)S(1)}, bf16[160,1728]{1,0:T(8,128)(2,1)S(1)}, u32[]{:S(2)}, u32[]{:S(2)}) %collective-permute-start.19) | collective-permute-done | bytes 552992 | tf_op jit(solution)/shard_map/ppermute | solution.py:33
  137.2 1.1 fusion
  (42 shorter events, 5.1 us)
Async XLA Ops:
  0.6 1.7 %copy-start = (bf16[256,5120]{1,0:T(8,128)(2,1)S(1)}, bf16[256,5120]{1,0:T(8,128)(2,1)}, u32[]{:S(2)}) copy-start(bf16[256,5120]{1,0:T(8,128)(2,1)} %refs_0_.3) | copy-start | bytes 7864324
  2.4 1.7 %copy-start.2 = (bf16[256,5120]{1,0:T(8,128)(2,1)S(1)}, bf16[256,5120]{1,0:T(8,128)(2,1)}, u32[]{:S(2)}) copy-start(bf16[256,5120]{1,0:T(8,128)(2,1)} %refs_1_.3) | copy-start | bytes 7864324
  4.1 7.8 %copy-start.5 = (bf16[256,1728]{0,1:T(8,128)(2,1)S(1)}, bf16[256,1728]{0,1:T(8,128)(2,1)}, u32[]{:S(2)}) copy-start(bf16[256,1728]{0,1:T(8,128)(2,1)} %param.8) | copy-start | bytes 2654212
  6.8 21.1 %collective-permute-start = (bf16[1280,256]{1,0:T(8,128)(2,1)}, bf16[1280,256]{1,0:T(8,128)(2,1)}, u32[]{:S(2)}, u32[]{:S(2)}) collective-permute-start(bf16[1280,256]{1,0:T(8,128)(2,1)} %get-tuple-element.20), channel_id=1, source_target_pairs={{0,32},{1,9},{8,40},{9,17},{16,48},{17,25},{24,56},{25,1},{32,64},... | collective-permute-start | bytes 1966088 | tf_op jit(solution)/shard_map/ppermute | solution.py:40
  8.4 20.0 %collective-permute-start.1 = (bf16[1280,256]{1,0:T(8,128)(2,1)}, bf16[1280,256]{1,0:T(8,128)(2,1)}, u32[]{:S(2)}, u32[]{:S(2)}) collective-permute-start(bf16[1280,256]{1,0:T(8,128)(2,1)} %get-tuple-element.21), channel_id=1, source_target_pairs={{0,96},{1,25},{8,104},{9,1},{16,112},{17,9},{24,120},{25,17},{32,0... | collective-permute-start | bytes 1966088 | tf_op jit(solution)/shard_map/ppermute | solution.py:40
  10.1 21.0 %collective-permute-start.2 = (bf16[1280,256]{1,0:T(8,128)(2,1)}, bf16[1280,256]{1,0:T(8,128)(2,1)}, u32[]{:S(2)}, u32[]{:S(2)}) collective-permute-start(bf16[1280,256]{1,0:T(8,128)(2,1)} %get-tuple-element.22), channel_id=1, source_target_pairs={{0,64},{1,17},{8,72},{9,25},{16,80},{17,1},{24,88},{25,9},{32,96},... | collective-permute-start | bytes 1966088 | tf_op jit(solution)/shard_map/ppermute | solution.py:40
  24.6 22.5 %collective-permute-start.10 = (bf16[1728,256]{1,0:T(8,128)(2,1)}, bf16[1728,256]{1,0:T(8,128)(2,1)}, u32[]{:S(2)}, u32[]{:S(2)}) collective-permute-start(bf16[1728,256]{1,0:T(8,128)(2,1)} %get-tuple-element.23.refs_4_.refs_3_), channel_id=1, source_target_pairs={{0,8},{8,16},{16,24},{24,0},{1,9},{9,17},{17,25},{25,1},{2,10},{10... | collective-permute-start | bytes 2654216 | tf_op jit(solution)/shard_map/ppermute | solution.py:33
  26.1 24.9 %collective-permute-start.11 = (bf16[1728,256]{1,0:T(8,128)(2,1)}, bf16[1728,256]{1,0:T(8,128)(2,1)}, u32[]{:S(2)}, u32[]{:S(2)}) collective-permute-start(bf16[1728,256]{1,0:T(8,128)(2,1)} %get-tuple-element.23.refs_4_.refs_3_), channel_id=1, source_target_pairs={{0,24},{8,0},{16,8},{24,16},{1,25},{9,1},{17,9},{25,17},{2,26},{10... | collective-permute-start | bytes 2654216 | tf_op jit(solution)/shard_map/ppermute | solution.py:33
  27.8 7.2 %copy-start.1 = (bf16[256,5120]{1,0:T(8,128)(2,1)S(1)}, bf16[256,5120]{1,0:T(8,128)(2,1)}, u32[]{:S(2)}) copy-start(bf16[256,5120]{1,0:T(8,128)(2,1)} %refs_0_.3) | copy-start | bytes 7864324
  27.8 7.2 %copy-start.3 = (bf16[256,5120]{1,0:T(8,128)(2,1)S(1)}, bf16[256,5120]{1,0:T(8,128)(2,1)}, u32[]{:S(2)}) copy-start(bf16[256,5120]{1,0:T(8,128)(2,1)} %refs_1_.3) | copy-start | bytes 7864324
  27.8 23.3 %collective-permute-start.8 = (bf16[1728,256]{1,0:T(8,128)(2,1)}, bf16[1728,256]{1,0:T(8,128)(2,1)}, u32[]{:S(2)}, u32[]{:S(2)}) collective-permute-start(bf16[1728,256]{1,0:T(8,128)(2,1)} %get-tuple-element.24.refs_2_.refs_3_), channel_id=1, source_target_pairs={{0,32},{32,64},{64,96},{96,0},{1,33},{33,65},{65,97},{97,1},{2,34}... | collective-permute-start | bytes 2654216 | tf_op jit(solution)/shard_map/ppermute | solution.py:33
  28.4 22.7 %collective-permute-start.9 = (bf16[1728,256]{1,0:T(8,128)(2,1)}, bf16[1728,256]{1,0:T(8,128)(2,1)}, u32[]{:S(2)}, u32[]{:S(2)}) collective-permute-start(bf16[1728,256]{1,0:T(8,128)(2,1)} %get-tuple-element.24.refs_2_.refs_3_), channel_id=1, source_target_pairs={{0,96},{32,0},{64,32},{96,64},{1,97},{33,1},{65,33},{97,65},{2,98}... | collective-permute-start | bytes 2654216 | tf_op jit(solution)/shard_map/ppermute | solution.py:33
  35.0 5.3 %collective-permute-start.3 = (bf16[4,1280,256]{2,1,0:T(8,128)(2,1)}, bf16[4,1280,256]{2,1,0:T(8,128)(2,1)}, u32[]{:S(2)}, u32[]{:S(2)}) collective-permute-start(bf16[4,1280,256]{2,1,0:T(8,128)(2,1)} %stack.1.refs_0_), channel_id=1, source_target_pairs={{0,1},{1,0},{2,3},{3,2},{4,5},{5,4},{6,7},{7,6},{8,9},{9,8},{10,11... | collective-permute-start | bytes 7864328 | tf_op jit(solution)/shard_map/ppermute | solution.py:44
  38.7 17.5 %copy-start.4 = (f32[2]{0:T(128)S(1)}, f32[2]{0:T(128)}, u32[]{:S(2)}) copy-start(f32[2]{0:T(128)} %refs_4_.1) | copy-start | bytes 28
  40.3 1.2 collective-permute-start.4
  41.5 9.7 %collective-permute-start.5 = (f32[8,128]{1,0:T(8,128)S(1)}, f32[8,128]{1,0:T(8,128)S(1)}, u32[]{:S(2)}, u32[]{:S(2)}) collective-permute-start(f32[8,128]{1,0:T(8,128)S(1)} %add.39.refs_0_), channel_id=1, source_target_pairs={{0,2},{2,4},{4,6},{6,0},{1,3},{3,5},{5,7},{7,1},{8,10},{10,12},{12... | collective-permute-start | bytes 12296 | tf_op jit(solution)/shard_map/ppermute | solution.py:33
  47.0 5.4 %collective-permute-start.6 = (f32[8,128]{1,0:T(8,128)S(1)}, f32[8,128]{1,0:T(8,128)S(1)}, u32[]{:S(2)}, u32[]{:S(2)}) collective-permute-start(f32[8,128]{1,0:T(8,128)S(1)} %add.39.refs_0_), channel_id=1, source_target_pairs={{0,6},{2,0},{4,2},{6,4},{1,7},{3,1},{5,3},{7,5},{8,14},{10,8},{12,... | collective-permute-start | bytes 12296 | tf_op jit(solution)/shard_map/ppermute | solution.py:33
  51.1 5.1 %collective-permute-start.7 = (f32[8,128]{1,0:T(8,128)S(1)}, f32[8,128]{1,0:T(8,128)S(1)}, u32[]{:S(2)}, u32[]{:S(2)}) collective-permute-start(f32[8,128]{1,0:T(8,128)S(1)} %add.39.refs_0_), channel_id=1, source_target_pairs={{0,4},{2,6},{4,0},{6,2},{1,5},{3,7},{5,1},{7,3},{8,12},{10,14},{12... | collective-permute-start | bytes 12296 | tf_op jit(solution)/shard_map/ppermute | solution.py:33
  56.8 5.1 %collective-permute-start.12 = (f32[8,128]{1,0:T(8,128)S(1)}, f32[8,128]{1,0:T(8,128)S(1)}, u32[]{:S(2)}, u32[]{:S(2)}) collective-permute-start(f32[8,128]{1,0:T(8,128)S(1)} %factor.1.refs_2_), channel_id=1, source_target_pairs={{0,32},{1,9},{8,40},{9,17},{16,48},{17,25},{24,56},{25,1},{32,64},... | collective-permute-start | bytes 12296 | tf_op jit(solution)/shard_map/ppermute | solution.py:40
  58.3 3.6 %collective-permute-start.13 = (f32[8,128]{1,0:T(8,128)S(1)}, f32[8,128]{1,0:T(8,128)S(1)}, u32[]{:S(2)}, u32[]{:S(2)}) collective-permute-start(f32[8,128]{1,0:T(8,128)S(1)} %factor.1.refs_2_), channel_id=1, source_target_pairs={{0,96},{1,25},{8,104},{9,1},{16,112},{17,9},{24,120},{25,17},{32,0... | collective-permute-start | bytes 12296 | tf_op jit(solution)/shard_map/ppermute | solution.py:40
  60.1 5.1 %collective-permute-start.14 = (f32[8,128]{1,0:T(8,128)S(1)}, f32[8,128]{1,0:T(8,128)S(1)}, u32[]{:S(2)}, u32[]{:S(2)}) collective-permute-start(f32[8,128]{1,0:T(8,128)S(1)} %factor.1.refs_2_), channel_id=1, source_target_pairs={{0,64},{1,17},{8,72},{9,25},{16,80},{17,1},{24,88},{25,9},{32,96},... | collective-permute-start | bytes 12296 | tf_op jit(solution)/shard_map/ppermute | solution.py:40
  65.2 18.6 %collective-permute-start.21 = (bf16[1728,256]{1,0:T(8,128)(2,1)}, bf16[1728,256]{1,0:T(8,128)(2,1)S(1)}, u32[]{:S(2)}, u32[]{:S(2)}) collective-permute-start(bf16[1728,256]{1,0:T(8,128)(2,1)} %get-tuple-element.32.refs_0_), channel_id=1, source_target_pairs={{0,16},{8,24},{16,0},{24,8},{1,17},{9,25},{17,1},{25,9},{2,18},{10... | collective-permute-start | bytes 2654216 | tf_op jit(solution)/shard_map/ppermute | solution.py:33
  65.7 27.7 %collective-permute-start.16 = (bf16[1728,256]{1,0:T(8,128)(2,1)}, bf16[1728,256]{1,0:T(8,128)(2,1)S(1)}, u32[]{:S(2)}, u32[]{:S(2)}) collective-permute-start(bf16[1728,256]{1,0:T(8,128)(2,1)} %get-tuple-element.27.refs_0_), channel_id=1, source_target_pairs={{0,64},{32,96},{64,0},{96,32},{1,65},{33,97},{65,1},{97,33},{2,66}... | collective-permute-start | bytes 2654216 | tf_op jit(solution)/shard_map/ppermute | solution.py:33
  67.4 1.2 collective-permute-start.15
  87.4 26.4 %collective-permute-start.22 = (bf16[320,1728]{1,0:T(8,128)(2,1)S(1)}, bf16[320,1728]{1,0:T(8,128)(2,1)S(1)}, u32[]{:S(2)}, u32[]{:S(2)}) collective-permute-start(bf16[320,1728]{1,0:T(8,128)(2,1)S(1)} %convolution_convert_fusion.2), channel_id=1, source_target_pairs={{0,96},{32,0},{64,32},{96,64},{1,97},{33,1},{65,33},{97,65},{2,98}... | collective-permute-start | bytes 3317768 | tf_op jit(solution)/shard_map/ppermute | solution.py:33
  93.2 25.5 %collective-permute-start.23 = (bf16[320,1728]{1,0:T(8,128)(2,1)S(1)}, bf16[320,1728]{1,0:T(8,128)(2,1)S(1)}, u32[]{:S(2)}, u32[]{:S(2)}) collective-permute-start(bf16[320,1728]{1,0:T(8,128)(2,1)S(1)} %convolution_convert_fusion), channel_id=1, source_target_pairs={{0,32},{32,64},{64,96},{96,0},{1,33},{33,65},{65,97},{97,1},{2,34}... | collective-permute-start | bytes 3317768 | tf_op jit(solution)/shard_map/ppermute | solution.py:33
  96.9 26.8 %collective-permute-start.17 = (bf16[320,1728]{1,0:T(8,128)(2,1)S(1)}, bf16[320,1728]{1,0:T(8,128)(2,1)S(1)}, u32[]{:S(2)}, u32[]{:S(2)}) collective-permute-start(bf16[320,1728]{1,0:T(8,128)(2,1)S(1)} %convolution_convert_fusion.6), channel_id=1, source_target_pairs={{0,24},{8,0},{16,8},{24,16},{1,25},{9,1},{17,9},{25,17},{2,26},{10... | collective-permute-start | bytes 3317768 | tf_op jit(solution)/shard_map/ppermute | solution.py:33
  98.7 25.6 %collective-permute-start.18 = (bf16[320,1728]{1,0:T(8,128)(2,1)S(1)}, bf16[320,1728]{1,0:T(8,128)(2,1)S(1)}, u32[]{:S(2)}, u32[]{:S(2)}) collective-permute-start(bf16[320,1728]{1,0:T(8,128)(2,1)S(1)} %convolution_convert_fusion.4), channel_id=1, source_target_pairs={{0,8},{8,16},{16,24},{24,0},{1,9},{9,17},{17,25},{25,1},{2,10},{10... | collective-permute-start | bytes 3317768 | tf_op jit(solution)/shard_map/ppermute | solution.py:33
  119.0 12.3 %collective-permute-start.24 = (bf16[160,1728]{1,0:T(8,128)(2,1)S(1)}, bf16[160,1728]{1,0:T(8,128)(2,1)S(1)}, u32[]{:S(2)}, u32[]{:S(2)}) collective-permute-start(bf16[160,1728]{1,0:T(8,128)(2,1)S(1)} %get-tuple-element.38), channel_id=1, source_target_pairs={{0,32},{32,64},{64,96},{96,0},{1,33},{33,65},{65,97},{97,1},{2,34}... | collective-permute-start | bytes 1658888 | tf_op jit(solution)/shard_map/ppermute | solution.py:33
  119.1 12.2 %collective-permute-start.25 = (bf16[160,1728]{1,0:T(8,128)(2,1)S(1)}, bf16[160,1728]{1,0:T(8,128)(2,1)S(1)}, u32[]{:S(2)}, u32[]{:S(2)}) collective-permute-start(bf16[160,1728]{1,0:T(8,128)(2,1)S(1)} %get-tuple-element.39), channel_id=1, source_target_pairs={{0,96},{32,0},{64,32},{96,64},{1,97},{33,1},{65,33},{97,65},{2,98}... | collective-permute-start | bytes 1658888 | tf_op jit(solution)/shard_map/ppermute | solution.py:33
  124.5 12.3 %collective-permute-start.19 = (bf16[160,1728]{1,0:T(8,128)(2,1)S(1)}, bf16[160,1728]{1,0:T(8,128)(2,1)S(1)}, u32[]{:S(2)}, u32[]{:S(2)}) collective-permute-start(bf16[160,1728]{1,0:T(8,128)(2,1)S(1)} %get-tuple-element.42), channel_id=1, source_target_pairs={{0,8},{8,16},{16,24},{24,0},{1,9},{9,17},{17,25},{25,1},{2,10},{10... | collective-permute-start | bytes 1658888 | tf_op jit(solution)/shard_map/ppermute | solution.py:33
  125.5 11.4 %collective-permute-start.20 = (bf16[160,1728]{1,0:T(8,128)(2,1)S(1)}, bf16[160,1728]{1,0:T(8,128)(2,1)S(1)}, u32[]{:S(2)}, u32[]{:S(2)}) collective-permute-start(bf16[160,1728]{1,0:T(8,128)(2,1)S(1)} %get-tuple-element.43), channel_id=1, source_target_pairs={{0,24},{8,0},{16,8},{24,16},{1,25},{9,1},{17,9},{25,17},{2,26},{10... | collective-permute-start | bytes 1658888 | tf_op jit(solution)/shard_map/ppermute | solution.py:33

commit v3 on v2

--- a/solution.py
+++ b/solution.py
@@ -143,10 +143,10 @@
 
 
 def factor_kernel(unit, *refs):
-    total = refs[0][...] + refs[1][...] + refs[2][...] + refs[3][...]
+    total = refs[0][...] + refs[1][...]
     row = lax.broadcasted_iota(jnp.int32, total.shape, 0)
-    radius = jnp.where(row < RING, refs[4][0], refs[4][1]) * unit
-    refs[5][...] = radius / jnp.maximum(jnp.sqrt(total), radius)
+    radius = jnp.where(row < RING, refs[2][0], refs[2][1]) * unit
+    refs[3][...] = radius / jnp.maximum(jnp.sqrt(total), radius)
 
 
 def wide_kernel(*refs):
@@ -297,7 +297,7 @@
 
     parts = column_parts(out_grad, activations)
     parts_here = [parts[0], *(shift(p, "spread", s) for p, s in zip(parts[1:], STEPS[1:], strict=True))]
-    hidden, gate_grad = hidden_and_gradient(down_weight.T, out_grad, gate_pre.T, up_pre.T, [parts[0]], 288)
+    hidden, gate_grad = hidden_and_gradient(down_weight.T, out_grad, gate_pre.T, up_pre.T, [parts[0]], 864)
     near_hidden = [shift(hidden, "x", s) for s in STEPS[1:3]]
     near_gate = [shift(gate_grad, "y", s) for s in STEPS[1:3]]
 
@@ -308,16 +308,17 @@
         squares_kernel, "squares", [out_grad, activations, hidden, gate_grad], parts_here[1:], [small], HEAVY, 10
     )
     (squares,) = call(copy_kernel, "held", [squares], [other], [small], SMALL, 1)
-    sums = around(squares + swap(squares, "core", 1), "z")
+    total = squares + swap(squares, "core", 1)
+    total = total + swap(total, "z", 1)
     (factor,) = call(
         functools.partial(factor_kernel, math.sqrt(float(model_width * full_hidden * SEQ))),
         "factor",
-        [*sums, clip_bounds],
+        [total, swap(total, "z", 2), clip_bounds],
         [*near_hidden, *near_gate],
         [small],
         SMALL,
         1,
-        in_specs=[VMEM] * 4 + [SMEM],
+        in_specs=[VMEM] * 2 + [SMEM],
     )
     mine_factors, hidden, gate_grad = call(
         pack_kernel,

time: 139 us -> 131 us (0.942)
  waiting for transfers between devices: 48.7 us -> 44.8 us
  starting transfers between devices: 38.5 us -> 35.2 us
  Pallas kernels: 32.1 us -> 30.2 us
    ppermute x17 -> x14, waiting for transfers between devices: 41.6 us -> 32.7 us  [shift(): lax.ppermute(value, axis, [(i, (i + step) % RING) for i in range(RING)])]
    ppermute x17 -> x14, starting transfers between devices: 28 us -> 20.6 us  [shift(): lax.ppermute(value, axis, [(i, (i + step) % RING) for i in range(RING)])]
    ppermute x3 -> x5, starting transfers between devices: 0.14 us -> 6.1 us  [swap(): lax.ppermute(value, axis, [(i, i ^ bit) for i in range(2 if axis == 'core...]
    ppermute x3 -> x5, waiting for transfers between devices: 3.79 us -> 6.96 us  [swap(): lax.ppermute(value, axis, [(i, i ^ bit) for i in range(2 if axis == 'core...]
    pallas_call x1, Pallas kernels: 12.6 us -> 10.8 us  [hidden_and_gradient(): pl.pallas_call(gate_kernel, grid=(width // rows,), in_specs=[pl.BlockSpec...]
    ppermute x6, starting transfers between devices: 10.3 us -> 8.5 us  [shift(): return lax.ppermute(value, ('x', 'y', 'core'), pairs)]
    ppermute x6, waiting for transfers between devices: 3.31 us -> 5.12 us  [shift(): return lax.ppermute(value, ('x', 'y', 'core'), pairs)]
  transfers between devices with their start and end apart: 26 -> 25, of which waited for: 13 -> 13; matrix products, arithmetic and copies ran while one was open for 10% -> 10% of each run, Pallas kernels for 21% -> 21%
where the time goes in v3:
time: 131 us; the launch traced here: 129 us
  waiting for transfers between devices  44.8 us (34%)
  starting transfers between devices  35.2 us (27%)
  Pallas kernels  30.2 us (23%)
  matrix products  11.2 us (9%)
  other arithmetic  3.57 us (3%)
  local copies, waits for them, and re-layouts  3.49 us (3%)
    ppermute x14, waiting for transfers between devices, shift(): lax.ppermute(value, axis, [(i, (i + step) % RING) for i in range(RING)])  32.7 us
    ppermute x14, starting transfers between devices, shift(): lax.ppermute(value, axis, [(i, (i + step) % RING) for i in range(RING)])  20.6 us
    pallas_call x9, Pallas kernels, call(): pl.pallas_call(body, in_specs=(in_specs or [VMEM] * count) + [ANY] * len(...  15.5 us
    dot_general x8, matrix products, dot_last(): lax.dot_general(left, right, (((1,), (1,)), ((), ())), preferred_element_...  11.2 us
    pallas_call x1, Pallas kernels, hidden_and_gradient(): pl.pallas_call(gate_kernel, grid=(width // rows,), in_specs=[pl.BlockSpec...  10.8 us
    ppermute x6, starting transfers between devices, shift(): return lax.ppermute(value, ('x', 'y', 'core'), pairs)  8.5 us
    ppermute x5, waiting for transfers between devices, swap(): lax.ppermute(value, axis, [(i, i ^ bit) for i in range(2 if axis == 'core...  6.96 us
    ppermute x5, starting transfers between devices, swap(): lax.ppermute(value, axis, [(i, i ^ bit) for i in range(2 if axis == 'core...  6.1 us
  transfers between devices with their start and end apart: 25, of which 13 were waited for; matrix products, arithmetic and copies ran while one was open for 10% of the time, Pallas kernels for 21%

profile of v3, /device:TPU:0, one launch (start us, length us, event | category | flops | bytes accessed | tf_op | source)
XLA Modules:
  0.0 129.3 jit_solution(8935929849685932372)
XLA Ops:
  0.6 1.7 %copy-done = bf16[256,5120]{1,0:T(8,128)(2,1)S(1)} copy-done((bf16[256,5120]{1,0:T(8,128)(2,1)S(1)}, bf16[256,5120]{1,0:T(8,128)(2,1)}, u32[]{:S(2)}) %copy-start) | copy-done | bytes 2621464
  2.4 1.7 %copy-done.2 = bf16[256,5120]{1,0:T(8,128)(2,1)S(1)} copy-done((bf16[256,5120]{1,0:T(8,128)(2,1)S(1)}, bf16[256,5120]{1,0:T(8,128)(2,1)}, u32[]{:S(2)}) %copy-start.2) | copy-done | bytes 2621464
  4.1 2.6 %column_parts.1 = (bf16[1280,256]{1,0:T(8,128)(2,1)S(1)}, bf16[1280,256]{1,0:T(8,128)(2,1)}, bf16[1280,256]{1,0:T(8,128)(2,1)}, bf16[1280,256]{1,0:T(8,128)(2,1)}) custom-call(bf16[256,5120]{1,0:T(8,128)(2,1)S(1)} %copy-done, bf16[256,5120]{1,0:T(8,128)(2,1)S(1)} %copy-done.2), custom_call_target="tpu_custom_call" | custom-call | tf_op jit(solution)/shard_map/column_parts/pallas_call | solution.py:83
  6.7 1.6 %collective-permute-start = (bf16[1280,256]{1,0:T(8,128)(2,1)}, bf16[1280,256]{1,0:T(8,128)(2,1)}, u32[]{:S(2)}, u32[]{:S(2)}) collective-permute-start(bf16[1280,256]{1,0:T(8,128)(2,1)} %get-tuple-element.20), channel_id=1, source_target_pairs={{0,32},{1,9},{8,40},{9,17},{16,48},{17,25},{24,56},{25,1},{32,64},... | collective-permute-start | bytes 1966088 | tf_op jit(solution)/shard_map/ppermute | solution.py:40
  8.4 1.7 %collective-permute-start.1 = (bf16[1280,256]{1,0:T(8,128)(2,1)}, bf16[1280,256]{1,0:T(8,128)(2,1)}, u32[]{:S(2)}, u32[]{:S(2)}) collective-permute-start(bf16[1280,256]{1,0:T(8,128)(2,1)} %get-tuple-element.21), channel_id=1, source_target_pairs={{0,96},{1,25},{8,104},{9,1},{16,112},{17,9},{24,120},{25,17},{32,0... | collective-permute-start | bytes 1966088 | tf_op jit(solution)/shard_map/ppermute | solution.py:40
  10.1 1.9 %collective-permute-start.2 = (bf16[1280,256]{1,0:T(8,128)(2,1)}, bf16[1280,256]{1,0:T(8,128)(2,1)}, u32[]{:S(2)}, u32[]{:S(2)}) collective-permute-start(bf16[1280,256]{1,0:T(8,128)(2,1)} %get-tuple-element.22), channel_id=1, source_target_pairs={{0,64},{1,17},{8,72},{9,25},{16,80},{17,1},{24,88},{25,9},{32,96},... | collective-permute-start | bytes 1966088 | tf_op jit(solution)/shard_map/ppermute | solution.py:40
  11.9 10.8 %hidden_and_gradient.1 = (bf16[1728,256]{1,0:T(8,128)(2,1)}, bf16[1728,256]{1,0:T(8,128)(2,1)}) custom-call(bf16[1728,5120]{1,0:T(8,128)(2,1)} %bitcast.20, bf16[256,5120]{1,0:T(8,128)(2,1)} %refs_0_.3, bf16[1728,256]{1,0:T(8,128)(2,1)S(1)} %bitcast.19, bf16[1728,256]{1,0:T(8,128)(2,1)} %bitcast.21, bf16[1280,256]{1,0:T(8,128)(2,1)S(1)} %get-tuple-element.19.rest_0_.refs_0_), custom_call_target="tpu_custom_call" | custom-call | flops 999999995904 | bytes 1000000000 | tf_op jit(solution)/shard_map/hidden_and_gradient/pallas_call | solution.py:111
  22.7 3.0 %collective-permute-start.10 = (bf16[1728,256]{1,0:T(8,128)(2,1)}, bf16[1728,256]{1,0:T(8,128)(2,1)}, u32[]{:S(2)}, u32[]{:S(2)}) collective-permute-start(bf16[1728,256]{1,0:T(8,128)(2,1)} %get-tuple-element.23.refs_4_.refs_3_), channel_id=1, source_target_pairs={{0,24},{8,0},{16,8},{24,16},{1,25},{9,1},{17,9},{25,17},{2,26},{10... | collective-permute-start | bytes 2654216 | tf_op jit(solution)/shard_map/ppermute | solution.py:33
  25.8 0.7 collective-permute-start.7
  26.4 2.7 %collective-permute-start.8 = (bf16[1728,256]{1,0:T(8,128)(2,1)}, bf16[1728,256]{1,0:T(8,128)(2,1)}, u32[]{:S(2)}, u32[]{:S(2)}) collective-permute-start(bf16[1728,256]{1,0:T(8,128)(2,1)} %get-tuple-element.24.refs_2_.refs_3_), channel_id=1, source_target_pairs={{0,96},{32,0},{64,32},{96,64},{1,97},{33,1},{65,33},{97,65},{2,98}... | collective-permute-start | bytes 2654216 | tf_op jit(solution)/shard_map/ppermute | solution.py:33
  29.2 4.0 %stack.1.refs_0_ = bf16[4,1280,256]{2,1,0:T(8,128)(2,1)} custom-call(bf16[1280,256]{1,0:T(8,128)(2,1)S(1)} %get-tuple-element.19.rest_0_.refs_0_, bf16[1280,256]{1,0:T(8,128)(2,1)} %collective-permute-done.refs_1_.refs_4_, bf16[1280,256]{1,0:T(8,128)(2,1)} %collective-permute-done.1.refs_2_.refs_5_, ...), custom_call_target="tpu_custom_call" | custom-call | tf_op jit(solution)/shard_map/stack/pallas_call | solution.py:173
  33.2 3.6 %squares.1.refs_0_ = f32[8,128]{1,0:T(8,128)S(1)} custom-call(bf16[256,5120]{1,0:T(8,128)(2,1)S(1)} %copy-done.1, bf16[256,5120]{1,0:T(8,128)(2,1)S(1)} %copy-done.3, bf16[1728,256]{1,0:T(8,128)(2,1)} %get-tuple-element.24.refs_2_.refs_3_, bf16[1728,256]{1,0:T(8,128)(2,1)} %get-tuple-element.23.refs_4_.refs_3_, ...), custom_call_target="tpu_custom_call" | custom-call | flops 999999995904 | bytes 1000000000 | tf_op jit(solution)/shard_map/squares/pallas_call | solution.py:83
  36.8 1.6 %collective-permute-done.3.refs_1_ = bf16[4,1280,256]{2,1,0:T(8,128)(2,1)} collective-permute-done((bf16[4,1280,256]{2,1,0:T(8,128)(2,1)}, bf16[4,1280,256]{2,1,0:T(8,128)(2,1)}, u32[]{:S(2)}, u32[]{:S(2)}) %collective-permute-start.3) | collective-permute-done | bytes 2621472 | tf_op jit(solution)/shard_map/ppermute | solution.py:44
  38.5 1.0 collective-permute-done.4
  39.6 2.0 %collective-permute-start.5 = (f32[8,128]{1,0:T(8,128)S(1)}, f32[8,128]{1,0:T(8,128)S(1)}, u32[]{:S(2)}, u32[]{:S(2)}) collective-permute-start(f32[8,128]{1,0:T(8,128)S(1)} %add.42), channel_id=1, source_target_pairs={{0,2},{2,0},{4,6},{6,4},{1,3},{3,1},{5,7},{7,5},{8,10},{10,8},{12,... | collective-permute-start | bytes 12296 | tf_op jit(solution)/shard_map/ppermute | solution.py:44
  41.6 1.6 %collective-permute-done.5 = f32[8,128]{1,0:T(8,128)S(1)} collective-permute-done((f32[8,128]{1,0:T(8,128)S(1)}, f32[8,128]{1,0:T(8,128)S(1)}, u32[]{:S(2)}, u32[]{:S(2)}) %collective-permute-start.5) | collective-permute-done | bytes 4128 | tf_op jit(solution)/shard_map/ppermute | solution.py:44
  43.2 4.0 %collective-permute-start.6 = (f32[8,128]{1,0:T(8,128)S(1)}, f32[8,128]{1,0:T(8,128)S(1)}, u32[]{:S(2)}, u32[]{:S(2)}) collective-permute-start(f32[8,128]{1,0:T(8,128)S(1)} %add.43.refs_0_), channel_id=1, source_target_pairs={{0,4},{2,6},{4,0},{6,2},{1,5},{3,7},{5,1},{7,3},{8,12},{10,14},{12... | collective-permute-start | bytes 12296 | tf_op jit(solution)/shard_map/ppermute | solution.py:44
  47.2 1.6 %collective-permute-done.6.refs_1_ = f32[8,128]{1,0:T(8,128)S(1)} collective-permute-done((f32[8,128]{1,0:T(8,128)S(1)}, f32[8,128]{1,0:T(8,128)S(1)}, u32[]{:S(2)}, u32[]{:S(2)}) %collective-permute-start.6) | collective-permute-done | bytes 4128 | tf_op jit(solution)/shard_map/ppermute | solution.py:44
  49.4 3.2 %collective-permute-start.12 = (f32[8,128]{1,0:T(8,128)S(1)}, f32[8,128]{1,0:T(8,128)S(1)}, u32[]{:S(2)}, u32[]{:S(2)}) collective-permute-start(f32[8,128]{1,0:T(8,128)S(1)} %factor.1.refs_2_), channel_id=1, source_target_pairs={{0,96},{1,25},{8,104},{9,1},{16,112},{17,9},{24,120},{25,17},{32,0... | collective-permute-start | bytes 12296 | tf_op jit(solution)/shard_map/ppermute | solution.py:40
  52.6 1.6 %collective-permute-done.11.refs_0_ = f32[8,128]{1,0:T(8,128)S(1)} collective-permute-done((f32[8,128]{1,0:T(8,128)S(1)}, f32[8,128]{1,0:T(8,128)S(1)}, u32[]{:S(2)}, u32[]{:S(2)}) %collective-permute-start.11) | collective-permute-done | bytes 4128 | tf_op jit(solution)/shard_map/ppermute | solution.py:40
  54.2 3.5 %collective-permute-done.13.refs_2_ = f32[8,128]{1,0:T(8,128)S(1)} collective-permute-done((f32[8,128]{1,0:T(8,128)S(1)}, f32[8,128]{1,0:T(8,128)S(1)}, u32[]{:S(2)}, u32[]{:S(2)}) %collective-permute-start.13) | collective-permute-done | bytes 4128 | tf_op jit(solution)/shard_map/ppermute | solution.py:40
  57.7 3.2 %collective-permute-start.20 = (bf16[1728,256]{1,0:T(8,128)(2,1)}, bf16[1728,256]{1,0:T(8,128)(2,1)S(1)}, u32[]{:S(2)}, u32[]{:S(2)}) collective-permute-start(bf16[1728,256]{1,0:T(8,128)(2,1)} %get-tuple-element.32.refs_0_), channel_id=1, source_target_pairs={{0,16},{8,24},{16,0},{24,8},{1,17},{9,25},{17,1},{25,9},{2,18},{10... | collective-permute-start | bytes 2654216 | tf_op jit(solution)/shard_map/ppermute | solution.py:33
  60.9 1.2 collective-permute-done.14.refs_4_
  62.1 2.1 %lefts.3 = (bf16[320,1024]{1,0:T(8,128)(2,1)S(1)}, bf16[320,1024]{1,0:T(8,128)(2,1)S(1)}, bf16[320,1024]{1,0:T(8,128)(2,1)S(1)}, bf16[320,1024]{1,0:T(8,128)(2,1)S(1)}) custom-call(bf16[4,1280,256]{2,1,0:T(8,128)(2,1)} %stack.1.refs_0_, bf16[4,1280,256]{2,1,0:T(8,128)(2,1)} %collective-permute-done.3.refs_1_, f32[8,128]{1,0:T(8,128)S(1)} %factor.1.refs_2_, ...), custom_call_target="tpu_custom_call" | custom-call | tf_op jit(solution)/shard_map/lefts/pallas_call | solution.py:83
  64.3 2.2 %lefts.2 = (bf16[320,1024]{1,0:T(8,128)(2,1)S(1)}, bf16[320,1024]{1,0:T(8,128)(2,1)S(1)}, bf16[320,1024]{1,0:T(8,128)(2,1)S(1)}, bf16[320,1024]{1,0:T(8,128)(2,1)S(1)}) custom-call(bf16[4,1280,256]{2,1,0:T(8,128)(2,1)} %stack.1.refs_0_, bf16[4,1280,256]{2,1,0:T(8,128)(2,1)} %collective-permute-done.3.refs_1_, f32[8,128]{1,0:T(8,128)S(1)} %factor.1.refs_2_, ...), custom_call_target="tpu_custom_call" | custom-call | tf_op jit(solution)/shard_map/lefts/pallas_call | solution.py:83
  66.4 11.5 %collective-permute-done.20.refs_3_ = bf16[1728,256]{1,0:T(8,128)(2,1)S(1)} collective-permute-done((bf16[1728,256]{1,0:T(8,128)(2,1)}, bf16[1728,256]{1,0:T(8,128)(2,1)S(1)}, u32[]{:S(2)}, u32[]{:S(2)}) %collective-permute-start.20) | collective-permute-done | bytes 884768 | tf_op jit(solution)/shard_map/ppermute | solution.py:33
  78.0 2.2 %wide.3 = bf16[1728,1024]{1,0:T(8,128)(2,1)S(1)} custom-call(bf16[1728,256]{1,0:T(8,128)(2,1)} %get-tuple-element.32.refs_0_, bf16[1728,256]{1,0:T(8,128)(2,1)} %collective-permute-done.9.refs_5_.refs_1_, bf16[1728,256]{1,0:T(8,128)(2,1)} %collective-permute-done.10.refs_6_.refs_2_, bf16[1728,256]{1,0:T(8,128)(2,1)S(1)} %collective-permute-done.20.refs_3_), custom_call_target="tpu_custom_call" | custom-call | tf_op jit(solution)/shard_map/wide/pallas_call | solution.py:83
  80.1 1.4 %convolution_convert_fusion.2 = bf16[320,1728]{1,0:T(8,128)(2,1)S(1)} fusion(bf16[320,1024]{1,0:T(8,128)(2,1)S(1)} %get-tuple-element.33, bf16[1728,1024]{1,0:T(8,128)(2,1)S(1)} %wide.3), kind=kOutput, calls=%fused_computation.2 | convolution fusion | flops 1133015040 | bytes 5300224 | tf_op jit(solution)/shard_map/dot_general | solution.py:48
  81.6 1.8 %collective-permute-start.21 = (bf16[320,1728]{1,0:T(8,128)(2,1)S(1)}, bf16[320,1728]{1,0:T(8,128)(2,1)S(1)}, u32[]{:S(2)}, u32[]{:S(2)}) collective-permute-start(bf16[320,1728]{1,0:T(8,128)(2,1)S(1)} %convolution_convert_fusion.2), channel_id=1, source_target_pairs={{0,96},{32,0},{64,32},{96,64},{1,97},{33,1},{65,33},{97,65},{2,98}... | collective-permute-start | bytes 3317768 | tf_op jit(solution)/shard_map/ppermute | solution.py:33
  83.4 1.4 %convolution_convert_fusion = bf16[320,1728]{1,0:T(8,128)(2,1)S(1)} fusion(bf16[320,1024]{1,0:T(8,128)(2,1)S(1)} %get-tuple-element.35, bf16[1728,1024]{1,0:T(8,128)(2,1)S(1)} %wide.3), kind=kOutput, calls=%fused_computation | convolution fusion | flops 1133015040 | bytes 5300224 | tf_op jit(solution)/shard_map/dot_general | solution.py:48
  85.1 2.2 %wide.2 = bf16[1728,1024]{1,0:T(8,128)(2,1)S(1)} custom-call(bf16[1728,256]{1,0:T(8,128)(2,1)} %get-tuple-element.27.refs_0_, bf16[1728,256]{1,0:T(8,128)(2,1)} %collective-permute-done.7.refs_3_.refs_1_, bf16[1728,256]{1,0:T(8,128)(2,1)} %collective-permute-done.8.refs_4_.refs_2_, bf16[1728,256]{1,0:T(8,128)(2,1)S(1)} %collective-permute-done.15.refs_3_), custom_call_target="tpu_custom_call" | custom-call | tf_op jit(solution)/shard_map/wide/pallas_call | solution.py:83
  87.3 1.4 %convolution_convert_fusion.6 = bf16[320,1728]{1,0:T(8,128)(2,1)S(1)} fusion(bf16[320,1024]{1,0:T(8,128)(2,1)S(1)} %get-tuple-element.28, bf16[1728,1024]{1,0:T(8,128)(2,1)S(1)} %wide.2), kind=kOutput, calls=%fused_computation.6 | convolution fusion | flops 1133015040 | bytes 5300224 | tf_op jit(solution)/shard_map/dot_general | solution.py:48
  88.7 1.7 %collective-permute-start.16 = (bf16[320,1728]{1,0:T(8,128)(2,1)S(1)}, bf16[320,1728]{1,0:T(8,128)(2,1)S(1)}, u32[]{:S(2)}, u32[]{:S(2)}) collective-permute-start(bf16[320,1728]{1,0:T(8,128)(2,1)S(1)} %convolution_convert_fusion.6), channel_id=1, source_target_pairs={{0,24},{8,0},{16,8},{24,16},{1,25},{9,1},{17,9},{25,17},{2,26},{10... | collective-permute-start | bytes 3317768 | tf_op jit(solution)/shard_map/ppermute | solution.py:33
  90.5 1.4 %convolution_convert_fusion.4 = bf16[320,1728]{1,0:T(8,128)(2,1)S(1)} fusion(bf16[320,1024]{1,0:T(8,128)(2,1)S(1)} %get-tuple-element.30, bf16[1728,1024]{1,0:T(8,128)(2,1)S(1)} %wide.2), kind=kOutput, calls=%fused_computation.4 | convolution fusion | flops 1133015040 | bytes 5300224 | tf_op jit(solution)/shard_map/dot_general | solution.py:48
  92.3 1.4 %convolution_convert_fusion.3 = bf16[320,1728]{1,0:T(8,128)(2,1)S(1)} fusion(bf16[320,1024]{1,0:T(8,128)(2,1)S(1)} %get-tuple-element.31, bf16[1728,1024]{1,0:T(8,128)(2,1)S(1)} %wide.3), kind=kOutput, calls=%fused_computation.3 | convolution fusion | flops 1133015040 | bytes 5300224 | tf_op jit(solution)/shard_map/dot_general | solution.py:48
  93.7 1.4 %convolution_convert_fusion.1 = bf16[320,1728]{1,0:T(8,128)(2,1)S(1)} fusion(bf16[320,1024]{1,0:T(8,128)(2,1)S(1)} %get-tuple-element.34, bf16[1728,1024]{1,0:T(8,128)(2,1)S(1)} %wide.3), kind=kOutput, calls=%fused_computation.1 | convolution fusion | flops 1133015040 | bytes 5300224 | tf_op jit(solution)/shard_map/dot_general | solution.py:48
  95.1 1.4 %convolution_convert_fusion.7 = bf16[320,1728]{1,0:T(8,128)(2,1)S(1)} fusion(bf16[320,1024]{1,0:T(8,128)(2,1)S(1)} %get-tuple-element.26, bf16[1728,1024]{1,0:T(8,128)(2,1)S(1)} %wide.2), kind=kOutput, calls=%fused_computation.7 | convolution fusion | flops 1133015040 | bytes 5300224 | tf_op jit(solution)/shard_map/dot_general | solution.py:48
  96.5 8.9 %collective-permute-done.21 = bf16[320,1728]{1,0:T(8,128)(2,1)S(1)} collective-permute-done((bf16[320,1728]{1,0:T(8,128)(2,1)S(1)}, bf16[320,1728]{1,0:T(8,128)(2,1)S(1)}, u32[]{:S(2)}, u32[]{:S(2)}) %collective-permute-start.21) | collective-permute-done | bytes 1105952 | tf_op jit(solution)/shard_map/ppermute | solution.py:33
  105.4 4.9 %collective-permute-done.22 = bf16[320,1728]{1,0:T(8,128)(2,1)S(1)} collective-permute-done((bf16[320,1728]{1,0:T(8,128)(2,1)S(1)}, bf16[320,1728]{1,0:T(8,128)(2,1)S(1)}, u32[]{:S(2)}, u32[]{:S(2)}) %collective-permute-start.22) | collective-permute-done | bytes 1105952 | tf_op jit(solution)/shard_map/ppermute | solution.py:33
  110.7 3.2 %collective-permute-start.24 = (bf16[160,1728]{1,0:T(8,128)(2,1)S(1)}, bf16[160,1728]{1,0:T(8,128)(2,1)S(1)}, u32[]{:S(2)}, u32[]{:S(2)}) collective-permute-start(bf16[160,1728]{1,0:T(8,128)(2,1)S(1)} %get-tuple-element.39), channel_id=1, source_target_pairs={{0,96},{32,0},{64,32},{96,64},{1,97},{33,1},{65,33},{97,65},{2,98}... | collective-permute-start | bytes 1658888 | tf_op jit(solution)/shard_map/ppermute | solution.py:33
  113.9 1.4 %convolution_convert_fusion.5 = bf16[320,1728]{1,0:T(8,128)(2,1)S(1)} fusion(bf16[320,1024]{1,0:T(8,128)(2,1)S(1)} %get-tuple-element.29, bf16[1728,1024]{1,0:T(8,128)(2,1)S(1)} %wide.2), kind=kOutput, calls=%fused_computation.5 | convolution fusion | flops 1133015040 | bytes 5300224 | tf_op jit(solution)/shard_map/dot_general | solution.py:48
  115.3 0.6 collective-permute-done.17
  116.1 1.6 %collective-permute-start.18 = (bf16[160,1728]{1,0:T(8,128)(2,1)S(1)}, bf16[160,1728]{1,0:T(8,128)(2,1)S(1)}, u32[]{:S(2)}, u32[]{:S(2)}) collective-permute-start(bf16[160,1728]{1,0:T(8,128)(2,1)S(1)} %get-tuple-element.42), channel_id=1, source_target_pairs={{0,8},{8,16},{16,24},{24,0},{1,9},{9,17},{17,25},{25,1},{2,10},{10... | collective-permute-start | bytes 1658888 | tf_op jit(solution)/shard_map/ppermute | solution.py:33
  117.7 1.7 %collective-permute-start.19 = (bf16[160,1728]{1,0:T(8,128)(2,1)S(1)}, bf16[160,1728]{1,0:T(8,128)(2,1)S(1)}, u32[]{:S(2)}, u32[]{:S(2)}) collective-permute-start(bf16[160,1728]{1,0:T(8,128)(2,1)S(1)} %get-tuple-element.43), channel_id=1, source_target_pairs={{0,24},{8,0},{16,8},{24,16},{1,25},{9,1},{17,9},{25,17},{2,26},{10... | collective-permute-start | bytes 1658888 | tf_op jit(solution)/shard_map/ppermute | solution.py:33
  119.5 3.4 %collective-permute-done.23 = bf16[160,1728]{1,0:T(8,128)(2,1)S(1)} collective-permute-done((bf16[160,1728]{1,0:T(8,128)(2,1)S(1)}, bf16[160,1728]{1,0:T(8,128)(2,1)S(1)}, u32[]{:S(2)}, u32[]{:S(2)}) %collective-permute-start.23) | collective-permute-done | bytes 552992 | tf_op jit(solution)/shard_map/ppermute | solution.py:33
  123.3 1.1 fusion.1
  124.4 3.4 %collective-permute-done.18 = bf16[160,1728]{1,0:T(8,128)(2,1)S(1)} collective-permute-done((bf16[160,1728]{1,0:T(8,128)(2,1)S(1)}, bf16[160,1728]{1,0:T(8,128)(2,1)S(1)}, u32[]{:S(2)}, u32[]{:S(2)}) %collective-permute-start.18) | collective-permute-done | bytes 552992 | tf_op jit(solution)/shard_map/ppermute | solution.py:33
  128.2 1.1 fusion
  (41 shorter events, 3.0 us)
Async XLA Ops:
  0.6 1.7 %copy-start = (bf16[256,5120]{1,0:T(8,128)(2,1)S(1)}, bf16[256,5120]{1,0:T(8,128)(2,1)}, u32[]{:S(2)}) copy-start(bf16[256,5120]{1,0:T(8,128)(2,1)} %refs_0_.3) | copy-start | bytes 7864324
  2.4 1.7 %copy-start.2 = (bf16[256,5120]{1,0:T(8,128)(2,1)S(1)}, bf16[256,5120]{1,0:T(8,128)(2,1)}, u32[]{:S(2)}) copy-start(bf16[256,5120]{1,0:T(8,128)(2,1)} %refs_1_.3) | copy-start | bytes 7864324
  4.1 7.8 %copy-start.5 = (bf16[256,1728]{0,1:T(8,128)(2,1)S(1)}, bf16[256,1728]{0,1:T(8,128)(2,1)}, u32[]{:S(2)}) copy-start(bf16[256,1728]{0,1:T(8,128)(2,1)} %param.8) | copy-start | bytes 2654212
  6.7 19.0 %collective-permute-start = (bf16[1280,256]{1,0:T(8,128)(2,1)}, bf16[1280,256]{1,0:T(8,128)(2,1)}, u32[]{:S(2)}, u32[]{:S(2)}) collective-permute-start(bf16[1280,256]{1,0:T(8,128)(2,1)} %get-tuple-element.20), channel_id=1, source_target_pairs={{0,32},{1,9},{8,40},{9,17},{16,48},{17,25},{24,56},{25,1},{32,64},... | collective-permute-start | bytes 1966088 | tf_op jit(solution)/shard_map/ppermute | solution.py:40
  8.4 18.1 %collective-permute-start.1 = (bf16[1280,256]{1,0:T(8,128)(2,1)}, bf16[1280,256]{1,0:T(8,128)(2,1)}, u32[]{:S(2)}, u32[]{:S(2)}) collective-permute-start(bf16[1280,256]{1,0:T(8,128)(2,1)} %get-tuple-element.21), channel_id=1, source_target_pairs={{0,96},{1,25},{8,104},{9,1},{16,112},{17,9},{24,120},{25,17},{32,0... | collective-permute-start | bytes 1966088 | tf_op jit(solution)/shard_map/ppermute | solution.py:40
  10.1 19.1 %collective-permute-start.2 = (bf16[1280,256]{1,0:T(8,128)(2,1)}, bf16[1280,256]{1,0:T(8,128)(2,1)}, u32[]{:S(2)}, u32[]{:S(2)}) collective-permute-start(bf16[1280,256]{1,0:T(8,128)(2,1)} %get-tuple-element.22), channel_id=1, source_target_pairs={{0,64},{1,17},{8,72},{9,25},{16,80},{17,1},{24,88},{25,9},{32,96},... | collective-permute-start | bytes 1966088 | tf_op jit(solution)/shard_map/ppermute | solution.py:40
  22.7 24.4 %collective-permute-start.10 = (bf16[1728,256]{1,0:T(8,128)(2,1)}, bf16[1728,256]{1,0:T(8,128)(2,1)}, u32[]{:S(2)}, u32[]{:S(2)}) collective-permute-start(bf16[1728,256]{1,0:T(8,128)(2,1)} %get-tuple-element.23.refs_4_.refs_3_), channel_id=1, source_target_pairs={{0,24},{8,0},{16,8},{24,16},{1,25},{9,1},{17,9},{25,17},{2,26},{10... | collective-permute-start | bytes 2654216 | tf_op jit(solution)/shard_map/ppermute | solution.py:33
  25.7 21.4 %collective-permute-start.9 = (bf16[1728,256]{1,0:T(8,128)(2,1)}, bf16[1728,256]{1,0:T(8,128)(2,1)}, u32[]{:S(2)}, u32[]{:S(2)}) collective-permute-start(bf16[1728,256]{1,0:T(8,128)(2,1)} %get-tuple-element.23.refs_4_.refs_3_), channel_id=1, source_target_pairs={{0,8},{8,16},{16,24},{24,0},{1,9},{9,17},{17,25},{25,1},{2,10},{10... | collective-permute-start | bytes 2654216 | tf_op jit(solution)/shard_map/ppermute | solution.py:33
  25.8 7.4 %copy-start.1 = (bf16[256,5120]{1,0:T(8,128)(2,1)S(1)}, bf16[256,5120]{1,0:T(8,128)(2,1)}, u32[]{:S(2)}) copy-start(bf16[256,5120]{1,0:T(8,128)(2,1)} %refs_0_.3) | copy-start | bytes 7864324
  25.8 7.4 %copy-start.3 = (bf16[256,5120]{1,0:T(8,128)(2,1)S(1)}, bf16[256,5120]{1,0:T(8,128)(2,1)}, u32[]{:S(2)}) copy-start(bf16[256,5120]{1,0:T(8,128)(2,1)} %refs_1_.3) | copy-start | bytes 7864324
  25.8 21.4 %collective-permute-start.7 = (bf16[1728,256]{1,0:T(8,128)(2,1)}, bf16[1728,256]{1,0:T(8,128)(2,1)}, u32[]{:S(2)}, u32[]{:S(2)}) collective-permute-start(bf16[1728,256]{1,0:T(8,128)(2,1)} %get-tuple-element.24.refs_2_.refs_3_), channel_id=1, source_target_pairs={{0,32},{32,64},{64,96},{96,0},{1,33},{33,65},{65,97},{97,1},{2,34}... | collective-permute-start | bytes 2654216 | tf_op jit(solution)/shard_map/ppermute | solution.py:33
  26.4 20.7 %collective-permute-start.8 = (bf16[1728,256]{1,0:T(8,128)(2,1)}, bf16[1728,256]{1,0:T(8,128)(2,1)}, u32[]{:S(2)}, u32[]{:S(2)}) collective-permute-start(bf16[1728,256]{1,0:T(8,128)(2,1)} %get-tuple-element.24.refs_2_.refs_3_), channel_id=1, source_target_pairs={{0,96},{32,0},{64,32},{96,64},{1,97},{33,1},{65,33},{97,65},{2,98}... | collective-permute-start | bytes 2654216 | tf_op jit(solution)/shard_map/ppermute | solution.py:33
  33.1 5.3 %collective-permute-start.3 = (bf16[4,1280,256]{2,1,0:T(8,128)(2,1)}, bf16[4,1280,256]{2,1,0:T(8,128)(2,1)}, u32[]{:S(2)}, u32[]{:S(2)}) collective-permute-start(bf16[4,1280,256]{2,1,0:T(8,128)(2,1)} %stack.1.refs_0_), channel_id=1, source_target_pairs={{0,1},{1,0},{2,3},{3,2},{4,5},{5,4},{6,7},{7,6},{8,9},{9,8},{10,11... | collective-permute-start | bytes 7864328 | tf_op jit(solution)/shard_map/ppermute | solution.py:44
  36.8 11.9 %copy-start.4 = (f32[2]{0:T(128)S(1)}, f32[2]{0:T(128)}, u32[]{:S(2)}) copy-start(f32[2]{0:T(128)} %refs_2_.1) | copy-start | bytes 28
  38.4 1.2 collective-permute-start.4
  39.6 3.6 %collective-permute-start.5 = (f32[8,128]{1,0:T(8,128)S(1)}, f32[8,128]{1,0:T(8,128)S(1)}, u32[]{:S(2)}, u32[]{:S(2)}) collective-permute-start(f32[8,128]{1,0:T(8,128)S(1)} %add.42), channel_id=1, source_target_pairs={{0,2},{2,0},{4,6},{6,4},{1,3},{3,1},{5,7},{7,5},{8,10},{10,8},{12,... | collective-permute-start | bytes 12296 | tf_op jit(solution)/shard_map/ppermute | solution.py:44
  43.2 5.5 %collective-permute-start.6 = (f32[8,128]{1,0:T(8,128)S(1)}, f32[8,128]{1,0:T(8,128)S(1)}, u32[]{:S(2)}, u32[]{:S(2)}) collective-permute-start(f32[8,128]{1,0:T(8,128)S(1)} %add.43.refs_0_), channel_id=1, source_target_pairs={{0,4},{2,6},{4,0},{6,2},{1,5},{3,7},{5,1},{7,3},{8,12},{10,14},{12... | collective-permute-start | bytes 12296 | tf_op jit(solution)/shard_map/ppermute | solution.py:44
  49.3 4.9 %collective-permute-start.11 = (f32[8,128]{1,0:T(8,128)S(1)}, f32[8,128]{1,0:T(8,128)S(1)}, u32[]{:S(2)}, u32[]{:S(2)}) collective-permute-start(f32[8,128]{1,0:T(8,128)S(1)} %factor.1.refs_2_), channel_id=1, source_target_pairs={{0,32},{1,9},{8,40},{9,17},{16,48},{17,25},{24,56},{25,1},{32,64},... | collective-permute-start | bytes 12296 | tf_op jit(solution)/shard_map/ppermute | solution.py:40
  49.4 4.8 %collective-permute-start.12 = (f32[8,128]{1,0:T(8,128)S(1)}, f32[8,128]{1,0:T(8,128)S(1)}, u32[]{:S(2)}, u32[]{:S(2)}) collective-permute-start(f32[8,128]{1,0:T(8,128)S(1)} %factor.1.refs_2_), channel_id=1, source_target_pairs={{0,96},{1,25},{8,104},{9,1},{16,112},{17,9},{24,120},{25,17},{32,0... | collective-permute-start | bytes 12296 | tf_op jit(solution)/shard_map/ppermute | solution.py:40
  52.6 5.1 %collective-permute-start.13 = (f32[8,128]{1,0:T(8,128)S(1)}, f32[8,128]{1,0:T(8,128)S(1)}, u32[]{:S(2)}, u32[]{:S(2)}) collective-permute-start(f32[8,128]{1,0:T(8,128)S(1)} %factor.1.refs_2_), channel_id=1, source_target_pairs={{0,64},{1,17},{8,72},{9,25},{16,80},{17,1},{24,88},{25,9},{32,96},... | collective-permute-start | bytes 12296 | tf_op jit(solution)/shard_map/ppermute | solution.py:40
  57.7 20.2 %collective-permute-start.20 = (bf16[1728,256]{1,0:T(8,128)(2,1)}, bf16[1728,256]{1,0:T(8,128)(2,1)S(1)}, u32[]{:S(2)}, u32[]{:S(2)}) collective-permute-start(bf16[1728,256]{1,0:T(8,128)(2,1)} %get-tuple-element.32.refs_0_), channel_id=1, source_target_pairs={{0,16},{8,24},{16,0},{24,8},{1,17},{9,25},{17,1},{25,9},{2,18},{10... | collective-permute-start | bytes 2654216 | tf_op jit(solution)/shard_map/ppermute | solution.py:33
  60.9 24.2 %collective-permute-start.15 = (bf16[1728,256]{1,0:T(8,128)(2,1)}, bf16[1728,256]{1,0:T(8,128)(2,1)S(1)}, u32[]{:S(2)}, u32[]{:S(2)}) collective-permute-start(bf16[1728,256]{1,0:T(8,128)(2,1)} %get-tuple-element.27.refs_0_), channel_id=1, source_target_pairs={{0,64},{32,96},{64,0},{96,32},{1,65},{33,97},{65,1},{97,33},{2,66}... | collective-permute-start | bytes 2654216 | tf_op jit(solution)/shard_map/ppermute | solution.py:33
  60.9 1.2 collective-permute-start.14
  81.6 23.9 %collective-permute-start.21 = (bf16[320,1728]{1,0:T(8,128)(2,1)S(1)}, bf16[320,1728]{1,0:T(8,128)(2,1)S(1)}, u32[]{:S(2)}, u32[]{:S(2)}) collective-permute-start(bf16[320,1728]{1,0:T(8,128)(2,1)S(1)} %convolution_convert_fusion.2), channel_id=1, source_target_pairs={{0,96},{32,0},{64,32},{96,64},{1,97},{33,1},{65,33},{97,65},{2,98}... | collective-permute-start | bytes 3317768 | tf_op jit(solution)/shard_map/ppermute | solution.py:33
  84.8 25.5 %collective-permute-start.22 = (bf16[320,1728]{1,0:T(8,128)(2,1)S(1)}, bf16[320,1728]{1,0:T(8,128)(2,1)S(1)}, u32[]{:S(2)}, u32[]{:S(2)}) collective-permute-start(bf16[320,1728]{1,0:T(8,128)(2,1)S(1)} %convolution_convert_fusion), channel_id=1, source_target_pairs={{0,32},{32,64},{64,96},{96,0},{1,33},{33,65},{65,97},{97,1},{2,34}... | collective-permute-start | bytes 3317768 | tf_op jit(solution)/shard_map/ppermute | solution.py:33
  88.7 26.6 %collective-permute-start.16 = (bf16[320,1728]{1,0:T(8,128)(2,1)S(1)}, bf16[320,1728]{1,0:T(8,128)(2,1)S(1)}, u32[]{:S(2)}, u32[]{:S(2)}) collective-permute-start(bf16[320,1728]{1,0:T(8,128)(2,1)S(1)} %convolution_convert_fusion.6), channel_id=1, source_target_pairs={{0,24},{8,0},{16,8},{24,16},{1,25},{9,1},{17,9},{25,17},{2,26},{10... | collective-permute-start | bytes 3317768 | tf_op jit(solution)/shard_map/ppermute | solution.py:33
  91.9 24.0 %collective-permute-start.17 = (bf16[320,1728]{1,0:T(8,128)(2,1)S(1)}, bf16[320,1728]{1,0:T(8,128)(2,1)S(1)}, u32[]{:S(2)}, u32[]{:S(2)}) collective-permute-start(bf16[320,1728]{1,0:T(8,128)(2,1)S(1)} %convolution_convert_fusion.4), channel_id=1, source_target_pairs={{0,8},{8,16},{16,24},{24,0},{1,9},{9,17},{17,25},{25,1},{2,10},{10... | collective-permute-start | bytes 3317768 | tf_op jit(solution)/shard_map/ppermute | solution.py:33
  110.6 12.3 %collective-permute-start.23 = (bf16[160,1728]{1,0:T(8,128)(2,1)S(1)}, bf16[160,1728]{1,0:T(8,128)(2,1)S(1)}, u32[]{:S(2)}, u32[]{:S(2)}) collective-permute-start(bf16[160,1728]{1,0:T(8,128)(2,1)S(1)} %get-tuple-element.38), channel_id=1, source_target_pairs={{0,32},{32,64},{64,96},{96,0},{1,33},{33,65},{65,97},{97,1},{2,34}... | collective-permute-start | bytes 1658888 | tf_op jit(solution)/shard_map/ppermute | solution.py:33
  110.7 12.2 %collective-permute-start.24 = (bf16[160,1728]{1,0:T(8,128)(2,1)S(1)}, bf16[160,1728]{1,0:T(8,128)(2,1)S(1)}, u32[]{:S(2)}, u32[]{:S(2)}) collective-permute-start(bf16[160,1728]{1,0:T(8,128)(2,1)S(1)} %get-tuple-element.39), channel_id=1, source_target_pairs={{0,96},{32,0},{64,32},{96,64},{1,97},{33,1},{65,33},{97,65},{2,98}... | collective-permute-start | bytes 1658888 | tf_op jit(solution)/shard_map/ppermute | solution.py:33
  116.1 11.6 %collective-permute-start.18 = (bf16[160,1728]{1,0:T(8,128)(2,1)S(1)}, bf16[160,1728]{1,0:T(8,128)(2,1)S(1)}, u32[]{:S(2)}, u32[]{:S(2)}) collective-permute-start(bf16[160,1728]{1,0:T(8,128)(2,1)S(1)} %get-tuple-element.42), channel_id=1, source_target_pairs={{0,8},{8,16},{16,24},{24,0},{1,9},{9,17},{17,25},{25,1},{2,10},{10... | collective-permute-start | bytes 1658888 | tf_op jit(solution)/shard_map/ppermute | solution.py:33
  117.7 10.0 %collective-permute-start.19 = (bf16[160,1728]{1,0:T(8,128)(2,1)S(1)}, bf16[160,1728]{1,0:T(8,128)(2,1)S(1)}, u32[]{:S(2)}, u32[]{:S(2)}) collective-permute-start(bf16[160,1728]{1,0:T(8,128)(2,1)S(1)} %get-tuple-element.43), channel_id=1, source_target_pairs={{0,24},{8,0},{16,8},{24,16},{1,25},{9,1},{17,9},{25,17},{2,26},{10... | collective-permute-start | bytes 1658888 | tf_op jit(solution)/shard_map/ppermute | solution.py:33

commit v4 on v3

--- a/solution.py
+++ b/solution.py
@@ -150,15 +150,16 @@
 
 
 def wide_kernel(*refs):
-    tokens = refs[0].shape[1]
-    for at in range(RING):
-        refs[RING][:, pl.ds(at * tokens, tokens)] = refs[at][...]
-
-
-def wide(blocks, after):
-    rows, tokens = blocks[0].shape
-    shape = jax.ShapeDtypeStruct((rows, RING * tokens), blocks[0].dtype)
-    return call(wide_kernel, "wide", blocks, after, [shape], SMALL, 12)[0]
+    start = 0
+    for block in refs[:-1]:
+        refs[-1][:, pl.ds(start, block.shape[1])] = block[...]
+        start += block.shape[1]
+
+
+def wide(blocks):
+    width = sum(b.shape[1] for b in blocks)
+    shape = jax.ShapeDtypeStruct((blocks[0].shape[0], width), blocks[0].dtype)
+    return call(wide_kernel, "wide", blocks, [], [shape], SMALL, 12)[0]
 
 
 def stack_kernel(*refs):
@@ -217,14 +218,14 @@
         out[...] = (held_ref[at].astype(jnp.float32) * scale).astype(out.dtype)
 
 
-def lefts_of(owner, axis, mine, other, factors):
+def lefts_of(owner, axis, mine, other, factors, after):
     blocks, depth, tokens = mine.shape
     shape = (depth // RING, blocks * tokens)
     return call(
         functools.partial(lefts_kernel, owner, axis),
         "lefts",
         [mine, other, *factors],
-        [],
+        after,
         [jax.ShapeDtypeStruct(shape, mine.dtype)] * RING,
         SMALL,
         10,
@@ -336,13 +337,13 @@
         [VMEM] * (RING - 1) + [ANY] * 2,
         [VMEM] + [ANY] * 2,
     )
-    hidden_blocks = [hidden, *near_hidden, shift(hidden, "x", 2)]
-    gate_blocks = [gate_grad, *near_gate, shift(gate_grad, "y", 2)]
+    far_hidden, far_gate = shift(hidden, "x", 2), shift(gate_grad, "y", 2)
+    near_hidden, near_gate = wide([hidden, *near_hidden]), wide([gate_grad, *near_gate])
     factors = [factor, mine_factors, swap(mine_factors, "core", 1)]
-    gate_lefts = lefts_of(1, "x", mine, other, factors)
-    down_lefts = lefts_of(0, "y", mine, other, factors)
-    down = ring_reduce(down_lefts, wide(hidden_blocks, []), "y")
-    gated = ring_reduce(gate_lefts, wide(gate_blocks, []), "x")
+    gate_lefts = lefts_of(1, "x", mine, other, factors, [near_hidden, near_gate])
+    down_lefts = lefts_of(0, "y", mine, other, factors, [gate_lefts[0]])
+    down = ring_reduce(down_lefts, wide([near_hidden, far_hidden]), "y")
+    gated = ring_reduce(gate_lefts, wide([near_gate, far_gate]), "x")
     return ((down / example_total).astype(jnp.bfloat16), (gated / example_total).astype(jnp.bfloat16))
 
 

time: 131 us -> 133 us (1.015)
  starting transfers between devices: 35.2 us -> 38.5 us
    ppermute x14, starting transfers between devices: 20.6 us -> 23.9 us  [shift(): lax.ppermute(value, axis, [(i, (i + step) % RING) for i in range(RING)])]
    ppermute x5, waiting for transfers between devices: 6.96 us -> 5.12 us  [swap(): lax.ppermute(value, axis, [(i, i ^ bit) for i in range(2 if axis == 'core...]
    pallas_call x9 -> x11, Pallas kernels: 15.5 us -> 15.5 us  [call(): pl.pallas_call(body, in_specs=(in_specs or [VMEM] * count) + [ANY] * len(...]
  transfers between devices with their start and end apart: 25 -> 25, of which waited for: 13 -> 14; matrix products, arithmetic and copies ran while one was open for 10% -> 10% of each run, Pallas kernels for 21% -> 20%
where the time goes in v4:
time: 133 us; the launch traced here: 132 us
  waiting for transfers between devices  44.1 us (33%)
  starting transfers between devices  38.5 us (29%)
  Pallas kernels  30.2 us (23%)
  matrix products  11.2 us (8%)
  other arithmetic  3.57 us (3%)
  local copies, waits for them, and re-layouts  3.49 us (3%)
    ppermute x14, waiting for transfers between devices, shift(): lax.ppermute(value, axis, [(i, (i + step) % RING) for i in range(RING)])  34 us
    ppermute x14, starting transfers between devices, shift(): lax.ppermute(value, axis, [(i, (i + step) % RING) for i in range(RING)])  23.9 us
    pallas_call x11, Pallas kernels, call(): pl.pallas_call(body, in_specs=(in_specs or [VMEM] * count) + [ANY] * len(...  15.5 us
    dot_general x8, matrix products, dot_last(): lax.dot_general(left, right, (((1,), (1,)), ((), ())), preferred_element_...  11.2 us
    pallas_call x1, Pallas kernels, hidden_and_gradient(): pl.pallas_call(gate_kernel, grid=(width // rows,), in_specs=[pl.BlockSpec...  10.8 us
    ppermute x6, starting transfers between devices, shift(): return lax.ppermute(value, ('x', 'y', 'core'), pairs)  8.64 us
    ppermute x5, starting transfers between devices, swap(): lax.ppermute(value, axis, [(i, i ^ bit) for i in range(2 if axis == 'core...  5.93 us
    ppermute x5, waiting for transfers between devices, swap(): lax.ppermute(value, axis, [(i, i ^ bit) for i in range(2 if axis == 'core...  5.12 us
  transfers between devices with their start and end apart: 25, of which 14 were waited for; matrix products, arithmetic and copies ran while one was open for 10% of the time, Pallas kernels for 20%

profile of v4, /device:TPU:0, one launch (start us, length us, event | category | flops | bytes accessed | tf_op | source)
XLA Modules:
  0.0 132.0 jit_solution(8006848035555636076)
XLA Ops:
  0.6 1.7 %copy-done = bf16[256,5120]{1,0:T(8,128)(2,1)S(1)} copy-done((bf16[256,5120]{1,0:T(8,128)(2,1)S(1)}, bf16[256,5120]{1,0:T(8,128)(2,1)}, u32[]{:S(2)}) %copy-start) | copy-done | bytes 2621464
  2.4 1.7 %copy-done.2 = bf16[256,5120]{1,0:T(8,128)(2,1)S(1)} copy-done((bf16[256,5120]{1,0:T(8,128)(2,1)S(1)}, bf16[256,5120]{1,0:T(8,128)(2,1)}, u32[]{:S(2)}) %copy-start.2) | copy-done | bytes 2621464
  4.1 2.6 %column_parts.1 = (bf16[1280,256]{1,0:T(8,128)(2,1)S(1)}, bf16[1280,256]{1,0:T(8,128)(2,1)}, bf16[1280,256]{1,0:T(8,128)(2,1)}, bf16[1280,256]{1,0:T(8,128)(2,1)}) custom-call(bf16[256,5120]{1,0:T(8,128)(2,1)S(1)} %copy-done, bf16[256,5120]{1,0:T(8,128)(2,1)S(1)} %copy-done.2), custom_call_target="tpu_custom_call" | custom-call | tf_op jit(solution)/shard_map/column_parts/pallas_call | solution.py:83
  6.7 1.6 %collective-permute-start = (bf16[1280,256]{1,0:T(8,128)(2,1)}, bf16[1280,256]{1,0:T(8,128)(2,1)}, u32[]{:S(2)}, u32[]{:S(2)}) collective-permute-start(bf16[1280,256]{1,0:T(8,128)(2,1)} %get-tuple-element.20), channel_id=1, source_target_pairs={{0,32},{1,9},{8,40},{9,17},{16,48},{17,25},{24,56},{25,1},{32,64},... | collective-permute-start | bytes 1966088 | tf_op jit(solution)/shard_map/ppermute | solution.py:40
  8.4 1.7 %collective-permute-start.1 = (bf16[1280,256]{1,0:T(8,128)(2,1)}, bf16[1280,256]{1,0:T(8,128)(2,1)}, u32[]{:S(2)}, u32[]{:S(2)}) collective-permute-start(bf16[1280,256]{1,0:T(8,128)(2,1)} %get-tuple-element.21), channel_id=1, source_target_pairs={{0,96},{1,25},{8,104},{9,1},{16,112},{17,9},{24,120},{25,17},{32,0... | collective-permute-start | bytes 1966088 | tf_op jit(solution)/shard_map/ppermute | solution.py:40
  10.1 1.9 %collective-permute-start.2 = (bf16[1280,256]{1,0:T(8,128)(2,1)}, bf16[1280,256]{1,0:T(8,128)(2,1)}, u32[]{:S(2)}, u32[]{:S(2)}) collective-permute-start(bf16[1280,256]{1,0:T(8,128)(2,1)} %get-tuple-element.22), channel_id=1, source_target_pairs={{0,64},{1,17},{8,72},{9,25},{16,80},{17,1},{24,88},{25,9},{32,96},... | collective-permute-start | bytes 1966088 | tf_op jit(solution)/shard_map/ppermute | solution.py:40
  11.9 10.8 %hidden_and_gradient.1 = (bf16[1728,256]{1,0:T(8,128)(2,1)}, bf16[1728,256]{1,0:T(8,128)(2,1)}) custom-call(bf16[1728,5120]{1,0:T(8,128)(2,1)} %bitcast.20, bf16[256,5120]{1,0:T(8,128)(2,1)} %refs_0_.3, bf16[1728,256]{1,0:T(8,128)(2,1)S(1)} %bitcast.19, bf16[1728,256]{1,0:T(8,128)(2,1)} %bitcast.21, bf16[1280,256]{1,0:T(8,128)(2,1)S(1)} %get-tuple-element.19.rest_0_.refs_0_), custom_call_target="tpu_custom_call" | custom-call | flops 999999995904 | bytes 1000000000 | tf_op jit(solution)/shard_map/hidden_and_gradient/pallas_call | solution.py:111
  23.3 2.6 %collective-permute-start.8 = (bf16[1728,256]{1,0:T(8,128)(2,1)}, bf16[1728,256]{1,0:T(8,128)(2,1)}, u32[]{:S(2)}, u32[]{:S(2)}) collective-permute-start(bf16[1728,256]{1,0:T(8,128)(2,1)} %get-tuple-element.24.refs_2_.refs_3_), channel_id=1, source_target_pairs={{0,96},{32,0},{64,32},{96,64},{1,97},{33,1},{65,33},{97,65},{2,98}... | collective-permute-start | bytes 2654216 | tf_op jit(solution)/shard_map/ppermute | solution.py:33
  26.0 1.6 %collective-permute-start.9 = (bf16[1728,256]{1,0:T(8,128)(2,1)}, bf16[1728,256]{1,0:T(8,128)(2,1)}, u32[]{:S(2)}, u32[]{:S(2)}) collective-permute-start(bf16[1728,256]{1,0:T(8,128)(2,1)} %get-tuple-element.23.refs_4_.refs_3_), channel_id=1, source_target_pairs={{0,8},{8,16},{16,24},{24,0},{1,9},{9,17},{17,25},{25,1},{2,10},{10... | collective-permute-start | bytes 2654216 | tf_op jit(solution)/shard_map/ppermute | solution.py:33
  27.6 1.7 %collective-permute-start.10 = (bf16[1728,256]{1,0:T(8,128)(2,1)}, bf16[1728,256]{1,0:T(8,128)(2,1)}, u32[]{:S(2)}, u32[]{:S(2)}) collective-permute-start(bf16[1728,256]{1,0:T(8,128)(2,1)} %get-tuple-element.23.refs_4_.refs_3_), channel_id=1, source_target_pairs={{0,24},{8,0},{16,8},{24,16},{1,25},{9,1},{17,9},{25,17},{2,26},{10... | collective-permute-start | bytes 2654216 | tf_op jit(solution)/shard_map/ppermute | solution.py:33
  29.2 4.0 %stack.1.refs_0_ = bf16[4,1280,256]{2,1,0:T(8,128)(2,1)} custom-call(bf16[1280,256]{1,0:T(8,128)(2,1)S(1)} %get-tuple-element.19.rest_0_.refs_0_, bf16[1280,256]{1,0:T(8,128)(2,1)} %collective-permute-done.refs_1_.refs_4_, bf16[1280,256]{1,0:T(8,128)(2,1)} %collective-permute-done.1.refs_2_.refs_5_, ...), custom_call_target="tpu_custom_call" | custom-call | tf_op jit(solution)/shard_map/stack/pallas_call | solution.py:174
  33.2 3.6 %squares.1.refs_0_ = f32[8,128]{1,0:T(8,128)S(1)} custom-call(bf16[256,5120]{1,0:T(8,128)(2,1)S(1)} %copy-done.1, bf16[256,5120]{1,0:T(8,128)(2,1)S(1)} %copy-done.3, bf16[1728,256]{1,0:T(8,128)(2,1)} %get-tuple-element.24.refs_2_.refs_3_, bf16[1728,256]{1,0:T(8,128)(2,1)} %get-tuple-element.23.refs_4_.refs_3_, ...), custom_call_target="tpu_custom_call" | custom-call | flops 999999995904 | bytes 1000000000 | tf_op jit(solution)/shard_map/squares/pallas_call | solution.py:83
  36.9 1.6 %collective-permute-done.3.refs_1_ = bf16[4,1280,256]{2,1,0:T(8,128)(2,1)} collective-permute-done((bf16[4,1280,256]{2,1,0:T(8,128)(2,1)}, bf16[4,1280,256]{2,1,0:T(8,128)(2,1)}, u32[]{:S(2)}, u32[]{:S(2)}) %collective-permute-start.3) | collective-permute-done | bytes 2621472 | tf_op jit(solution)/shard_map/ppermute | solution.py:44
  38.6 1.0 collective-permute-done.4
  39.6 1.9 %collective-permute-start.5 = (f32[8,128]{1,0:T(8,128)S(1)}, f32[8,128]{1,0:T(8,128)S(1)}, u32[]{:S(2)}, u32[]{:S(2)}) collective-permute-start(f32[8,128]{1,0:T(8,128)S(1)} %add.42), channel_id=1, source_target_pairs={{0,2},{2,0},{4,6},{6,4},{1,3},{3,1},{5,7},{7,5},{8,10},{10,8},{12,... | collective-permute-start | bytes 12296 | tf_op jit(solution)/shard_map/ppermute | solution.py:44
  41.5 1.7 %collective-permute-done.5 = f32[8,128]{1,0:T(8,128)S(1)} collective-permute-done((f32[8,128]{1,0:T(8,128)S(1)}, f32[8,128]{1,0:T(8,128)S(1)}, u32[]{:S(2)}, u32[]{:S(2)}) %collective-permute-start.5) | collective-permute-done | bytes 4128 | tf_op jit(solution)/shard_map/ppermute | solution.py:44
  43.2 3.9 %collective-permute-start.6 = (f32[8,128]{1,0:T(8,128)S(1)}, f32[8,128]{1,0:T(8,128)S(1)}, u32[]{:S(2)}, u32[]{:S(2)}) collective-permute-start(f32[8,128]{1,0:T(8,128)S(1)} %add.43.refs_0_), channel_id=1, source_target_pairs={{0,4},{2,6},{4,0},{6,2},{1,5},{3,7},{5,1},{7,3},{8,12},{10,14},{12... | collective-permute-start | bytes 12296 | tf_op jit(solution)/shard_map/ppermute | solution.py:44
  47.1 0.8 collective-permute-done.9.refs_5_.refs_1_
  47.9 0.8 collective-permute-done.6.refs_1_
  49.5 3.1 %collective-permute-start.12 = (f32[8,128]{1,0:T(8,128)S(1)}, f32[8,128]{1,0:T(8,128)S(1)}, u32[]{:S(2)}, u32[]{:S(2)}) collective-permute-start(f32[8,128]{1,0:T(8,128)S(1)} %factor.1.refs_2_), channel_id=1, source_target_pairs={{0,96},{1,25},{8,104},{9,1},{16,112},{17,9},{24,120},{25,17},{32,0... | collective-permute-start | bytes 12296 | tf_op jit(solution)/shard_map/ppermute | solution.py:40
  52.7 1.4 %collective-permute-done.11.refs_0_ = f32[8,128]{1,0:T(8,128)S(1)} collective-permute-done((f32[8,128]{1,0:T(8,128)S(1)}, f32[8,128]{1,0:T(8,128)S(1)}, u32[]{:S(2)}, u32[]{:S(2)}) %collective-permute-start.11) | collective-permute-done | bytes 4128 | tf_op jit(solution)/shard_map/ppermute | solution.py:40
  54.1 3.5 %collective-permute-done.13.refs_2_ = f32[8,128]{1,0:T(8,128)S(1)} collective-permute-done((f32[8,128]{1,0:T(8,128)S(1)}, f32[8,128]{1,0:T(8,128)S(1)}, u32[]{:S(2)}, u32[]{:S(2)}) %collective-permute-start.13) | collective-permute-done | bytes 4128 | tf_op jit(solution)/shard_map/ppermute | solution.py:40
  57.8 2.8 %collective-permute-start.20 = (bf16[1728,256]{1,0:T(8,128)(2,1)}, bf16[1728,256]{1,0:T(8,128)(2,1)S(1)}, u32[]{:S(2)}, u32[]{:S(2)}) collective-permute-start(bf16[1728,256]{1,0:T(8,128)(2,1)} %get-tuple-element.27.refs_0_), channel_id=1, source_target_pairs={{0,16},{8,24},{16,0},{24,8},{1,17},{9,25},{17,1},{25,9},{2,18},{10... | collective-permute-start | bytes 2654216 | tf_op jit(solution)/shard_map/ppermute | solution.py:33
  60.6 1.9 %wide.4.refs_5_.refs_0_ = bf16[1728,768]{1,0:T(8,128)(2,1)S(1)} custom-call(bf16[1728,256]{1,0:T(8,128)(2,1)} %get-tuple-element.26.refs_0_, bf16[1728,256]{1,0:T(8,128)(2,1)} %collective-permute-done.7.refs_3_.refs_1_, bf16[1728,256]{1,0:T(8,128)(2,1)} %collective-permute-done.8.refs_4_.refs_2_), custom_call_target="tpu_custom_call" | custom-call | tf_op jit(solution)/shard_map/wide/pallas_call | solution.py:83
  62.4 1.9 %wide.5.refs_6_.refs_0_ = bf16[1728,768]{1,0:T(8,128)(2,1)S(1)} custom-call(bf16[1728,256]{1,0:T(8,128)(2,1)} %get-tuple-element.27.refs_0_, bf16[1728,256]{1,0:T(8,128)(2,1)} %collective-permute-done.9.refs_5_.refs_1_, bf16[1728,256]{1,0:T(8,128)(2,1)} %collective-permute-done.10.refs_6_.refs_2_), custom_call_target="tpu_custom_call" | custom-call | tf_op jit(solution)/shard_map/wide/pallas_call | solution.py:83
  64.3 2.2 %lefts.2 = (bf16[320,1024]{1,0:T(8,128)(2,1)S(1)}, bf16[320,1024]{1,0:T(8,128)(2,1)S(1)}, bf16[320,1024]{1,0:T(8,128)(2,1)S(1)}, bf16[320,1024]{1,0:T(8,128)(2,1)S(1)}) custom-call(bf16[4,1280,256]{2,1,0:T(8,128)(2,1)} %stack.1.refs_0_, bf16[4,1280,256]{2,1,0:T(8,128)(2,1)} %collective-permute-done.3.refs_1_, f32[8,128]{1,0:T(8,128)S(1)} %factor.1.refs_2_, ...), custom_call_target="tpu_custom_call" | custom-call | tf_op jit(solution)/shard_map/lefts/pallas_call | solution.py:83
  66.5 2.2 %lefts.3 = (bf16[320,1024]{1,0:T(8,128)(2,1)S(1)}, bf16[320,1024]{1,0:T(8,128)(2,1)S(1)}, bf16[320,1024]{1,0:T(8,128)(2,1)S(1)}, bf16[320,1024]{1,0:T(8,128)(2,1)S(1)}) custom-call(bf16[4,1280,256]{2,1,0:T(8,128)(2,1)} %stack.1.refs_0_, bf16[4,1280,256]{2,1,0:T(8,128)(2,1)} %collective-permute-done.3.refs_1_, f32[8,128]{1,0:T(8,128)S(1)} %factor.1.refs_2_, ...), custom_call_target="tpu_custom_call" | custom-call | tf_op jit(solution)/shard_map/lefts/pallas_call | solution.py:83
  68.7 9.2 %collective-permute-done.15.refs_1_ = bf16[1728,256]{1,0:T(8,128)(2,1)S(1)} collective-permute-done((bf16[1728,256]{1,0:T(8,128)(2,1)}, bf16[1728,256]{1,0:T(8,128)(2,1)S(1)}, u32[]{:S(2)}, u32[]{:S(2)}) %collective-permute-start.15) | collective-permute-done | bytes 884768 | tf_op jit(solution)/shard_map/ppermute | solution.py:33
  78.2 1.4 %convolution_convert_fusion.4 = bf16[320,1728]{1,0:T(8,128)(2,1)S(1)} fusion(bf16[320,1024]{1,0:T(8,128)(2,1)S(1)} %get-tuple-element.32, bf16[1728,1024]{1,0:T(8,128)(2,1)S(1)} %wide.6), kind=kOutput, calls=%fused_computation.4 | convolution fusion | flops 1133015040 | bytes 5300224 | tf_op jit(solution)/shard_map/dot_general | solution.py:48
  79.7 1.4 %convolution_convert_fusion.6 = bf16[320,1728]{1,0:T(8,128)(2,1)S(1)} fusion(bf16[320,1024]{1,0:T(8,128)(2,1)S(1)} %get-tuple-element.30, bf16[1728,1024]{1,0:T(8,128)(2,1)S(1)} %wide.6), kind=kOutput, calls=%fused_computation.6 | convolution fusion | flops 1133015040 | bytes 5300224 | tf_op jit(solution)/shard_map/dot_general | solution.py:48
  81.1 3.3 %collective-permute-start.16 = (bf16[320,1728]{1,0:T(8,128)(2,1)S(1)}, bf16[320,1728]{1,0:T(8,128)(2,1)S(1)}, u32[]{:S(2)}, u32[]{:S(2)}) collective-permute-start(bf16[320,1728]{1,0:T(8,128)(2,1)S(1)} %convolution_convert_fusion.6), channel_id=1, source_target_pairs={{0,24},{8,0},{16,8},{24,16},{1,25},{9,1},{17,9},{25,17},{2,26},{10... | collective-permute-start | bytes 3317768 | tf_op jit(solution)/shard_map/ppermute | solution.py:33
  84.7 1.4 %convolution_convert_fusion = bf16[320,1728]{1,0:T(8,128)(2,1)S(1)} fusion(bf16[320,1024]{1,0:T(8,128)(2,1)S(1)} %get-tuple-element.28.refs_5_, bf16[1728,1024]{1,0:T(8,128)(2,1)S(1)} %wide.7), kind=kOutput, calls=%fused_computation | convolution fusion | flops 1133015040 | bytes 5300224 | tf_op jit(solution)/shard_map/dot_general | solution.py:48
  86.1 2.5 %collective-permute-start.22 = (bf16[320,1728]{1,0:T(8,128)(2,1)S(1)}, bf16[320,1728]{1,0:T(8,128)(2,1)S(1)}, u32[]{:S(2)}, u32[]{:S(2)}) collective-permute-start(bf16[320,1728]{1,0:T(8,128)(2,1)S(1)} %convolution_convert_fusion), channel_id=1, source_target_pairs={{0,32},{32,64},{64,96},{96,0},{1,33},{33,65},{65,97},{97,1},{2,34}... | collective-permute-start | bytes 3317768 | tf_op jit(solution)/shard_map/ppermute | solution.py:33
  88.6 1.4 %convolution_convert_fusion.2 = bf16[320,1728]{1,0:T(8,128)(2,1)S(1)} fusion(bf16[320,1024]{1,0:T(8,128)(2,1)S(1)} %get-tuple-element.34, bf16[1728,1024]{1,0:T(8,128)(2,1)S(1)} %wide.7), kind=kOutput, calls=%fused_computation.2 | convolution fusion | flops 1133015040 | bytes 5300224 | tf_op jit(solution)/shard_map/dot_general | solution.py:48
  90.0 1.4 %collective-permute-start.21 = (bf16[320,1728]{1,0:T(8,128)(2,1)S(1)}, bf16[320,1728]{1,0:T(8,128)(2,1)S(1)}, u32[]{:S(2)}, u32[]{:S(2)}) collective-permute-start(bf16[320,1728]{1,0:T(8,128)(2,1)S(1)} %convolution_convert_fusion.2), channel_id=1, source_target_pairs={{0,96},{32,0},{64,32},{96,64},{1,97},{33,1},{65,33},{97,65},{2,98}... | collective-permute-start | bytes 3317768 | tf_op jit(solution)/shard_map/ppermute | solution.py:33
  91.4 1.4 %convolution_convert_fusion.5 = bf16[320,1728]{1,0:T(8,128)(2,1)S(1)} fusion(bf16[320,1024]{1,0:T(8,128)(2,1)S(1)} %get-tuple-element.31, bf16[1728,1024]{1,0:T(8,128)(2,1)S(1)} %wide.6), kind=kOutput, calls=%fused_computation.5 | convolution fusion | flops 1133015040 | bytes 5300224 | tf_op jit(solution)/shard_map/dot_general | solution.py:48
  92.8 1.4 %convolution_convert_fusion.7 = bf16[320,1728]{1,0:T(8,128)(2,1)S(1)} fusion(bf16[320,1024]{1,0:T(8,128)(2,1)S(1)} %get-tuple-element.29, bf16[1728,1024]{1,0:T(8,128)(2,1)S(1)} %wide.6), kind=kOutput, calls=%fused_computation.7 | convolution fusion | flops 1133015040 | bytes 5300224 | tf_op jit(solution)/shard_map/dot_general | solution.py:48
  94.2 1.4 %convolution_convert_fusion.1 = bf16[320,1728]{1,0:T(8,128)(2,1)S(1)} fusion(bf16[320,1024]{1,0:T(8,128)(2,1)S(1)} %get-tuple-element.35, bf16[1728,1024]{1,0:T(8,128)(2,1)S(1)} %wide.7), kind=kOutput, calls=%fused_computation.1 | convolution fusion | flops 1133015040 | bytes 5300224 | tf_op jit(solution)/shard_map/dot_general | solution.py:48
  95.6 11.1 %collective-permute-done.17 = bf16[320,1728]{1,0:T(8,128)(2,1)S(1)} collective-permute-done((bf16[320,1728]{1,0:T(8,128)(2,1)S(1)}, bf16[320,1728]{1,0:T(8,128)(2,1)S(1)}, u32[]{:S(2)}, u32[]{:S(2)}) %collective-permute-start.17) | collective-permute-done | bytes 1105952 | tf_op jit(solution)/shard_map/ppermute | solution.py:33
  107.8 4.0 %collective-permute-start.19 = (bf16[160,1728]{1,0:T(8,128)(2,1)S(1)}, bf16[160,1728]{1,0:T(8,128)(2,1)S(1)}, u32[]{:S(2)}, u32[]{:S(2)}) collective-permute-start(bf16[160,1728]{1,0:T(8,128)(2,1)S(1)} %get-tuple-element.43), channel_id=1, source_target_pairs={{0,24},{8,0},{16,8},{24,16},{1,25},{9,1},{17,9},{25,17},{2,26},{10... | collective-permute-start | bytes 1658888 | tf_op jit(solution)/shard_map/ppermute | solution.py:33
  111.8 1.4 %convolution_convert_fusion.3 = bf16[320,1728]{1,0:T(8,128)(2,1)S(1)} fusion(bf16[320,1024]{1,0:T(8,128)(2,1)S(1)} %get-tuple-element.33, bf16[1728,1024]{1,0:T(8,128)(2,1)S(1)} %wide.7), kind=kOutput, calls=%fused_computation.3 | convolution fusion | flops 1133015040 | bytes 5300224 | tf_op jit(solution)/shard_map/dot_general | solution.py:48
  113.2 0.8 collective-permute-done.22
  114.1 2.0 %collective-permute-done.21 = bf16[320,1728]{1,0:T(8,128)(2,1)S(1)} collective-permute-done((bf16[320,1728]{1,0:T(8,128)(2,1)S(1)}, bf16[320,1728]{1,0:T(8,128)(2,1)S(1)}, u32[]{:S(2)}, u32[]{:S(2)}) %collective-permute-start.21) | collective-permute-done | bytes 1105952 | tf_op jit(solution)/shard_map/ppermute | solution.py:33
  117.0 2.6 %collective-permute-start.24 = (bf16[160,1728]{1,0:T(8,128)(2,1)S(1)}, bf16[160,1728]{1,0:T(8,128)(2,1)S(1)}, u32[]{:S(2)}, u32[]{:S(2)}) collective-permute-start(bf16[160,1728]{1,0:T(8,128)(2,1)S(1)} %get-tuple-element.39), channel_id=1, source_target_pairs={{0,96},{32,0},{64,32},{96,64},{1,97},{33,1},{65,33},{97,65},{2,98}... | collective-permute-start | bytes 1658888 | tf_op jit(solution)/shard_map/ppermute | solution.py:33
  119.7 2.4 %collective-permute-done.18 = bf16[160,1728]{1,0:T(8,128)(2,1)S(1)} collective-permute-done((bf16[160,1728]{1,0:T(8,128)(2,1)S(1)}, bf16[160,1728]{1,0:T(8,128)(2,1)S(1)}, u32[]{:S(2)}, u32[]{:S(2)}) %collective-permute-start.18) | collective-permute-done | bytes 552992 | tf_op jit(solution)/shard_map/ppermute | solution.py:33
  122.5 1.1 fusion
  123.6 6.8 %collective-permute-done.23 = bf16[160,1728]{1,0:T(8,128)(2,1)S(1)} collective-permute-done((bf16[160,1728]{1,0:T(8,128)(2,1)S(1)}, bf16[160,1728]{1,0:T(8,128)(2,1)S(1)}, u32[]{:S(2)}, u32[]{:S(2)}) %collective-permute-start.23) | collective-permute-done | bytes 552992 | tf_op jit(solution)/shard_map/ppermute | solution.py:33
  130.8 1.1 fusion.1
  (43 shorter events, 5.3 us)
Async XLA Ops:
  0.6 1.7 %copy-start = (bf16[256,5120]{1,0:T(8,128)(2,1)S(1)}, bf16[256,5120]{1,0:T(8,128)(2,1)}, u32[]{:S(2)}) copy-start(bf16[256,5120]{1,0:T(8,128)(2,1)} %refs_0_.3) | copy-start | bytes 7864324
  2.4 1.7 %copy-start.2 = (bf16[256,5120]{1,0:T(8,128)(2,1)S(1)}, bf16[256,5120]{1,0:T(8,128)(2,1)}, u32[]{:S(2)}) copy-start(bf16[256,5120]{1,0:T(8,128)(2,1)} %refs_1_.3) | copy-start | bytes 7864324
  4.1 7.8 %copy-start.5 = (bf16[256,1728]{0,1:T(8,128)(2,1)S(1)}, bf16[256,1728]{0,1:T(8,128)(2,1)}, u32[]{:S(2)}) copy-start(bf16[256,1728]{0,1:T(8,128)(2,1)} %param.8) | copy-start | bytes 2654212
  6.7 19.2 %collective-permute-start = (bf16[1280,256]{1,0:T(8,128)(2,1)}, bf16[1280,256]{1,0:T(8,128)(2,1)}, u32[]{:S(2)}, u32[]{:S(2)}) collective-permute-start(bf16[1280,256]{1,0:T(8,128)(2,1)} %get-tuple-element.20), channel_id=1, source_target_pairs={{0,32},{1,9},{8,40},{9,17},{16,48},{17,25},{24,56},{25,1},{32,64},... | collective-permute-start | bytes 1966088 | tf_op jit(solution)/shard_map/ppermute | solution.py:40
  8.4 19.2 %collective-permute-start.1 = (bf16[1280,256]{1,0:T(8,128)(2,1)}, bf16[1280,256]{1,0:T(8,128)(2,1)}, u32[]{:S(2)}, u32[]{:S(2)}) collective-permute-start(bf16[1280,256]{1,0:T(8,128)(2,1)} %get-tuple-element.21), channel_id=1, source_target_pairs={{0,96},{1,25},{8,104},{9,1},{16,112},{17,9},{24,120},{25,17},{32,0... | collective-permute-start | bytes 1966088 | tf_op jit(solution)/shard_map/ppermute | solution.py:40
  10.1 19.2 %collective-permute-start.2 = (bf16[1280,256]{1,0:T(8,128)(2,1)}, bf16[1280,256]{1,0:T(8,128)(2,1)}, u32[]{:S(2)}, u32[]{:S(2)}) collective-permute-start(bf16[1280,256]{1,0:T(8,128)(2,1)} %get-tuple-element.22), channel_id=1, source_target_pairs={{0,64},{1,17},{8,72},{9,25},{16,80},{17,1},{24,88},{25,9},{32,96},... | collective-permute-start | bytes 1966088 | tf_op jit(solution)/shard_map/ppermute | solution.py:40
  22.7 24.4 %collective-permute-start.7 = (bf16[1728,256]{1,0:T(8,128)(2,1)}, bf16[1728,256]{1,0:T(8,128)(2,1)}, u32[]{:S(2)}, u32[]{:S(2)}) collective-permute-start(bf16[1728,256]{1,0:T(8,128)(2,1)} %get-tuple-element.24.refs_2_.refs_3_), channel_id=1, source_target_pairs={{0,32},{32,64},{64,96},{96,0},{1,33},{33,65},{65,97},{97,1},{2,34}... | collective-permute-start | bytes 2654216 | tf_op jit(solution)/shard_map/ppermute | solution.py:33
  23.3 23.8 %collective-permute-start.8 = (bf16[1728,256]{1,0:T(8,128)(2,1)}, bf16[1728,256]{1,0:T(8,128)(2,1)}, u32[]{:S(2)}, u32[]{:S(2)}) collective-permute-start(bf16[1728,256]{1,0:T(8,128)(2,1)} %get-tuple-element.24.refs_2_.refs_3_), channel_id=1, source_target_pairs={{0,96},{32,0},{64,32},{96,64},{1,97},{33,1},{65,33},{97,65},{2,98}... | collective-permute-start | bytes 2654216 | tf_op jit(solution)/shard_map/ppermute | solution.py:33
  26.0 7.2 %copy-start.1 = (bf16[256,5120]{1,0:T(8,128)(2,1)S(1)}, bf16[256,5120]{1,0:T(8,128)(2,1)}, u32[]{:S(2)}) copy-start(bf16[256,5120]{1,0:T(8,128)(2,1)} %refs_0_.3) | copy-start | bytes 7864324
  26.0 7.2 %copy-start.3 = (bf16[256,5120]{1,0:T(8,128)(2,1)S(1)}, bf16[256,5120]{1,0:T(8,128)(2,1)}, u32[]{:S(2)}) copy-start(bf16[256,5120]{1,0:T(8,128)(2,1)} %refs_1_.3) | copy-start | bytes 7864324
  26.0 21.9 %collective-permute-start.9 = (bf16[1728,256]{1,0:T(8,128)(2,1)}, bf16[1728,256]{1,0:T(8,128)(2,1)}, u32[]{:S(2)}, u32[]{:S(2)}) collective-permute-start(bf16[1728,256]{1,0:T(8,128)(2,1)} %get-tuple-element.23.refs_4_.refs_3_), channel_id=1, source_target_pairs={{0,8},{8,16},{16,24},{24,0},{1,9},{9,17},{17,25},{25,1},{2,10},{10... | collective-permute-start | bytes 2654216 | tf_op jit(solution)/shard_map/ppermute | solution.py:33
  27.6 20.3 %collective-permute-start.10 = (bf16[1728,256]{1,0:T(8,128)(2,1)}, bf16[1728,256]{1,0:T(8,128)(2,1)}, u32[]{:S(2)}, u32[]{:S(2)}) collective-permute-start(bf16[1728,256]{1,0:T(8,128)(2,1)} %get-tuple-element.23.refs_4_.refs_3_), channel_id=1, source_target_pairs={{0,24},{8,0},{16,8},{24,16},{1,25},{9,1},{17,9},{25,17},{2,26},{10... | collective-permute-start | bytes 2654216 | tf_op jit(solution)/shard_map/ppermute | solution.py:33
  33.2 5.3 %collective-permute-start.3 = (bf16[4,1280,256]{2,1,0:T(8,128)(2,1)}, bf16[4,1280,256]{2,1,0:T(8,128)(2,1)}, u32[]{:S(2)}, u32[]{:S(2)}) collective-permute-start(bf16[4,1280,256]{2,1,0:T(8,128)(2,1)} %stack.1.refs_0_), channel_id=1, source_target_pairs={{0,1},{1,0},{2,3},{3,2},{4,5},{5,4},{6,7},{7,6},{8,9},{9,8},{10,11... | collective-permute-start | bytes 7864328 | tf_op jit(solution)/shard_map/ppermute | solution.py:44
  36.8 11.9 %copy-start.4 = (f32[2]{0:T(128)S(1)}, f32[2]{0:T(128)}, u32[]{:S(2)}) copy-start(f32[2]{0:T(128)} %refs_2_.1) | copy-start | bytes 28
  38.4 1.2 collective-permute-start.4
  39.6 3.6 %collective-permute-start.5 = (f32[8,128]{1,0:T(8,128)S(1)}, f32[8,128]{1,0:T(8,128)S(1)}, u32[]{:S(2)}, u32[]{:S(2)}) collective-permute-start(f32[8,128]{1,0:T(8,128)S(1)} %add.42), channel_id=1, source_target_pairs={{0,2},{2,0},{4,6},{6,4},{1,3},{3,1},{5,7},{7,5},{8,10},{10,8},{12,... | collective-permute-start | bytes 12296 | tf_op jit(solution)/shard_map/ppermute | solution.py:44
  43.2 5.5 %collective-permute-start.6 = (f32[8,128]{1,0:T(8,128)S(1)}, f32[8,128]{1,0:T(8,128)S(1)}, u32[]{:S(2)}, u32[]{:S(2)}) collective-permute-start(f32[8,128]{1,0:T(8,128)S(1)} %add.43.refs_0_), channel_id=1, source_target_pairs={{0,4},{2,6},{4,0},{6,2},{1,5},{3,7},{5,1},{7,3},{8,12},{10,14},{12... | collective-permute-start | bytes 12296 | tf_op jit(solution)/shard_map/ppermute | solution.py:44
  49.2 4.9 %collective-permute-start.11 = (f32[8,128]{1,0:T(8,128)S(1)}, f32[8,128]{1,0:T(8,128)S(1)}, u32[]{:S(2)}, u32[]{:S(2)}) collective-permute-start(f32[8,128]{1,0:T(8,128)S(1)} %factor.1.refs_2_), channel_id=1, source_target_pairs={{0,32},{1,9},{8,40},{9,17},{16,48},{17,25},{24,56},{25,1},{32,64},... | collective-permute-start | bytes 12296 | tf_op jit(solution)/shard_map/ppermute | solution.py:40
  49.5 4.6 %collective-permute-start.12 = (f32[8,128]{1,0:T(8,128)S(1)}, f32[8,128]{1,0:T(8,128)S(1)}, u32[]{:S(2)}, u32[]{:S(2)}) collective-permute-start(f32[8,128]{1,0:T(8,128)S(1)} %factor.1.refs_2_), channel_id=1, source_target_pairs={{0,96},{1,25},{8,104},{9,1},{16,112},{17,9},{24,120},{25,17},{32,0... | collective-permute-start | bytes 12296 | tf_op jit(solution)/shard_map/ppermute | solution.py:40
  52.6 5.1 %collective-permute-start.13 = (f32[8,128]{1,0:T(8,128)S(1)}, f32[8,128]{1,0:T(8,128)S(1)}, u32[]{:S(2)}, u32[]{:S(2)}) collective-permute-start(f32[8,128]{1,0:T(8,128)S(1)} %factor.1.refs_2_), channel_id=1, source_target_pairs={{0,64},{1,17},{8,72},{9,25},{16,80},{17,1},{24,88},{25,9},{32,96},... | collective-permute-start | bytes 12296 | tf_op jit(solution)/shard_map/ppermute | solution.py:40
  57.7 20.3 %collective-permute-start.15 = (bf16[1728,256]{1,0:T(8,128)(2,1)}, bf16[1728,256]{1,0:T(8,128)(2,1)S(1)}, u32[]{:S(2)}, u32[]{:S(2)}) collective-permute-start(bf16[1728,256]{1,0:T(8,128)(2,1)} %get-tuple-element.26.refs_0_), channel_id=1, source_target_pairs={{0,64},{32,96},{64,0},{96,32},{1,65},{33,97},{65,1},{97,33},{2,66}... | collective-permute-start | bytes 2654216 | tf_op jit(solution)/shard_map/ppermute | solution.py:33
  57.8 26.6 %collective-permute-start.20 = (bf16[1728,256]{1,0:T(8,128)(2,1)}, bf16[1728,256]{1,0:T(8,128)(2,1)S(1)}, u32[]{:S(2)}, u32[]{:S(2)}) collective-permute-start(bf16[1728,256]{1,0:T(8,128)(2,1)} %get-tuple-element.27.refs_0_), channel_id=1, source_target_pairs={{0,16},{8,24},{16,0},{24,8},{1,17},{9,25},{17,1},{25,9},{2,18},{10... | collective-permute-start | bytes 2654216 | tf_op jit(solution)/shard_map/ppermute | solution.py:33
  60.6 3.8 %collective-permute-start.14 = (f32[3,8,128]{2,1,0:T(8,128)S(1)}, f32[3,8,128]{2,1,0:T(8,128)S(1)}, u32[]{:S(2)}, u32[]{:S(2)}) collective-permute-start(f32[3,8,128]{2,1,0:T(8,128)S(1)} %get-tuple-element.25.refs_3_), channel_id=1, source_target_pairs={{0,1},{1,0},{2,3},{3,2},{4,5},{5,4},{6,7},{7,6},{8,9},{9,8},{10,11... | collective-permute-start | bytes 36872 | tf_op jit(solution)/shard_map/ppermute | solution.py:44
  79.6 27.1 %collective-permute-start.17 = (bf16[320,1728]{1,0:T(8,128)(2,1)S(1)}, bf16[320,1728]{1,0:T(8,128)(2,1)S(1)}, u32[]{:S(2)}, u32[]{:S(2)}) collective-permute-start(bf16[320,1728]{1,0:T(8,128)(2,1)S(1)} %convolution_convert_fusion.4), channel_id=1, source_target_pairs={{0,8},{8,16},{16,24},{24,0},{1,9},{9,17},{17,25},{25,1},{2,10},{10... | collective-permute-start | bytes 3317768 | tf_op jit(solution)/shard_map/ppermute | solution.py:33
  81.1 26.3 %collective-permute-start.16 = (bf16[320,1728]{1,0:T(8,128)(2,1)S(1)}, bf16[320,1728]{1,0:T(8,128)(2,1)S(1)}, u32[]{:S(2)}, u32[]{:S(2)}) collective-permute-start(bf16[320,1728]{1,0:T(8,128)(2,1)S(1)} %convolution_convert_fusion.6), channel_id=1, source_target_pairs={{0,24},{8,0},{16,8},{24,16},{1,25},{9,1},{17,9},{25,17},{2,26},{10... | collective-permute-start | bytes 3317768 | tf_op jit(solution)/shard_map/ppermute | solution.py:33
  86.1 27.9 %collective-permute-start.22 = (bf16[320,1728]{1,0:T(8,128)(2,1)S(1)}, bf16[320,1728]{1,0:T(8,128)(2,1)S(1)}, u32[]{:S(2)}, u32[]{:S(2)}) collective-permute-start(bf16[320,1728]{1,0:T(8,128)(2,1)S(1)} %convolution_convert_fusion), channel_id=1, source_target_pairs={{0,32},{32,64},{64,96},{96,0},{1,33},{33,65},{65,97},{97,1},{2,34}... | collective-permute-start | bytes 3317768 | tf_op jit(solution)/shard_map/ppermute | solution.py:33
  90.0 26.1 %collective-permute-start.21 = (bf16[320,1728]{1,0:T(8,128)(2,1)S(1)}, bf16[320,1728]{1,0:T(8,128)(2,1)S(1)}, u32[]{:S(2)}, u32[]{:S(2)}) collective-permute-start(bf16[320,1728]{1,0:T(8,128)(2,1)S(1)} %convolution_convert_fusion.2), channel_id=1, source_target_pairs={{0,96},{32,0},{64,32},{96,64},{1,97},{33,1},{65,33},{97,65},{2,98}... | collective-permute-start | bytes 3317768 | tf_op jit(solution)/shard_map/ppermute | solution.py:33
  107.8 14.3 %collective-permute-start.18 = (bf16[160,1728]{1,0:T(8,128)(2,1)S(1)}, bf16[160,1728]{1,0:T(8,128)(2,1)S(1)}, u32[]{:S(2)}, u32[]{:S(2)}) collective-permute-start(bf16[160,1728]{1,0:T(8,128)(2,1)S(1)} %get-tuple-element.42), channel_id=1, source_target_pairs={{0,8},{8,16},{16,24},{24,0},{1,9},{9,17},{17,25},{25,1},{2,10},{10... | collective-permute-start | bytes 1658888 | tf_op jit(solution)/shard_map/ppermute | solution.py:33
  107.8 14.3 %collective-permute-start.19 = (bf16[160,1728]{1,0:T(8,128)(2,1)S(1)}, bf16[160,1728]{1,0:T(8,128)(2,1)S(1)}, u32[]{:S(2)}, u32[]{:S(2)}) collective-permute-start(bf16[160,1728]{1,0:T(8,128)(2,1)S(1)} %get-tuple-element.43), channel_id=1, source_target_pairs={{0,24},{8,0},{16,8},{24,16},{1,25},{9,1},{17,9},{25,17},{2,26},{10... | collective-permute-start | bytes 1658888 | tf_op jit(solution)/shard_map/ppermute | solution.py:33
  116.4 14.1 %collective-permute-start.23 = (bf16[160,1728]{1,0:T(8,128)(2,1)S(1)}, bf16[160,1728]{1,0:T(8,128)(2,1)S(1)}, u32[]{:S(2)}, u32[]{:S(2)}) collective-permute-start(bf16[160,1728]{1,0:T(8,128)(2,1)S(1)} %get-tuple-element.38), channel_id=1, source_target_pairs={{0,32},{32,64},{64,96},{96,0},{1,33},{33,65},{65,97},{97,1},{2,34}... | collective-permute-start | bytes 1658888 | tf_op jit(solution)/shard_map/ppermute | solution.py:33
  117.0 13.4 %collective-permute-start.24 = (bf16[160,1728]{1,0:T(8,128)(2,1)S(1)}, bf16[160,1728]{1,0:T(8,128)(2,1)S(1)}, u32[]{:S(2)}, u32[]{:S(2)}) collective-permute-start(bf16[160,1728]{1,0:T(8,128)(2,1)S(1)} %get-tuple-element.39), channel_id=1, source_target_pairs={{0,96},{32,0},{64,32},{96,64},{1,97},{33,1},{65,33},{97,65},{2,98}... | collective-permute-start | bytes 1658888 | tf_op jit(solution)/shard_map/ppermute | solution.py:33

commit v5 on v3

--- a/solution.py
+++ b/solution.py
@@ -139,7 +139,18 @@
 
 def pack_kernel(*refs):
     for at in range(RING - 1):
-        refs[RING + 1][at] = refs[at][...]
+        refs[RING - 1][at] = refs[at][...]
+
+
+def held_kernel(*refs):
+    pass
+
+
+def held_back(values, after):
+    count = len(values)
+    shapes = [jax.ShapeDtypeStruct(v.shape, v.dtype) for v in values]
+    aliases = {at: at for at in range(count)}
+    return call(held_kernel, "held_back", values, after, shapes, SMALL, 1, (), aliases, [ANY] * count, [ANY] * count)
 
 
 def factor_kernel(unit, *refs):
@@ -320,21 +331,10 @@
         1,
         in_specs=[VMEM] * 2 + [SMEM],
     )
-    mine_factors, hidden, gate_grad = call(
-        pack_kernel,
-        "pack",
-        [*(shift(factor, "spread", s) for s in STEPS[1:]), hidden, gate_grad],
-        [],
-        [
-            jax.ShapeDtypeStruct((RING - 1, *small.shape), jnp.float32),
-            *(jax.ShapeDtypeStruct(v.shape, v.dtype) for v in (hidden, gate_grad)),
-        ],
-        SMALL,
-        1,
-        (),
-        {RING - 1: 1, RING: 2},
-        [VMEM] * (RING - 1) + [ANY] * 2,
-        [VMEM] + [ANY] * 2,
+    given = [shift(factor, "spread", s) for s in STEPS[1:]]
+    hidden, gate_grad = held_back([hidden, gate_grad], given[:2])
+    (mine_factors,) = call(
+        pack_kernel, "pack", given, [], [jax.ShapeDtypeStruct((RING - 1, *small.shape), jnp.float32)], SMALL, 1
     )
     hidden_blocks = [hidden, *near_hidden, shift(hidden, "x", 2)]
     gate_blocks = [gate_grad, *near_gate, shift(gate_grad, "y", 2)]

time: 131 us -> 142 us (1.084)
  waiting for transfers between devices: 44.8 us -> 53.2 us
  starting transfers between devices: 35.2 us -> 38.7 us
    ppermute x6, waiting for transfers between devices: 5.12 us -> 18.3 us  [shift(): return lax.ppermute(value, ('x', 'y', 'core'), pairs)]
    ppermute x14, waiting for transfers between devices: 32.7 us -> 28 us  [shift(): lax.ppermute(value, axis, [(i, (i + step) % RING) for i in range(RING)])]
    ppermute x6, starting transfers between devices: 8.5 us -> 10.6 us  [shift(): return lax.ppermute(value, ('x', 'y', 'core'), pairs)]
    ppermute x14, starting transfers between devices: 20.6 us -> 22 us  [shift(): lax.ppermute(value, axis, [(i, (i + step) % RING) for i in range(RING)])]
    pallas_call x9 -> x10, Pallas kernels: 15.5 us -> 15.5 us  [call(): pl.pallas_call(body, in_specs=(in_specs or [VMEM] * count) + [ANY] * len(...]
  transfers between devices with their start and end apart: 25 -> 25, of which waited for: 13 -> 12; matrix products, arithmetic and copies ran while one was open for 10% -> 9% of each run, Pallas kernels for 21% -> 19%
where the time goes in v5:
time: 142 us; the launch traced here: 141 us
  waiting for transfers between devices  53.2 us (37%)
  starting transfers between devices  38.7 us (27%)
  Pallas kernels  30.2 us (21%)
  matrix products  11.2 us (8%)
  other arithmetic  3.57 us (3%)
  local copies, waits for them, and re-layouts  3.49 us (2%)
    ppermute x14, waiting for transfers between devices, shift(): lax.ppermute(value, axis, [(i, (i + step) % RING) for i in range(RING)])  28 us
    ppermute x14, starting transfers between devices, shift(): lax.ppermute(value, axis, [(i, (i + step) % RING) for i in range(RING)])  22 us
    ppermute x6, waiting for transfers between devices, shift(): return lax.ppermute(value, ('x', 'y', 'core'), pairs)  18.3 us
    pallas_call x10, Pallas kernels, call(): pl.pallas_call(body, in_specs=(in_specs or [VMEM] * count) + [ANY] * len(...  15.5 us
    dot_general x8, matrix products, dot_last(): lax.dot_general(left, right, (((1,), (1,)), ((), ())), preferred_element_...  11.2 us
    pallas_call x1, Pallas kernels, hidden_and_gradient(): pl.pallas_call(gate_kernel, grid=(width // rows,), in_specs=[pl.BlockSpec...  10.8 us
    ppermute x6, starting transfers between devices, shift(): return lax.ppermute(value, ('x', 'y', 'core'), pairs)  10.6 us
    ppermute x5, waiting for transfers between devices, swap(): lax.ppermute(value, axis, [(i, i ^ bit) for i in range(2 if axis == 'core...  6.96 us
  transfers between devices with their start and end apart: 25, of which 12 were waited for; matrix products, arithmetic and copies ran while one was open for 9% of the time, Pallas kernels for 19%

profile of v5, /device:TPU:0, one launch (start us, length us, event | category | flops | bytes accessed | tf_op | source)
XLA Modules:
  0.0 141.3 jit_solution(3839189530359481849)
XLA Ops:
  0.6 1.7 %copy-done = bf16[256,5120]{1,0:T(8,128)(2,1)S(1)} copy-done((bf16[256,5120]{1,0:T(8,128)(2,1)S(1)}, bf16[256,5120]{1,0:T(8,128)(2,1)}, u32[]{:S(2)}) %copy-start) | copy-done | bytes 2621464
  2.4 1.7 %copy-done.2 = bf16[256,5120]{1,0:T(8,128)(2,1)S(1)} copy-done((bf16[256,5120]{1,0:T(8,128)(2,1)S(1)}, bf16[256,5120]{1,0:T(8,128)(2,1)}, u32[]{:S(2)}) %copy-start.2) | copy-done | bytes 2621464
  4.1 2.6 %column_parts.1 = (bf16[1280,256]{1,0:T(8,128)(2,1)S(1)}, bf16[1280,256]{1,0:T(8,128)(2,1)}, bf16[1280,256]{1,0:T(8,128)(2,1)}, bf16[1280,256]{1,0:T(8,128)(2,1)}) custom-call(bf16[256,5120]{1,0:T(8,128)(2,1)S(1)} %copy-done, bf16[256,5120]{1,0:T(8,128)(2,1)S(1)} %copy-done.2), custom_call_target="tpu_custom_call" | custom-call | tf_op jit(solution)/shard_map/column_parts/pallas_call | solution.py:83
  6.7 1.6 %collective-permute-start = (bf16[1280,256]{1,0:T(8,128)(2,1)}, bf16[1280,256]{1,0:T(8,128)(2,1)}, u32[]{:S(2)}, u32[]{:S(2)}) collective-permute-start(bf16[1280,256]{1,0:T(8,128)(2,1)} %get-tuple-element.19), channel_id=1, source_target_pairs={{0,32},{1,9},{8,40},{9,17},{16,48},{17,25},{24,56},{25,1},{32,64},... | collective-permute-start | bytes 1966088 | tf_op jit(solution)/shard_map/ppermute | solution.py:40
  8.4 1.7 %collective-permute-start.1 = (bf16[1280,256]{1,0:T(8,128)(2,1)}, bf16[1280,256]{1,0:T(8,128)(2,1)}, u32[]{:S(2)}, u32[]{:S(2)}) collective-permute-start(bf16[1280,256]{1,0:T(8,128)(2,1)} %get-tuple-element.20), channel_id=1, source_target_pairs={{0,96},{1,25},{8,104},{9,1},{16,112},{17,9},{24,120},{25,17},{32,0... | collective-permute-start | bytes 1966088 | tf_op jit(solution)/shard_map/ppermute | solution.py:40
  10.1 1.9 %collective-permute-start.2 = (bf16[1280,256]{1,0:T(8,128)(2,1)}, bf16[1280,256]{1,0:T(8,128)(2,1)}, u32[]{:S(2)}, u32[]{:S(2)}) collective-permute-start(bf16[1280,256]{1,0:T(8,128)(2,1)} %get-tuple-element.21), channel_id=1, source_target_pairs={{0,64},{1,17},{8,72},{9,25},{16,80},{17,1},{24,88},{25,9},{32,96},... | collective-permute-start | bytes 1966088 | tf_op jit(solution)/shard_map/ppermute | solution.py:40
  11.9 10.8 %hidden_and_gradient.1 = (bf16[1728,256]{1,0:T(8,128)(2,1)}, bf16[1728,256]{1,0:T(8,128)(2,1)}) custom-call(bf16[1728,5120]{1,0:T(8,128)(2,1)} %bitcast.20, bf16[256,5120]{1,0:T(8,128)(2,1)} %refs_0_.3, bf16[1728,256]{1,0:T(8,128)(2,1)S(1)} %bitcast.19, bf16[1728,256]{1,0:T(8,128)(2,1)} %bitcast.21, bf16[1280,256]{1,0:T(8,128)(2,1)S(1)} %get-tuple-element.18.rest_0_.refs_0_), custom_call_target="tpu_custom_call" | custom-call | flops 999999995904 | bytes 1000000000 | tf_op jit(solution)/shard_map/hidden_and_gradient/pallas_call | solution.py:111
  22.7 3.0 %collective-permute-start.10 = (bf16[1728,256]{1,0:T(8,128)(2,1)}, bf16[1728,256]{1,0:T(8,128)(2,1)}, u32[]{:S(2)}, u32[]{:S(2)}) collective-permute-start(bf16[1728,256]{1,0:T(8,128)(2,1)} %get-tuple-element.22.refs_4_.refs_3_.refs_1_), channel_id=1, source_target_pairs={{0,24},{8,0},{16,8},{24,16},{1,25},{9,1},{17,9},{25,17},{2,26},{10... | collective-permute-start | bytes 2654216 | tf_op jit(solution)/shard_map/ppermute | solution.py:33
  26.4 2.7 %collective-permute-start.8 = (bf16[1728,256]{1,0:T(8,128)(2,1)}, bf16[1728,256]{1,0:T(8,128)(2,1)}, u32[]{:S(2)}, u32[]{:S(2)}) collective-permute-start(bf16[1728,256]{1,0:T(8,128)(2,1)} %get-tuple-element.23.refs_2_.refs_0_), channel_id=1, source_target_pairs={{0,96},{32,0},{64,32},{96,64},{1,97},{33,1},{65,33},{97,65},{2,98}... | collective-permute-start | bytes 2654216 | tf_op jit(solution)/shard_map/ppermute | solution.py:33
  29.2 4.0 %stack.1.refs_0_ = bf16[4,1280,256]{2,1,0:T(8,128)(2,1)} custom-call(bf16[1280,256]{1,0:T(8,128)(2,1)S(1)} %get-tuple-element.18.rest_0_.refs_0_, bf16[1280,256]{1,0:T(8,128)(2,1)} %collective-permute-done.refs_1_.refs_4_, bf16[1280,256]{1,0:T(8,128)(2,1)} %collective-permute-done.1.refs_2_.refs_5_, ...), custom_call_target="tpu_custom_call" | custom-call | tf_op jit(solution)/shard_map/stack/pallas_call | solution.py:184
  33.2 3.6 %squares.1.refs_0_ = f32[8,128]{1,0:T(8,128)S(1)} custom-call(bf16[256,5120]{1,0:T(8,128)(2,1)S(1)} %copy-done.1, bf16[256,5120]{1,0:T(8,128)(2,1)S(1)} %copy-done.3, bf16[1728,256]{1,0:T(8,128)(2,1)} %get-tuple-element.23.refs_2_.refs_0_, bf16[1728,256]{1,0:T(8,128)(2,1)} %get-tuple-element.22.refs_4_.refs_3_.refs_1_, ...), custom_call_target="tpu_custom_call" | custom-call | flops 999999995904 | bytes 1000000000 | tf_op jit(solution)/shard_map/squares/pallas_call | solution.py:83
  36.8 1.6 %collective-permute-done.3.refs_1_ = bf16[4,1280,256]{2,1,0:T(8,128)(2,1)} collective-permute-done((bf16[4,1280,256]{2,1,0:T(8,128)(2,1)}, bf16[4,1280,256]{2,1,0:T(8,128)(2,1)}, u32[]{:S(2)}, u32[]{:S(2)}) %collective-permute-start.3) | collective-permute-done | bytes 2621472 | tf_op jit(solution)/shard_map/ppermute | solution.py:44
  38.5 1.0 collective-permute-done.4
  39.6 2.0 %collective-permute-start.5 = (f32[8,128]{1,0:T(8,128)S(1)}, f32[8,128]{1,0:T(8,128)S(1)}, u32[]{:S(2)}, u32[]{:S(2)}) collective-permute-start(f32[8,128]{1,0:T(8,128)S(1)} %add.42), channel_id=1, source_target_pairs={{0,2},{2,0},{4,6},{6,4},{1,3},{3,1},{5,7},{7,5},{8,10},{10,8},{12,... | collective-permute-start | bytes 12296 | tf_op jit(solution)/shard_map/ppermute | solution.py:44
  41.6 1.6 %collective-permute-done.5 = f32[8,128]{1,0:T(8,128)S(1)} collective-permute-done((f32[8,128]{1,0:T(8,128)S(1)}, f32[8,128]{1,0:T(8,128)S(1)}, u32[]{:S(2)}, u32[]{:S(2)}) %collective-permute-start.5) | collective-permute-done | bytes 4128 | tf_op jit(solution)/shard_map/ppermute | solution.py:44
  43.2 4.0 %collective-permute-start.6 = (f32[8,128]{1,0:T(8,128)S(1)}, f32[8,128]{1,0:T(8,128)S(1)}, u32[]{:S(2)}, u32[]{:S(2)}) collective-permute-start(f32[8,128]{1,0:T(8,128)S(1)} %add.43.refs_0_), channel_id=1, source_target_pairs={{0,4},{2,6},{4,0},{6,2},{1,5},{3,7},{5,1},{7,3},{8,12},{10,14},{12... | collective-permute-start | bytes 12296 | tf_op jit(solution)/shard_map/ppermute | solution.py:44
  47.2 1.6 %collective-permute-done.6.refs_1_ = f32[8,128]{1,0:T(8,128)S(1)} collective-permute-done((f32[8,128]{1,0:T(8,128)S(1)}, f32[8,128]{1,0:T(8,128)S(1)}, u32[]{:S(2)}, u32[]{:S(2)}) %collective-permute-start.6) | collective-permute-done | bytes 4128 | tf_op jit(solution)/shard_map/ppermute | solution.py:44
  49.4 3.2 %collective-permute-start.12 = (f32[8,128]{1,0:T(8,128)S(1)}, f32[8,128]{1,0:T(8,128)S(1)}, u32[]{:S(2)}, u32[]{:S(2)}) collective-permute-start(f32[8,128]{1,0:T(8,128)S(1)} %factor.1.refs_2_), channel_id=1, source_target_pairs={{0,96},{1,25},{8,104},{9,1},{16,112},{17,9},{24,120},{25,17},{32,0... | collective-permute-start | bytes 12296 | tf_op jit(solution)/shard_map/ppermute | solution.py:40
  52.6 1.6 %collective-permute-done.11.refs_0_.refs_2_ = f32[8,128]{1,0:T(8,128)S(1)} collective-permute-done((f32[8,128]{1,0:T(8,128)S(1)}, f32[8,128]{1,0:T(8,128)S(1)}, u32[]{:S(2)}, u32[]{:S(2)}) %collective-permute-start.11) | collective-permute-done | bytes 4128 | tf_op jit(solution)/shard_map/ppermute | solution.py:40
  54.2 3.2 %collective-permute-start.20 = (bf16[1728,256]{1,0:T(8,128)(2,1)}, bf16[1728,256]{1,0:T(8,128)(2,1)S(1)}, u32[]{:S(2)}, u32[]{:S(2)}) collective-permute-start(bf16[1728,256]{1,0:T(8,128)(2,1)} %get-tuple-element.30.refs_0_), channel_id=1, source_target_pairs={{0,16},{8,24},{16,0},{24,8},{1,17},{9,25},{17,1},{25,9},{2,18},{10... | collective-permute-start | bytes 2654216 | tf_op jit(solution)/shard_map/ppermute | solution.py:33
  57.4 1.5 %collective-permute-start.15 = (bf16[1728,256]{1,0:T(8,128)(2,1)}, bf16[1728,256]{1,0:T(8,128)(2,1)S(1)}, u32[]{:S(2)}, u32[]{:S(2)}) collective-permute-start(bf16[1728,256]{1,0:T(8,128)(2,1)} %get-tuple-element.25.refs_0_), channel_id=1, source_target_pairs={{0,64},{32,96},{64,0},{96,32},{1,65},{33,97},{65,1},{97,33},{2,66}... | collective-permute-start | bytes 2654216 | tf_op jit(solution)/shard_map/ppermute | solution.py:33
  58.9 2.1 %collective-permute-start.13 = (f32[8,128]{1,0:T(8,128)S(1)}, f32[8,128]{1,0:T(8,128)S(1)}, u32[]{:S(2)}, u32[]{:S(2)}) collective-permute-start(f32[8,128]{1,0:T(8,128)S(1)} %factor.1.refs_2_), channel_id=1, source_target_pairs={{0,64},{1,17},{8,72},{9,25},{16,80},{17,1},{24,88},{25,9},{32,96},... | collective-permute-start | bytes 12296 | tf_op jit(solution)/shard_map/ppermute | solution.py:40
  60.9 16.7 %collective-permute-done.13.refs_2_ = f32[8,128]{1,0:T(8,128)S(1)} collective-permute-done((f32[8,128]{1,0:T(8,128)S(1)}, f32[8,128]{1,0:T(8,128)S(1)}, u32[]{:S(2)}, u32[]{:S(2)}) %collective-permute-start.13) | collective-permute-done | bytes 4128 | tf_op jit(solution)/shard_map/ppermute | solution.py:40
  77.6 1.2 collective-permute-done.14.refs_4_
  78.8 2.1 %lefts.3 = (bf16[320,1024]{1,0:T(8,128)(2,1)S(1)}, bf16[320,1024]{1,0:T(8,128)(2,1)S(1)}, bf16[320,1024]{1,0:T(8,128)(2,1)S(1)}, bf16[320,1024]{1,0:T(8,128)(2,1)S(1)}) custom-call(bf16[4,1280,256]{2,1,0:T(8,128)(2,1)} %stack.1.refs_0_, bf16[4,1280,256]{2,1,0:T(8,128)(2,1)} %collective-permute-done.3.refs_1_, f32[8,128]{1,0:T(8,128)S(1)} %factor.1.refs_2_, ...), custom_call_target="tpu_custom_call" | custom-call | tf_op jit(solution)/shard_map/lefts/pallas_call | solution.py:83
  80.9 2.2 %lefts.2 = (bf16[320,1024]{1,0:T(8,128)(2,1)S(1)}, bf16[320,1024]{1,0:T(8,128)(2,1)S(1)}, bf16[320,1024]{1,0:T(8,128)(2,1)S(1)}, bf16[320,1024]{1,0:T(8,128)(2,1)S(1)}) custom-call(bf16[4,1280,256]{2,1,0:T(8,128)(2,1)} %stack.1.refs_0_, bf16[4,1280,256]{2,1,0:T(8,128)(2,1)} %collective-permute-done.3.refs_1_, f32[8,128]{1,0:T(8,128)S(1)} %factor.1.refs_2_, ...), custom_call_target="tpu_custom_call" | custom-call | tf_op jit(solution)/shard_map/lefts/pallas_call | solution.py:83
  83.1 2.2 %wide.3 = bf16[1728,1024]{1,0:T(8,128)(2,1)S(1)} custom-call(bf16[1728,256]{1,0:T(8,128)(2,1)} %get-tuple-element.30.refs_0_, bf16[1728,256]{1,0:T(8,128)(2,1)} %collective-permute-done.9.refs_5_.refs_1_, bf16[1728,256]{1,0:T(8,128)(2,1)} %collective-permute-done.10.refs_6_.refs_2_, bf16[1728,256]{1,0:T(8,128)(2,1)S(1)} %collective-permute-done.20.refs_3_), custom_call_target="tpu_custom_call" | custom-call | tf_op jit(solution)/shard_map/wide/pallas_call | solution.py:83
  85.3 1.4 convolution_convert_fusion.2
  86.7 1.8 %collective-permute-start.21 = (bf16[320,1728]{1,0:T(8,128)(2,1)S(1)}, bf16[320,1728]{1,0:T(8,128)(2,1)S(1)}, u32[]{:S(2)}, u32[]{:S(2)}) collective-permute-start(bf16[320,1728]{1,0:T(8,128)(2,1)S(1)} %convolution_convert_fusion.2), channel_id=1, source_target_pairs={{0,96},{32,0},{64,32},{96,64},{1,97},{33,1},{65,33},{97,65},{2,98}... | collective-permute-start | bytes 3317768 | tf_op jit(solution)/shard_map/ppermute | solution.py:33
  88.6 1.4 convolution_convert_fusion
  90.3 2.2 %wide.2 = bf16[1728,1024]{1,0:T(8,128)(2,1)S(1)} custom-call(bf16[1728,256]{1,0:T(8,128)(2,1)} %get-tuple-element.25.refs_0_, bf16[1728,256]{1,0:T(8,128)(2,1)} %collective-permute-done.7.refs_3_.refs_1_, bf16[1728,256]{1,0:T(8,128)(2,1)} %collective-permute-done.8.refs_4_.refs_2_, bf16[1728,256]{1,0:T(8,128)(2,1)S(1)} %collective-permute-done.15.refs_3_), custom_call_target="tpu_custom_call" | custom-call | tf_op jit(solution)/shard_map/wide/pallas_call | solution.py:83
  92.5 1.4 convolution_convert_fusion.6
  93.9 1.4 %collective-permute-start.16 = (bf16[320,1728]{1,0:T(8,128)(2,1)S(1)}, bf16[320,1728]{1,0:T(8,128)(2,1)S(1)}, u32[]{:S(2)}, u32[]{:S(2)}) collective-permute-start(bf16[320,1728]{1,0:T(8,128)(2,1)S(1)} %convolution_convert_fusion.6), channel_id=1, source_target_pairs={{0,24},{8,0},{16,8},{24,16},{1,25},{9,1},{17,9},{25,17},{2,26},{10... | collective-permute-start | bytes 3317768 | tf_op jit(solution)/shard_map/ppermute | solution.py:33
  95.3 1.4 convolution_convert_fusion.4
  96.7 0.7 collective-permute-start.17
  97.5 1.4 convolution_convert_fusion.3
  98.9 1.4 convolution_convert_fusion.1
  100.3 1.4 convolution_convert_fusion.7
  101.7 12.6 %collective-permute-done.21 = bf16[320,1728]{1,0:T(8,128)(2,1)S(1)} collective-permute-done((bf16[320,1728]{1,0:T(8,128)(2,1)S(1)}, bf16[320,1728]{1,0:T(8,128)(2,1)S(1)}, u32[]{:S(2)}, u32[]{:S(2)}) %collective-permute-start.21) | collective-permute-done | bytes 1105952 | tf_op jit(solution)/shard_map/ppermute | solution.py:33
  114.3 4.2 %collective-permute-done.22 = bf16[320,1728]{1,0:T(8,128)(2,1)S(1)} collective-permute-done((bf16[320,1728]{1,0:T(8,128)(2,1)S(1)}, bf16[320,1728]{1,0:T(8,128)(2,1)S(1)}, u32[]{:S(2)}, u32[]{:S(2)}) %collective-permute-start.22) | collective-permute-done | bytes 1105952 | tf_op jit(solution)/shard_map/ppermute | solution.py:33
  118.8 3.2 %collective-permute-start.24 = (bf16[160,1728]{1,0:T(8,128)(2,1)S(1)}, bf16[160,1728]{1,0:T(8,128)(2,1)S(1)}, u32[]{:S(2)}, u32[]{:S(2)}) collective-permute-start(bf16[160,1728]{1,0:T(8,128)(2,1)S(1)} %get-tuple-element.37), channel_id=1, source_target_pairs={{0,96},{32,0},{64,32},{96,64},{1,97},{33,1},{65,33},{97,65},{2,98}... | collective-permute-start | bytes 1658888 | tf_op jit(solution)/shard_map/ppermute | solution.py:33
  122.1 1.4 convolution_convert_fusion.5
  123.5 1.2 collective-permute-done.17
  125.1 3.2 %collective-permute-start.19 = (bf16[160,1728]{1,0:T(8,128)(2,1)S(1)}, bf16[160,1728]{1,0:T(8,128)(2,1)S(1)}, u32[]{:S(2)}, u32[]{:S(2)}) collective-permute-start(bf16[160,1728]{1,0:T(8,128)(2,1)S(1)} %get-tuple-element.41), channel_id=1, source_target_pairs={{0,24},{8,0},{16,8},{24,16},{1,25},{9,1},{17,9},{25,17},{2,26},{10... | collective-permute-start | bytes 1658888 | tf_op jit(solution)/shard_map/ppermute | solution.py:33
  128.3 5.9 %collective-permute-done.23 = bf16[160,1728]{1,0:T(8,128)(2,1)S(1)} collective-permute-done((bf16[160,1728]{1,0:T(8,128)(2,1)S(1)}, bf16[160,1728]{1,0:T(8,128)(2,1)S(1)}, u32[]{:S(2)}, u32[]{:S(2)}) %collective-permute-start.23) | collective-permute-done | bytes 552992 | tf_op jit(solution)/shard_map/ppermute | solution.py:33
  134.5 1.1 fusion.1
  135.7 4.1 %collective-permute-done.18 = bf16[160,1728]{1,0:T(8,128)(2,1)S(1)} collective-permute-done((bf16[160,1728]{1,0:T(8,128)(2,1)S(1)}, bf16[160,1728]{1,0:T(8,128)(2,1)S(1)}, u32[]{:S(2)}, u32[]{:S(2)}) %collective-permute-start.18) | collective-permute-done | bytes 552992 | tf_op jit(solution)/shard_map/ppermute | solution.py:33
  140.1 1.1 fusion
  (42 shorter events, 3.3 us)
Async XLA Ops:
  0.6 1.7 %copy-start = (bf16[256,5120]{1,0:T(8,128)(2,1)S(1)}, bf16[256,5120]{1,0:T(8,128)(2,1)}, u32[]{:S(2)}) copy-start(bf16[256,5120]{1,0:T(8,128)(2,1)} %refs_0_.3) | copy-start | bytes 7864324
  2.4 1.7 %copy-start.2 = (bf16[256,5120]{1,0:T(8,128)(2,1)S(1)}, bf16[256,5120]{1,0:T(8,128)(2,1)}, u32[]{:S(2)}) copy-start(bf16[256,5120]{1,0:T(8,128)(2,1)} %refs_1_.3) | copy-start | bytes 7864324
  4.1 7.8 %copy-start.5 = (bf16[256,1728]{0,1:T(8,128)(2,1)S(1)}, bf16[256,1728]{0,1:T(8,128)(2,1)}, u32[]{:S(2)}) copy-start(bf16[256,1728]{0,1:T(8,128)(2,1)} %param.8) | copy-start | bytes 2654212
  6.7 19.0 %collective-permute-start = (bf16[1280,256]{1,0:T(8,128)(2,1)}, bf16[1280,256]{1,0:T(8,128)(2,1)}, u32[]{:S(2)}, u32[]{:S(2)}) collective-permute-start(bf16[1280,256]{1,0:T(8,128)(2,1)} %get-tuple-element.19), channel_id=1, source_target_pairs={{0,32},{1,9},{8,40},{9,17},{16,48},{17,25},{24,56},{25,1},{32,64},... | collective-permute-start | bytes 1966088 | tf_op jit(solution)/shard_map/ppermute | solution.py:40
  8.4 18.1 %collective-permute-start.1 = (bf16[1280,256]{1,0:T(8,128)(2,1)}, bf16[1280,256]{1,0:T(8,128)(2,1)}, u32[]{:S(2)}, u32[]{:S(2)}) collective-permute-start(bf16[1280,256]{1,0:T(8,128)(2,1)} %get-tuple-element.20), channel_id=1, source_target_pairs={{0,96},{1,25},{8,104},{9,1},{16,112},{17,9},{24,120},{25,17},{32,0... | collective-permute-start | bytes 1966088 | tf_op jit(solution)/shard_map/ppermute | solution.py:40
  10.1 19.1 %collective-permute-start.2 = (bf16[1280,256]{1,0:T(8,128)(2,1)}, bf16[1280,256]{1,0:T(8,128)(2,1)}, u32[]{:S(2)}, u32[]{:S(2)}) collective-permute-start(bf16[1280,256]{1,0:T(8,128)(2,1)} %get-tuple-element.21), channel_id=1, source_target_pairs={{0,64},{1,17},{8,72},{9,25},{16,80},{17,1},{24,88},{25,9},{32,96},... | collective-permute-start | bytes 1966088 | tf_op jit(solution)/shard_map/ppermute | solution.py:40
  22.7 24.4 %collective-permute-start.10 = (bf16[1728,256]{1,0:T(8,128)(2,1)}, bf16[1728,256]{1,0:T(8,128)(2,1)}, u32[]{:S(2)}, u32[]{:S(2)}) collective-permute-start(bf16[1728,256]{1,0:T(8,128)(2,1)} %get-tuple-element.22.refs_4_.refs_3_.refs_1_), channel_id=1, source_target_pairs={{0,24},{8,0},{16,8},{24,16},{1,25},{9,1},{17,9},{25,17},{2,26},{10... | collective-permute-start | bytes 2654216 | tf_op jit(solution)/shard_map/ppermute | solution.py:33
  25.7 21.4 %collective-permute-start.9 = (bf16[1728,256]{1,0:T(8,128)(2,1)}, bf16[1728,256]{1,0:T(8,128)(2,1)}, u32[]{:S(2)}, u32[]{:S(2)}) collective-permute-start(bf16[1728,256]{1,0:T(8,128)(2,1)} %get-tuple-element.22.refs_4_.refs_3_.refs_1_), channel_id=1, source_target_pairs={{0,8},{8,16},{16,24},{24,0},{1,9},{9,17},{17,25},{25,1},{2,10},{10... | collective-permute-start | bytes 2654216 | tf_op jit(solution)/shard_map/ppermute | solution.py:33
  25.8 7.4 %copy-start.1 = (bf16[256,5120]{1,0:T(8,128)(2,1)S(1)}, bf16[256,5120]{1,0:T(8,128)(2,1)}, u32[]{:S(2)}) copy-start(bf16[256,5120]{1,0:T(8,128)(2,1)} %refs_0_.3) | copy-start | bytes 7864324
  25.8 7.4 %copy-start.3 = (bf16[256,5120]{1,0:T(8,128)(2,1)S(1)}, bf16[256,5120]{1,0:T(8,128)(2,1)}, u32[]{:S(2)}) copy-start(bf16[256,5120]{1,0:T(8,128)(2,1)} %refs_1_.3) | copy-start | bytes 7864324
  25.8 21.4 %collective-permute-start.7 = (bf16[1728,256]{1,0:T(8,128)(2,1)}, bf16[1728,256]{1,0:T(8,128)(2,1)}, u32[]{:S(2)}, u32[]{:S(2)}) collective-permute-start(bf16[1728,256]{1,0:T(8,128)(2,1)} %get-tuple-element.23.refs_2_.refs_0_), channel_id=1, source_target_pairs={{0,32},{32,64},{64,96},{96,0},{1,33},{33,65},{65,97},{97,1},{2,34}... | collective-permute-start | bytes 2654216 | tf_op jit(solution)/shard_map/ppermute | solution.py:33
  26.4 20.7 %collective-permute-start.8 = (bf16[1728,256]{1,0:T(8,128)(2,1)}, bf16[1728,256]{1,0:T(8,128)(2,1)}, u32[]{:S(2)}, u32[]{:S(2)}) collective-permute-start(bf16[1728,256]{1,0:T(8,128)(2,1)} %get-tuple-element.23.refs_2_.refs_0_), channel_id=1, source_target_pairs={{0,96},{32,0},{64,32},{96,64},{1,97},{33,1},{65,33},{97,65},{2,98}... | collective-permute-start | bytes 2654216 | tf_op jit(solution)/shard_map/ppermute | solution.py:33
  33.1 5.3 %collective-permute-start.3 = (bf16[4,1280,256]{2,1,0:T(8,128)(2,1)}, bf16[4,1280,256]{2,1,0:T(8,128)(2,1)}, u32[]{:S(2)}, u32[]{:S(2)}) collective-permute-start(bf16[4,1280,256]{2,1,0:T(8,128)(2,1)} %stack.1.refs_0_), channel_id=1, source_target_pairs={{0,1},{1,0},{2,3},{3,2},{4,5},{5,4},{6,7},{7,6},{8,9},{9,8},{10,11... | collective-permute-start | bytes 7864328 | tf_op jit(solution)/shard_map/ppermute | solution.py:44
  36.8 11.9 %copy-start.4 = (f32[2]{0:T(128)S(1)}, f32[2]{0:T(128)}, u32[]{:S(2)}) copy-start(f32[2]{0:T(128)} %refs_2_.1) | copy-start | bytes 28
  38.4 1.2 collective-permute-start.4
  39.6 3.6 %collective-permute-start.5 = (f32[8,128]{1,0:T(8,128)S(1)}, f32[8,128]{1,0:T(8,128)S(1)}, u32[]{:S(2)}, u32[]{:S(2)}) collective-permute-start(f32[8,128]{1,0:T(8,128)S(1)} %add.42), channel_id=1, source_target_pairs={{0,2},{2,0},{4,6},{6,4},{1,3},{3,1},{5,7},{7,5},{8,10},{10,8},{12,... | collective-permute-start | bytes 12296 | tf_op jit(solution)/shard_map/ppermute | solution.py:44
  43.2 5.5 %collective-permute-start.6 = (f32[8,128]{1,0:T(8,128)S(1)}, f32[8,128]{1,0:T(8,128)S(1)}, u32[]{:S(2)}, u32[]{:S(2)}) collective-permute-start(f32[8,128]{1,0:T(8,128)S(1)} %add.43.refs_0_), channel_id=1, source_target_pairs={{0,4},{2,6},{4,0},{6,2},{1,5},{3,7},{5,1},{7,3},{8,12},{10,14},{12... | collective-permute-start | bytes 12296 | tf_op jit(solution)/shard_map/ppermute | solution.py:44
  49.3 4.9 %collective-permute-start.11 = (f32[8,128]{1,0:T(8,128)S(1)}, f32[8,128]{1,0:T(8,128)S(1)}, u32[]{:S(2)}, u32[]{:S(2)}) collective-permute-start(f32[8,128]{1,0:T(8,128)S(1)} %factor.1.refs_2_), channel_id=1, source_target_pairs={{0,32},{1,9},{8,40},{9,17},{16,48},{17,25},{24,56},{25,1},{32,64},... | collective-permute-start | bytes 12296 | tf_op jit(solution)/shard_map/ppermute | solution.py:40
  49.4 4.8 %collective-permute-start.12 = (f32[8,128]{1,0:T(8,128)S(1)}, f32[8,128]{1,0:T(8,128)S(1)}, u32[]{:S(2)}, u32[]{:S(2)}) collective-permute-start(f32[8,128]{1,0:T(8,128)S(1)} %factor.1.refs_2_), channel_id=1, source_target_pairs={{0,96},{1,25},{8,104},{9,1},{16,112},{17,9},{24,120},{25,17},{32,0... | collective-permute-start | bytes 12296 | tf_op jit(solution)/shard_map/ppermute | solution.py:40
  54.2 28.9 %collective-permute-start.20 = (bf16[1728,256]{1,0:T(8,128)(2,1)}, bf16[1728,256]{1,0:T(8,128)(2,1)S(1)}, u32[]{:S(2)}, u32[]{:S(2)}) collective-permute-start(bf16[1728,256]{1,0:T(8,128)(2,1)} %get-tuple-element.30.refs_0_), channel_id=1, source_target_pairs={{0,16},{8,24},{16,0},{24,8},{1,17},{9,25},{17,1},{25,9},{2,18},{10... | collective-permute-start | bytes 2654216 | tf_op jit(solution)/shard_map/ppermute | solution.py:33
  57.4 32.9 %collective-permute-start.15 = (bf16[1728,256]{1,0:T(8,128)(2,1)}, bf16[1728,256]{1,0:T(8,128)(2,1)S(1)}, u32[]{:S(2)}, u32[]{:S(2)}) collective-permute-start(bf16[1728,256]{1,0:T(8,128)(2,1)} %get-tuple-element.25.refs_0_), channel_id=1, source_target_pairs={{0,64},{32,96},{64,0},{96,32},{1,65},{33,97},{65,1},{97,33},{2,66}... | collective-permute-start | bytes 2654216 | tf_op jit(solution)/shard_map/ppermute | solution.py:33
  58.9 18.7 %collective-permute-start.13 = (f32[8,128]{1,0:T(8,128)S(1)}, f32[8,128]{1,0:T(8,128)S(1)}, u32[]{:S(2)}, u32[]{:S(2)}) collective-permute-start(f32[8,128]{1,0:T(8,128)S(1)} %factor.1.refs_2_), channel_id=1, source_target_pairs={{0,64},{1,17},{8,72},{9,25},{16,80},{17,1},{24,88},{25,9},{32,96},... | collective-permute-start | bytes 12296 | tf_op jit(solution)/shard_map/ppermute | solution.py:40
  77.6 1.2 collective-permute-start.14
  86.7 27.6 %collective-permute-start.21 = (bf16[320,1728]{1,0:T(8,128)(2,1)S(1)}, bf16[320,1728]{1,0:T(8,128)(2,1)S(1)}, u32[]{:S(2)}, u32[]{:S(2)}) collective-permute-start(bf16[320,1728]{1,0:T(8,128)(2,1)S(1)} %convolution_convert_fusion.2), channel_id=1, source_target_pairs={{0,96},{32,0},{64,32},{96,64},{1,97},{33,1},{65,33},{97,65},{2,98}... | collective-permute-start | bytes 3317768 | tf_op jit(solution)/shard_map/ppermute | solution.py:33
  90.0 28.5 %collective-permute-start.22 = (bf16[320,1728]{1,0:T(8,128)(2,1)S(1)}, bf16[320,1728]{1,0:T(8,128)(2,1)S(1)}, u32[]{:S(2)}, u32[]{:S(2)}) collective-permute-start(bf16[320,1728]{1,0:T(8,128)(2,1)S(1)} %convolution_convert_fusion), channel_id=1, source_target_pairs={{0,32},{32,64},{64,96},{96,0},{1,33},{33,65},{65,97},{97,1},{2,34}... | collective-permute-start | bytes 3317768 | tf_op jit(solution)/shard_map/ppermute | solution.py:33
  93.9 29.6 %collective-permute-start.16 = (bf16[320,1728]{1,0:T(8,128)(2,1)S(1)}, bf16[320,1728]{1,0:T(8,128)(2,1)S(1)}, u32[]{:S(2)}, u32[]{:S(2)}) collective-permute-start(bf16[320,1728]{1,0:T(8,128)(2,1)S(1)} %convolution_convert_fusion.6), channel_id=1, source_target_pairs={{0,24},{8,0},{16,8},{24,16},{1,25},{9,1},{17,9},{25,17},{2,26},{10... | collective-permute-start | bytes 3317768 | tf_op jit(solution)/shard_map/ppermute | solution.py:33
  96.7 28.0 %collective-permute-start.17 = (bf16[320,1728]{1,0:T(8,128)(2,1)S(1)}, bf16[320,1728]{1,0:T(8,128)(2,1)S(1)}, u32[]{:S(2)}, u32[]{:S(2)}) collective-permute-start(bf16[320,1728]{1,0:T(8,128)(2,1)S(1)} %convolution_convert_fusion.4), channel_id=1, source_target_pairs={{0,8},{8,16},{16,24},{24,0},{1,9},{9,17},{17,25},{25,1},{2,10},{10... | collective-permute-start | bytes 3317768 | tf_op jit(solution)/shard_map/ppermute | solution.py:33
  118.8 15.4 %collective-permute-start.23 = (bf16[160,1728]{1,0:T(8,128)(2,1)S(1)}, bf16[160,1728]{1,0:T(8,128)(2,1)S(1)}, u32[]{:S(2)}, u32[]{:S(2)}) collective-permute-start(bf16[160,1728]{1,0:T(8,128)(2,1)S(1)} %get-tuple-element.36), channel_id=1, source_target_pairs={{0,32},{32,64},{64,96},{96,0},{1,33},{33,65},{65,97},{97,1},{2,34}... | collective-permute-start | bytes 1658888 | tf_op jit(solution)/shard_map/ppermute | solution.py:33
  118.8 15.3 %collective-permute-start.24 = (bf16[160,1728]{1,0:T(8,128)(2,1)S(1)}, bf16[160,1728]{1,0:T(8,128)(2,1)S(1)}, u32[]{:S(2)}, u32[]{:S(2)}) collective-permute-start(bf16[160,1728]{1,0:T(8,128)(2,1)S(1)} %get-tuple-element.37), channel_id=1, source_target_pairs={{0,96},{32,0},{64,32},{96,64},{1,97},{33,1},{65,33},{97,65},{2,98}... | collective-permute-start | bytes 1658888 | tf_op jit(solution)/shard_map/ppermute | solution.py:33
  125.0 14.8 %collective-permute-start.18 = (bf16[160,1728]{1,0:T(8,128)(2,1)S(1)}, bf16[160,1728]{1,0:T(8,128)(2,1)S(1)}, u32[]{:S(2)}, u32[]{:S(2)}) collective-permute-start(bf16[160,1728]{1,0:T(8,128)(2,1)S(1)} %get-tuple-element.40), channel_id=1, source_target_pairs={{0,8},{8,16},{16,24},{24,0},{1,9},{9,17},{17,25},{25,1},{2,10},{10... | collective-permute-start | bytes 1658888 | tf_op jit(solution)/shard_map/ppermute | solution.py:33
  125.1 14.7 %collective-permute-start.19 = (bf16[160,1728]{1,0:T(8,128)(2,1)S(1)}, bf16[160,1728]{1,0:T(8,128)(2,1)S(1)}, u32[]{:S(2)}, u32[]{:S(2)}) collective-permute-start(bf16[160,1728]{1,0:T(8,128)(2,1)S(1)} %get-tuple-element.41), channel_id=1, source_target_pairs={{0,24},{8,0},{16,8},{24,16},{1,25},{9,1},{17,9},{25,17},{2,26},{10... | collective-permute-start | bytes 1658888 | tf_op jit(solution)/shard_map/ppermute | solution.py:33
